TPU v7x, 32 devices: a whole 2x2x4 slice. The times are simulated.
32 devices in a mesh: section: 4 (over x, core), expert: 8 (over z, y).
Axes of the slice: x: 2, y: 2, z: 4, core: 2. Of those that a mesh axis runs over, the one named last changes fastest.
Arguments:
- act_in: bfloat16 [4, 1024, 6144], P('section', 'expert'), may hold values from -6 to 6
- saved_in: bfloat16 [4, 1024, 6144], P('section', 'expert'), may hold values from -6 to 6
- grad_in: bfloat16 [4, 1024, 6144], P('section', 'expert'), may hold values from -6 to 6
- fwd_routes: int32 [4, 1024, 2], P('section', 'expert'), may hold values from 0 to 7, as said below
- bwd_routes: int32 [4, 1024, 2], P('section', 'expert'), may hold values from 0 to 7, as said below
- w_gate: bfloat16 [4, 6144, 8192], P('section', None, 'expert'), may hold values from -0.078125 to 0.078125
- w_up: bfloat16 [4, 6144, 8192], P('section', None, 'expert'), may hold values from -0.078125 to 0.078125
- w_down: bfloat16 [4, 8192, 6144], P('section', 'expert'), may hold values from -0.0625 to 0.0625
- router: float32 [4, 6144, 8], P('section'), may hold values from -0.078125 to 0.078125
- norm_gain: float32 [4, 6144], P('section'), may hold values from 0.1 to 1.9
Outputs:
- act_out: bfloat16 [4, 1024, 6144], P('section', 'expert')
- grad_out: bfloat16 [4, 1024, 6144], P('section', 'expert')
Inputs may be any that keep to these rules, and one draw needn't show every extreme that they name: `fwd_routes`: per section, the 128 rows of one device name expert 0 between 16 and 32 times, and in every section some device's rows name it exactly 32 times; a token's two experts differ. `bwd_routes`: per section, the 128 rows of one device name expert 0 between 16 and 32 times, and in every section some device's rows name it exactly 32 times; a token's two experts differ.
All inputs are finite; a program needn't handle non-finite values.
Results may differ from a plain program's by a relative error of at most 0.007.
Values may be sent and summed in bfloat16 or wider, within the bound.
No kernel may reach another device: no remote copies, remote signals or barrier semaphores. Data moves between devices by JAX's collectives and lax.ppermute only.
A program may use at most 128 MiB of HBM per device.

v0:
```python
import jax
import jax.numpy as jnp
from jax import lax
from jax.sharding import PartitionSpec as P

epsilon = 1e-05
highest = lax.Precision.HIGHEST


def shifted(value, axis, steps):
    count = lax.axis_size(axis)
    pairs = [(source, (source + steps) % count) for source in range(count)]
    return lax.ppermute(value, axis, pairs)


def norm_route(inputs, gain_row, router_mat, chosen_ids):
    inverse = lax.rsqrt(jnp.mean(inputs * inputs, axis=1, keepdims=True) + epsilon)
    normed = inputs * inverse * gain_row[None, :]
    logits = jnp.dot(normed, router_mat, precision=highest)
    onehot = (
        chosen_ids[:, :, None] == jnp.arange(router_mat.shape[1], dtype=jnp.int32)[None, None, :]
    ).astype(jnp.float32)
    picked = jnp.sum(onehot * logits[:, None, :], axis=2)
    first_share = jax.nn.sigmoid(picked[:, 0] - picked[:, 1])
    shares = jnp.stack([first_share, 1.0 - first_share], axis=1)
    window_weight = jnp.sum(shares * (chosen_ids == 0).astype(jnp.float32), axis=1)
    return (normed, window_weight)


def assign_window(chosen_ids, capacity):
    named_zero = jnp.sum((chosen_ids == 0).astype(jnp.int32), axis=1)
    rank_in = jnp.cumsum(named_zero) - named_zero
    slot_of = jnp.where(named_zero > 0, rank_in, capacity)
    matches = (slot_of[None, :] == jnp.arange(capacity, dtype=jnp.int32)[:, None]).astype(jnp.int32)
    token_ids = jnp.arange(chosen_ids.shape[0], dtype=jnp.int32) + 1
    source = jnp.sum(matches * token_ids[None, :], axis=1) - 1
    return (slot_of, source)


def fill_rows(values, source):
    picked = jnp.take(values, jnp.maximum(source, 0), axis=0)
    keep = (source >= 0).reshape((-1,) + (1,) * (values.ndim - 1))
    return jnp.where(keep, picked, jnp.zeros_like(picked))


def unfill(lookup, slot_of):
    padded = jnp.concatenate([lookup, jnp.zeros((1,) + lookup.shape[1:], lookup.dtype)], axis=0)
    return jnp.take(padded, slot_of, axis=0)


def forward_part(slot_rows, gate_cols, up_cols, down_rows):
    gate_pre = jnp.dot(slot_rows, gate_cols, preferred_element_type=jnp.float32)
    up_pre = jnp.dot(slot_rows, up_cols, preferred_element_type=jnp.float32)
    active = (gate_pre * jax.nn.sigmoid(gate_pre) * up_pre).astype(jnp.bfloat16)
    return jnp.dot(active, down_rows, preferred_element_type=jnp.float32).astype(jnp.bfloat16)


def backward_part(slot_rows, upstream_rows, weight_col, gate_cols, up_cols, down_rows):
    last_dims = (((1,), (1,)), ((), ()))
    gate_pre = jnp.dot(slot_rows, gate_cols, preferred_element_type=jnp.float32)
    up_pre = jnp.dot(slot_rows, up_cols, preferred_element_type=jnp.float32)
    gate_sig = jax.nn.sigmoid(gate_pre)
    silu_val = gate_pre * gate_sig
    active = (silu_val * up_pre).astype(jnp.bfloat16)
    back_cols = lax.dot_general(
        upstream_rows, down_rows, last_dims, preferred_element_type=jnp.float32
    )
    slope_part = jnp.sum(active.astype(jnp.float32) * back_cols, axis=1).astype(jnp.bfloat16)
    act_cot = weight_col[:, None] * back_cols
    gate_cot = (act_cot * up_pre * gate_sig * (1.0 + gate_pre * (1.0 - gate_sig))).astype(
        jnp.bfloat16
    )
    up_cot = (act_cot * silu_val).astype(jnp.bfloat16)
    row_part = (
        lax.dot_general(gate_cot, gate_cols, last_dims, preferred_element_type=jnp.float32)
        + lax.dot_general(up_cot, up_cols, last_dims, preferred_element_type=jnp.float32)
    ).astype(jnp.bfloat16)
    return (row_part, slope_part)


def run_forward(slot_rows, weights_three):
    return forward_part(slot_rows, weights_three[0], weights_three[1], weights_three[2])


def run_backward(slot_rows, upstream_rows, weight_col, weights_three):
    return backward_part(
        slot_rows, upstream_rows, weight_col, weights_three[0], weights_three[1], weights_three[2]
    )


def local(
    act_in, saved_in, grad_in, fwd_routes, bwd_routes, w_gate, w_up, w_down, router, norm_gain
):
    tok_rows = act_in.shape[1]
    capacity = tok_rows // 4
    weights_three = (w_gate[0], w_up[0], w_down[0])
    gain_row = norm_gain[0]
    router_mat = router[0]
    fwd_x = act_in[0].astype(jnp.float32)
    fwd_ids = fwd_routes[0]
    normed_f, weight_f = norm_route(fwd_x, gain_row, router_mat, fwd_ids)
    slot_f, source_f = assign_window(fwd_ids, capacity)
    send_f = fill_rows(normed_f.astype(jnp.bfloat16), source_f)
    back_x = saved_in[0].astype(jnp.float32)
    upstream = grad_in[0]
    bwd_ids = bwd_routes[0]

    def front(inputs):
        return norm_route(inputs, gain_row, router_mat, bwd_ids)

    (normed_b, weight_b), pullback = jax.vjp(front, back_x)
    slot_b, source_b = assign_window(bwd_ids, capacity)
    send_h = fill_rows(normed_b.astype(jnp.bfloat16), source_b)
    send_u = fill_rows(upstream, source_b)
    send_q = fill_rows(weight_b.astype(jnp.bfloat16), source_b)
    gathered_f = lax.all_gather(send_f, "expert", axis=0, tiled=True)
    out_part = run_forward(gathered_f, weights_three)
    expert_out = lax.psum_scatter(
        out_part.astype(jnp.float32).astype(jnp.bfloat16), "expert", scatter_dimension=0, tiled=True
    ).astype(jnp.float32)
    gathered_b = (
        lax.all_gather(send_h, "expert", axis=0, tiled=True),
        lax.all_gather(send_u, "expert", axis=0, tiled=True),
        lax.all_gather(send_q, "expert", axis=0, tiled=True),
    )
    row_part, slope_part = run_backward(
        gathered_b[0], gathered_b[1], gathered_b[2].astype(jnp.float32), weights_three
    )
    row_cot, slope_sum = (
        lax.psum_scatter(
            row_part.astype(jnp.float32).astype(jnp.bfloat16),
            "expert",
            scatter_dimension=0,
            tiled=True,
        ).astype(jnp.float32),
        lax.psum_scatter(
            slope_part.astype(jnp.float32).astype(jnp.bfloat16),
            "expert",
            scatter_dimension=0,
            tiled=True,
        ).astype(jnp.float32),
    )
    picked_f = unfill(expert_out, slot_f)
    layer_out = (fwd_x + weight_f[:, None] * picked_f).astype(jnp.bfloat16)
    act_out = shifted(layer_out[None], "section", 1)
    cot_normed = unfill(row_cot, slot_b)
    cot_weight = unfill(slope_sum, slot_b)
    d_rows = pullback((cot_normed, cot_weight))[0]
    grad_rows = (upstream.astype(jnp.float32) + d_rows).astype(jnp.bfloat16)
    grad_out = shifted(grad_rows[None], "section", -1)
    return (act_out, grad_out)


def solution(mesh):
    in_specs = (
        P("section", "expert", None),
        P("section", "expert", None),
        P("section", "expert", None),
        P("section", "expert", None),
        P("section", "expert", None),
        P("section", None, "expert"),
        P("section", None, "expert"),
        P("section", "expert", None),
        P("section", None, None),
        P("section", None),
    )
    out_specs = (P("section", "expert", None), P("section", "expert", None))
    return jax.shard_map(local, mesh=mesh, in_specs=in_specs, out_specs=out_specs, check_vma=False)
```

profile of v0, /device:TPU:1, one launch (start us, length us, event | category | flops | bytes accessed | tf_op | source)
XLA Modules:
  0.0 397.9 jit_solution(5231932063768176335)
XLA Ops:
  17.7 3.5 gather_fusion.5
  22.8 2.2 select_select_fusion
  26.0 2.7 fusion.39
  28.8 50.7 %all-gather.4.cloned.1.call-done = bf16[256,6144]{1,0:T(8,128)(2,1)} async-done(((bf16[32,6144]{1,0:T(8,128)(2,1)}), bf16[256,6144]{1,0:T(8,128)(2,1)}) %all-gather.4.cloned.1.call-update) | async-done | bytes 3145744 | tf_op jit(solution)/shard_map/all_gather | solution.py:116
  79.5 7.4 %fusion.14 = f32[256,1024]{1,0:T(8,128)S(1)} fusion(bf16[256,6144]{1,0:T(8,128)(2,1)} %all-gather.4.cloned.1.call-done, bf16[1,6144,1024]{2,1,0:T(8,128)(2,1)} %param.19), kind=kOutput, calls=%fused_computation.21 | convolution fusion | flops 3221225472 | bytes 16777216 | tf_op jit(solution)/shard_map/dot_general | solution.py:52
  87.0 18.1 %fusion.19 = bf16[256,6144]{1,0:T(8,128)(2,1)} fusion(bf16[1,1024,6144]{2,1,0:T(8,128)(2,1)} %param.21, bf16[256,6144]{1,0:T(8,128)(2,1)} %all-gather.4.cloned.1.call-done, bf16[1,6144,1024]{2,1,0:T(8,128)(2,1)} %param.20, f32[256,1024]{1,0:T(8,128)S(1)} %fusion.14), kind=kOutput, calls=%fused_computation.24 | convolution fusion | flops 6445596672 | bytes 32505856 | tf_op jit(solution)/shard_map/dot_general | solution.py:55
  107.6 33.7 %all-gather.8.cloned.1.call-done = bf16[256,6144]{1,0:T(8,128)(2,1)} async-done(((bf16[32,6144]{1,0:T(8,128)(2,1)}), bf16[256,6144]{1,0:T(8,128)(2,1)}) %all-gather.8.cloned.1.call-update) | async-done | bytes 3145744 | tf_op jit(solution)/shard_map/all_gather | solution.py:122
  141.4 9.1 %fusion.6 = f32[256,1024]{1,0:T(8,128)S(1)} fusion(bf16[256,6144]{1,0:T(8,128)(2,1)} %all-gather.8.cloned.1.call-done, bf16[1,6144,1024]{2,1,0:T(8,128)(2,1)} %param.20), kind=kOutput, calls=%fused_computation.13 | convolution fusion | flops 3221225472 | bytes 16777216 | tf_op jit(solution)/shard_map/dot_general | solution.py:61
  150.5 7.7 %fusion.12 = f32[256,1024]{1,0:T(8,128)} fusion(bf16[256,6144]{1,0:T(8,128)(2,1)S(1)} %copy-done.10, bf16[1,6144,1024]{2,1,0:T(8,128)(2,1)} %param.19), kind=kOutput, calls=%fused_computation.19 | convolution fusion | flops 3221225472 | bytes 16777216 | tf_op jit(solution)/shard_map/dot_general | solution.py:60
  158.3 44.4 %all-gather.6.cloned.1.call-done = bf16[256,6144]{1,0:T(8,128)(2,1)} async-done(((bf16[32,6144]{1,0:T(8,128)(2,1)}), bf16[256,6144]{1,0:T(8,128)(2,1)}) %all-gather.6.cloned.1.call-update) | async-done | bytes 3145744 | tf_op jit(solution)/shard_map/all_gather | solution.py:123
  202.7 10.2 %multiply_reduce_fusion = (bf16[256]{0:T(256)(128)(2,1)S(1)}, f32[256,1024]{1,0:T(8,128)}) fusion(f32[256,1024]{1,0:T(8,128)S(1)} %fusion.6, f32[256,1024]{1,0:T(8,128)} %fusion.12, bf16[256,6144]{1,0:T(8,128)(2,1)} %all-gather.6.cloned.1.call-done, bf16[1,1024,6144]{2,1,0:T(8,128)(2,1)} %param.21), kind=kOutput, calls=%fused_computation.65 | convolution fusion | flops 3223584512 | bytes 18874880 | tf_op jit(solution)/shard_map/dot_general | solution.py:65
  212.9 17.3 %all-reduce.6 = (bf16[256]{0:T(256)(128)(2,1)S(1)}, bf16[256]{0:T(256)(128)(2,1)S(1)}) all-reduce(bf16[256]{0:T(256)(128)(2,1)S(1)} %get-tuple-element.32, bf16[256]{0:T(256)(128)(2,1)S(1)} %dynamic-update-slice), channel_id=4, replica_groups=mesh['section'=4,'expert'=8] {'expert'}, use_global_device_ids=true, to_apply=%region_15.18.clone | all-reduce | flops 512 | bytes 2048
  230.2 11.7 %fusion.4 = f32[256,6144]{1,0:T(8,128)} fusion(bf16[1,6144,1024]{2,1,0:T(8,128)(2,1)} %param.20, f32[256,1024]{1,0:T(8,128)} %get-tuple-element.33, f32[256]{0:T(256)S(1)} %convert_element_type.98, f32[256,1024]{1,0:T(8,128)} %fusion.12), kind=kOutput, calls=%fused_computation.11 | convolution fusion | flops 3223060480 | bytes 20972544 | tf_op jit(solution)/shard_map/dot_general | solution.py:76
  241.9 12.5 %fusion.22 = bf16[256,6144]{1,0:T(8,128)(2,1)} fusion(f32[256,6144]{1,0:T(8,128)} %fusion.4, bf16[1,6144,1024]{2,1,0:T(8,128)(2,1)} %param.19, f32[256,1024]{1,0:T(8,128)} %fusion.12, f32[256,1024]{1,0:T(8,128)S(1)} %fusion.6, f32[256,1024]{1,0:T(8,128)} %get-tuple-element.33, f32[256]{0:T(256)S(1)} %convert_element_type.98), kind=kOutput, calls=%fused_computation.25 | convolution fusion | flops 3227254784 | bytes 25166848 | tf_op jit(solution)/shard_map/dot_general | solution.py:75
  255.9 2.7 fusion.47
  260.1 19.4 %reduce-scatter.3.cloned.1.call-done = bf16[32,6144]{1,0:T(8,128)(2,1)} async-done(((bf16[256,6144]{1,0:T(8,128)(2,1)}), bf16[32,6144]{1,0:T(8,128)(2,1)}) %reduce-scatter.3.cloned.1.call-update) | async-done | bytes 393232 | tf_op jit(solution)/shard_map/reduce_scatter | solution.py:118
  280.5 3.2 gather_fusion.3
  283.7 4.1 %fusion.52 = bf16[1,128,6144]{2,1,0:T(8,128)(2,1)} fusion(f32[128,6144]{1,0:T(8,128)} %gather_fusion.3, bf16[1,128,6144]{2,1,0:T(8,128)(2,1)} %param.14, f32[128]{0:T(128)S(1)} %fusion.72, pred[128]{0:T(512)(128)(4,1)S(1)} %get-tuple-element.18), kind=kLoop, calls=%fused_computation.58 | loop fusion | flops 3932160 | bytes 6292096 | tf_op jit(solution)/shard_map/broadcast_in_dim | solution.py:145
  287.8 2.4 collective-permute-start
  290.2 66.3 %reduce-scatter.5.cloned.1.call-done = bf16[32,6144]{1,0:T(8,128)(2,1)} async-done(((bf16[256,6144]{1,0:T(8,128)(2,1)}), bf16[32,6144]{1,0:T(8,128)(2,1)}) %reduce-scatter.5.cloned.1.call-update) | async-done | bytes 393232 | tf_op jit(solution)/shard_map/reduce_scatter | solution.py:130
  357.6 3.2 gather_fusion.6
  360.8 5.2 %fusion.36 = (f32[128]{0:T(128)S(1)}, f32[128,6144]{1,0:T(8,128)S(1)}) fusion(bf16[1,128,6144]{2,1,0:T(8,128)(2,1)S(1)} %copy-done.1, f32[6144]{0:T(1024)S(1)} %bitcast.131, f32[128,8]{0,1:T(8,128)S(1)} %select_reduce_fusion.2, f32[1,6144,8]{1,2,0:T(8,128)S(1)} %copy-done, f32[128,6144]{1,0:T(8,128)} %gather_fusion.6, pred[128]{0:T(512)(128)(4,1)S(1)} %get-tuple-element.15), kind=kOutput, calls=%fused_computation.43 | convolution fusion | flops 80215936 | bytes 8090240 | tf_op jit(solution)/shard_map/transpose(jvp())/dot_general | solution.py:19
  368.3 19.2 %collective-permute-done.1 = bf16[1,128,6144]{2,1,0:T(8,128)(2,1)S(1)} collective-permute-done((bf16[1,128,6144]{2,1,0:T(8,128)(2,1)S(1)}, bf16[1,128,6144]{2,1,0:T(8,128)(2,1)S(1)}, u32[]{:S(2)}, u32[]{:S(2)}) %collective-permute-start.1) | collective-permute-done | bytes 1572896 | tf_op jit(solution)/shard_map/ppermute | solution.py:13
  387.5 2.7 copy.46
  (87 shorter events, 22.6 us)
Async XLA Ops:
  7.2 18.8 %copy-start = (f32[1,6144,8]{1,2,0:T(8,128)S(1)}, f32[1,6144,8]{1,2,0:T(8,128)}, u32[]{:S(2)}) copy-start(f32[1,6144,8]{1,2,0:T(8,128)} %param.22) | copy-start | bytes 589828
  7.2 4.4 %copy-start.1 = (bf16[1,128,6144]{2,1,0:T(8,128)(2,1)S(1)}, bf16[1,128,6144]{2,1,0:T(8,128)(2,1)}, u32[]{:S(2)}) copy-start(bf16[1,128,6144]{2,1,0:T(8,128)(2,1)} %param.15) | copy-start | bytes 4718596
  7.2 4.9 %copy-start.6 = (f32[1,6144]{1,0:T(1,128)S(1)}, f32[1,6144]{1,0:T(1,128)}, u32[]{:S(2)}) copy-start(f32[1,6144]{1,0:T(1,128)} %param.23) | copy-start | bytes 73732
  7.2 72.3 %all-gather.4.cloned.1.call-start = ((), (), s32[]{:S(2)}) async-start(), calls=%async_computation.2 | async-start | bytes 3538944 | tf_op jit(solution)/shard_map/all_gather | solution.py:116
  9.6 2.5 copy-start.4
  15.7 5.6 %copy-start.2 = (bf16[1,128,6144]{2,1,0:T(8,128)(2,1)S(1)}, bf16[1,128,6144]{2,1,0:T(8,128)(2,1)}, u32[]{:S(2)}) copy-start(bf16[1,128,6144]{2,1,0:T(8,128)(2,1)} %param.16) | copy-start | bytes 4718596
  17.7 123.7 %all-gather.8.cloned.1.call-start = ((), (), s32[]{:S(2)}) async-start(), calls=%async_computation.5 | async-start | bytes 3538944 | tf_op jit(solution)/shard_map/all_gather | solution.py:122
  22.8 5.9 %copy-start.7 = (s32[1,128,2]{1,2,0:T(2,128)S(1)}, s32[1,128,2]{1,2,0:T(2,128)}, u32[]{:S(2)}) copy-start(s32[1,128,2]{1,2,0:T(2,128)} %param.18) | copy-start | bytes 3076
  25.0 177.7 %all-gather.6.cloned.1.call-start = ((), (), s32[]{:S(2)}) async-start(), calls=%async_computation.4 | async-start | bytes 3538944 | tf_op jit(solution)/shard_map/all_gather | solution.py:123
  25.8 253.7 %reduce-scatter.3.cloned.1.call-start = ((), (), s32[]{:S(2)}) async-start(), calls=%async_computation.3 | async-start | bytes 3538944 | tf_op jit(solution)/shard_map/reduce_scatter | solution.py:118
  105.0 1.0 copy-start.9
  105.0 251.5 %reduce-scatter.5.cloned.1.call-start = ((), (), s32[]{:S(2)}) async-start(), calls=%async_computation.6 | async-start | bytes 3538944 | tf_op jit(solution)/shard_map/reduce_scatter | solution.py:130
  141.4 9.1 %copy-start.10 = (bf16[256,6144]{1,0:T(8,128)(2,1)S(1)}, bf16[256,6144]{1,0:T(8,128)(2,1)}, u32[]{:S(2)}) copy-start(bf16[256,6144]{1,0:T(8,128)(2,1)} %all-gather.8.cloned.1.call-done) | copy-start | bytes 9437188
  254.4 1.4 copy-start.5
  254.4 4.2 %copy-start.8 = (s32[1,128,2]{1,2,0:T(2,128)S(1)}, s32[1,128,2]{1,2,0:T(2,128)}, u32[]{:S(2)}) copy-start(s32[1,128,2]{1,2,0:T(2,128)} %param.17) | copy-start | bytes 3076
  287.8 80.5 %collective-permute-start = (bf16[1,128,6144]{2,1,0:T(8,128)(2,1)}, bf16[1,128,6144]{2,1,0:T(8,128)(2,1)}, u32[]{:S(2)}, u32[]{:S(2)}) collective-permute-start(bf16[1,128,6144]{2,1,0:T(8,128)(2,1)} %fusion.52), channel_id=1, source_target_pairs={{0,8},{8,16},{16,24},{24,0},{1,9},{9,17},{17,25},{25,1},{2,10},{10... | collective-permute-start | bytes 4718600 | tf_op jit(solution)/shard_map/ppermute | solution.py:13
  360.8 5.3 %copy-start.3 = (bf16[1,128,6144]{2,1,0:T(8,128)(2,1)S(1)}, bf16[1,128,6144]{2,1,0:T(8,128)(2,1)}, u32[]{:S(2)}) copy-start(bf16[1,128,6144]{2,1,0:T(8,128)(2,1)} %param.16) | copy-start | bytes 4718596
  366.9 20.6 %collective-permute-start.1 = (bf16[1,128,6144]{2,1,0:T(8,128)(2,1)S(1)}, bf16[1,128,6144]{2,1,0:T(8,128)(2,1)S(1)}, u32[]{:S(2)}, u32[]{:S(2)}) collective-permute-start(bf16[1,128,6144]{2,1,0:T(8,128)(2,1)S(1)} %fusion.51), channel_id=1, source_target_pairs={{0,24},{8,0},{16,8},{24,16},{1,25},{9,1},{17,9},{25,17},{2,26},{10... | collective-permute-start | bytes 4718600 | tf_op jit(solution)/shard_map/ppermute | solution.py:13
Sparse Core Ops, SparseCore 0:
  17.8 61.6 all-gather.3
  82.3 59.0 all-gather.7
  143.6 59.0 all-gather.5
  206.1 73.3 reduce-scatter.2
  282.9 73.5 reduce-scatter.4
where the time goes:
time: 398 us
  waiting for transfers between devices  234 us (59%)
  matrix products  87.5 us (22%)
  local copies, waits for them, and re-layouts  20.5 us (5%)
  other arithmetic  18.1 us (5%)
  blocking collectives  17.3 us (4%)
  between operations  15.5 us (4%)
  starting transfers between devices  4.47 us (1%)
    reduce_scatter x1, waiting for transfers between devices, local(): lax.psum_scatter(row_part.astype(jnp.float32).astype(jnp.bfloat16), 'expe...  66.3 us
    all_gather x1, waiting for transfers between devices, local(): gathered_f = lax.all_gather(send_f, 'expert', axis=0, tiled=True)  50.7 us
    all_gather x1, waiting for transfers between devices, local(): lax.all_gather(send_u, 'expert', axis=0, tiled=True)  44.4 us
    all_gather x1, waiting for transfers between devices, local(): lax.all_gather(send_h, 'expert', axis=0, tiled=True)  33.7 us
    reduce_scatter x1, waiting for transfers between devices, local(): lax.psum_scatter(out_part.astype(jnp.float32).astype(jnp.bfloat16), 'expe...  19.4 us
    ppermute x2, waiting for transfers between devices, shifted(): return lax.ppermute(value, axis, pairs)  19.2 us
    dot_general x1, matrix products, forward_part(): jnp.dot(active, down_rows, preferred_element_type=jnp.float32)  18.1 us
    unnamed x1, blocking collectives  17.3 us
  transfers between devices with their start and end apart: 7, of which 6 were waited for; matrix products, arithmetic and copies ran while one was open for 28% of the time, Pallas kernels for 0%

commit v1 on v0

v1 whole, which is shorter than its diff:
```python
import jax
import jax.numpy as jnp
from jax import lax
from jax.experimental import pallas as pl
from jax.experimental.pallas import tpu as pltpu
from jax.sharding import PartitionSpec as P

epsilon = 1e-05
highest = lax.Precision.HIGHEST
f32 = jnp.float32
bf16 = jnp.bfloat16
last_dims = (((1,), (1,)), ((), ()))
vmem_limit = 48 * 1024 * 1024


def ring_of(count):
    return list(range(0, count, 2)) + list(range(1, count, 2))[::-1]


def hop(value, steps):
    ring = ring_of(lax.axis_size("expert"))
    count = len(ring)
    return lax.ppermute(value, "expert", [(ring[i], ring[(i + steps) % count]) for i in range(count)])


def shifted(value, steps):
    count = lax.axis_size("section")
    return lax.ppermute(value, "section", [(source, (source + steps) % count) for source in range(count)])


def halves(value):
    middle = value.shape[1] // 2
    return [value[:, :middle], value[:, middle:]]


def reach(count, chunk):
    far, near = count // 2, (count - 1) // 2
    return (far, near) if chunk == 0 else (near, far)


def ring_gather(chunks):
    count = lax.axis_size("expert")
    held = [[None] * count for _ in chunks]
    state = []
    for c, value in enumerate(chunks):
        held[c][0] = value
        state.append([value, value])
    for step in range(count // 2):
        for c in range(len(chunks)):
            for way in (0, 1):
                if step < reach(count, c)[way]:
                    state[c][way] = hop(state[c][way], 1 - 2 * way)
                    held[c][(-1 - step) % count if way == 0 else step + 1] = state[c][way]
    return held


def ring_scatter(parts):
    count = lax.axis_size("expert")
    state = []
    for c in range(len(parts)):
        fore, back = reach(count, c)
        state.append([parts[c][fore], parts[c][-back % count]])
    for step in range(count // 2):
        for c in range(len(parts)):
            for way in (0, 1):
                left = reach(count, c)[way] - step
                if left <= 0:
                    continue
                value = hop(state[c][way], 1 - 2 * way)
                if left > 1:
                    own = parts[c][(left - 1) if way == 0 else (1 - left) % count]
                    value = (value.astype(f32) + own.astype(f32)).astype(bf16)
                state[c][way] = value
    return [
        parts[c][0].astype(f32) + state[c][0].astype(f32) + state[c][1].astype(f32) for c in range(len(parts))
    ]


def cost(flops, moved):
    return pl.CostEstimate(flops=int(flops), bytes_accessed=int(moved), transcendentals=0)


def params():
    return pltpu.CompilerParams(vmem_limit_bytes=vmem_limit)


def dot_t(left, right):
    return lax.dot_general(left, right, last_dims, preferred_element_type=f32)


def dot_n(left, right):
    return jnp.dot(left, right, preferred_element_type=f32)


def whole(array):
    return pl.BlockSpec(array.shape, lambda i: (0,) * array.ndim)


def back_kernel(rows_ref, down_ref, out_ref):
    out_ref[...] = dot_t(rows_ref[...], down_ref[...])


def back_call(rows, down):
    count, width = rows.shape
    hid = down.shape[0]
    block = min(256, hid)
    return pl.pallas_call(
        back_kernel,
        grid=(hid // block,),
        in_specs=[whole(rows), pl.BlockSpec((block, width), lambda i: (i, 0))],
        out_specs=pl.BlockSpec((count, block), lambda i: (0, i)),
        out_shape=jax.ShapeDtypeStruct((count, hid), f32),
        compiler_params=params(),
        cost_estimate=cost(2 * count * width * hid, 2 * width * (hid + count)),
    )(rows, down)


def cots_kernel(rows_ref, gate_ref, up_ref, back_ref, gate_cot_ref, up_cot_ref, slope_ref):
    gate_pre = dot_n(rows_ref[...], gate_ref[...])
    up_pre = dot_n(rows_ref[...], up_ref[...])
    sig = jax.nn.sigmoid(gate_pre)
    silu = gate_pre * sig
    back = back_ref[...]
    active = (silu * up_pre).astype(bf16).astype(f32)
    part = jnp.sum(active * back, axis=1, keepdims=True)

    @pl.when(pl.program_id(0) == 0)
    def _():
        slope_ref[...] = jnp.zeros_like(slope_ref)

    slope_ref[...] += jnp.broadcast_to(part, slope_ref.shape)
    gate_cot_ref[...] = (back * up_pre * sig * (1.0 + gate_pre * (1.0 - sig))).astype(bf16)
    up_cot_ref[...] = (back * silu).astype(bf16)


def cots_call(rows, gate, up, back):
    count, width = rows.shape
    hid = gate.shape[1]
    block = min(256, hid)
    wide = pl.BlockSpec((width, block), lambda i: (0, i))
    tall = pl.BlockSpec((count, block), lambda i: (0, i))
    return pl.pallas_call(
        cots_kernel,
        grid=(hid // block,),
        in_specs=[whole(rows), wide, wide, tall],
        out_specs=[tall, tall, pl.BlockSpec((count, 128), lambda i: (0, 0))],
        out_shape=[
            jax.ShapeDtypeStruct((count, hid), bf16),
            jax.ShapeDtypeStruct((count, hid), bf16),
            jax.ShapeDtypeStruct((count, 128), f32),
        ],
        compiler_params=params(),
        cost_estimate=cost(4 * count * width * hid, 2 * width * (2 * hid + count)),
    )(rows, gate, up, back)


def rowpart_kernel(gate_cot_ref, up_cot_ref, gate_ref, up_ref, out_ref):
    out_ref[...] = (
        dot_t(gate_cot_ref[...], gate_ref[...]) + dot_t(up_cot_ref[...], up_ref[...])
    ).astype(bf16)


def rowpart_call(gate_cot, up_cot, gate, up, chunk):
    count, hid = gate_cot.shape
    width = gate.shape[0] // 2
    block = 512 if width % 512 == 0 else 128
    steps = width // block
    wide = pl.BlockSpec((block, hid), lambda i: (i + chunk * steps, 0))
    return pl.pallas_call(
        rowpart_kernel,
        grid=(steps,),
        in_specs=[whole(gate_cot), whole(up_cot), wide, wide],
        out_specs=pl.BlockSpec((count, block), lambda i: (0, i)),
        out_shape=jax.ShapeDtypeStruct((count, width), bf16),
        compiler_params=params(),
        cost_estimate=cost(4 * count * width * hid, 4 * width * hid),
    )(gate_cot, up_cot, gate, up)


def active_kernel(rows_ref, gate_ref, up_ref, out_ref):
    gate_pre = dot_n(rows_ref[...], gate_ref[...])
    up_pre = dot_n(rows_ref[...], up_ref[...])
    out_ref[...] = (gate_pre * jax.nn.sigmoid(gate_pre) * up_pre).astype(bf16)


def active_call(rows, gate, up):
    count, width = rows.shape
    hid = gate.shape[1]
    block = min(256, hid)
    wide = pl.BlockSpec((width, block), lambda i: (0, i))
    return pl.pallas_call(
        active_kernel,
        grid=(hid // block,),
        in_specs=[whole(rows), wide, wide],
        out_specs=pl.BlockSpec((count, block), lambda i: (0, i)),
        out_shape=jax.ShapeDtypeStruct((count, hid), bf16),
        compiler_params=params(),
        cost_estimate=cost(4 * count * width * hid, 2 * width * (2 * hid + count)),
    )(rows, gate, up)


def outpart_kernel(active_ref, down_ref, out_ref):
    out_ref[...] = dot_n(active_ref[...], down_ref[...]).astype(bf16)


def outpart_call(active, down, chunk):
    count, hid = active.shape
    width = down.shape[1] // 2
    block = 512 if width % 512 == 0 else 128
    steps = width // block
    return pl.pallas_call(
        outpart_kernel,
        grid=(steps,),
        in_specs=[whole(active), pl.BlockSpec((hid, block), lambda i: (0, i + chunk * steps))],
        out_specs=pl.BlockSpec((count, block), lambda i: (0, i)),
        out_shape=jax.ShapeDtypeStruct((count, width), bf16),
        compiler_params=params(),
        cost_estimate=cost(2 * count * width * hid, 2 * width * hid),
    )(active, down)


def select_matrix(ids, capacity):
    tokens = ids.shape[0]
    named = jnp.sum((ids == 0).astype(bf16), axis=1)
    earlier = jnp.tril(jnp.ones((tokens, tokens), bf16), -1)
    rank = jnp.dot(earlier, named, preferred_element_type=f32)
    slot = jnp.where(named > 0, rank, float(capacity))
    return (slot[None, :] == jnp.arange(capacity, dtype=f32)[:, None]).astype(bf16)


def pick_ids(select, ids):
    return jnp.dot(select, ids.astype(bf16), preferred_element_type=f32).astype(jnp.int32)


def norm_route(inputs, gain_row, router_mat, chosen_ids):
    inverse = lax.rsqrt(jnp.mean(inputs * inputs, axis=1, keepdims=True) + epsilon)
    normed = inputs * inverse * gain_row[None, :]
    logits = jnp.dot(normed, router_mat, precision=highest)
    onehot = (
        chosen_ids[:, :, None] == jnp.arange(router_mat.shape[1], dtype=jnp.int32)[None, None, :]
    ).astype(f32)
    picked = jnp.sum(onehot * logits[:, None, :], axis=2)
    first_share = jax.nn.sigmoid(picked[:, 0] - picked[:, 1])
    shares = jnp.stack([first_share, 1.0 - first_share], axis=1)
    return (normed, jnp.sum(shares * (chosen_ids == 0).astype(f32), axis=1))


def split_rows(array, count):
    rows = array.shape[0] // count
    return [array[k * rows : (k + 1) * rows] for k in range(count)]


def joined(held):
    return jnp.concatenate([jnp.concatenate(shards, axis=0) for shards in held], axis=1)


def place(select, rows, base):
    spread = lax.dot_general(select, rows, (((0,), (0,)), ((), ())), preferred_element_type=f32).astype(bf16)
    used = jnp.sum(select.astype(f32), axis=0) > 0
    return jnp.where(used[:, None], spread, base)


def local(
    act_in, saved_in, grad_in, fwd_routes, bwd_routes, w_gate, w_up, w_down, router, norm_gain
):
    count = lax.axis_size("expert")
    capacity = act_in.shape[1] // 4
    gate, up, down = w_gate[0], w_up[0], w_down[0]
    gain_row, router_mat = norm_gain[0], router[0]
    fwd_ids, bwd_ids = fwd_routes[0], bwd_routes[0]

    select_b = select_matrix(bwd_ids, capacity)
    rows_u = jnp.dot(select_b, grad_in[0], preferred_element_type=f32)
    held_u = ring_gather(halves(rows_u.astype(bf16)))

    rows_b = jnp.dot(select_b, saved_in[0], preferred_element_type=f32)
    ids_b = pick_ids(select_b, bwd_ids)
    (normed_b, weight_b), pullback = jax.vjp(
        lambda inputs: norm_route(inputs, gain_row, router_mat, ids_b), rows_b
    )
    held_h = ring_gather(halves(normed_b.astype(bf16)))

    select_f = select_matrix(fwd_ids, capacity)
    rows_f = jnp.dot(select_f, act_in[0], preferred_element_type=f32)
    normed_f, weight_f = norm_route(rows_f, gain_row, router_mat, pick_ids(select_f, fwd_ids))
    held_f = ring_gather(halves(normed_f.astype(bf16)))

    act_base = shifted(act_in[0], 1)
    grad_base = shifted(grad_in[0], -1)
    select_f_there = shifted(select_f, 1)
    select_b_there = shifted(select_b, -1)

    back = back_call(joined(held_u), down)
    gate_cot, up_cot, slope = cots_call(joined(held_h), gate, up, back)
    row_parts = [split_rows(rowpart_call(gate_cot, up_cot, gate, up, c), count) for c in (0, 1)]
    slope_parts = split_rows(slope.astype(bf16), count)
    row_parts[1] = [jnp.concatenate(pair, axis=1) for pair in zip(row_parts[1], slope_parts, strict=True)]

    active = active_call(joined(held_f), gate, up)
    out_parts = [split_rows(outpart_call(active, down, c), count) for c in (0, 1)]

    sums = ring_scatter(row_parts)
    middle = sums[0].shape[1]
    scale = weight_b.astype(bf16).astype(f32)[:, None]
    cot_normed = jnp.concatenate([sums[0], sums[1][:, :middle]], axis=1) * scale
    d_rows = pullback((cot_normed, sums[1][:, middle]))[0]
    grad_rows = shifted((rows_u + d_rows).astype(bf16), -1)

    sums_f = ring_scatter(out_parts)
    layer_rows = [
        shifted((base + weight_f[:, None] * total).astype(bf16), 1)
        for base, total in zip(halves(rows_f), sums_f, strict=True)
    ]
    act_out = place(select_f_there, jnp.concatenate(layer_rows, axis=1), act_base)
    grad_out = place(select_b_there, grad_rows, grad_base)
    return (act_out[None], grad_out[None])


def solution(mesh):
    in_specs = (
        P("section", "expert", None),
        P("section", "expert", None),
        P("section", "expert", None),
        P("section", "expert", None),
        P("section", "expert", None),
        P("section", None, "expert"),
        P("section", None, "expert"),
        P("section", "expert", None),
        P("section", None, None),
        P("section", None),
    )
    out_specs = (P("section", "expert", None), P("section", "expert", None))
    return jax.shard_map(local, mesh=mesh, in_specs=in_specs, out_specs=out_specs, check_vma=False)
```

time: 398 us -> 328 us (0.82)
  starting transfers between devices: 4.47 us -> 115 us
  waiting for transfers between devices: 234 us -> 130 us
  matrix products: 87.5 us -> 9.4 us
  Pallas kernels: 0 us -> 57.7 us
  blocking collectives: 17.3 us -> 0 us
  local copies, waits for them, and re-layouts: 20.5 us -> 5.2 us
  between operations: 15.5 us -> 1.55 us
  other arithmetic: 18.1 us -> 4.94 us
    all_gather x3 -> x0, waiting for transfers between devices: 129 us -> none  [the longest x1 50.7 us: local(): gathered_f = lax.all_gather(send_f, 'expert', axis=0, tiled=True)]
    ppermute x2 -> x77, starting transfers between devices: 3.87 us -> 115 us  [the longest x70 71.5 us: hop(): lax.ppermute(value, 'expert', [(ring[i], ring[(i + steps) % count]) for i...]
    ppermute x2 -> x77, waiting for transfers between devices: 19.2 us -> 130 us  [the longest x70 122 us: hop(): lax.ppermute(value, 'expert', [(ring[i], ring[(i + steps) % count]) for i...]
    reduce_scatter x2 -> x0, waiting for transfers between devices: 85.6 us -> none  [the longest x1 66.3 us: local(): lax.psum_scatter(row_part.astype(jnp.float32).astype(jnp.bfloat16), 'expe...]
    dot_general x7 -> x9, matrix products: 76.8 us -> 6.8 us  [the longest x2 4.88 us: place(): lax.dot_general(select, rows, (((0,), (0,)), ((), ())), preferred_element...]
    pallas_call x0 -> x7, Pallas kernels: none -> 57.7 us  [the longest x2 16 us: rowpart_call(): pl.pallas_call(rowpart_kernel, grid=(steps,), in_specs=[whole(gate_cot),...]
    unnamed x1 -> x0, blocking collectives: 17.3 us -> none
    gather x7 -> x0, local copies, waits for them, and re-layouts: 14.9 us -> none  [the longest x3 7.58 us: unfill(): return jnp.take(padded, slot_of, axis=0)]
  transfers between devices with their start and end apart: 7 -> 77, of which waited for: 6 -> 39; matrix products, arithmetic and copies ran while one was open for 28% -> 4% of each run, Pallas kernels for 0% -> 18%
where the time goes in v1:
time: 328 us; the launch traced here: 324 us
  waiting for transfers between devices  130 us (40%)
  starting transfers between devices  115 us (35%)
  Pallas kernels  57.7 us (18%)
  matrix products  9.4 us (3%)
  local copies, waits for them, and re-layouts  5.2 us (2%)
  other arithmetic  4.94 us (2%)
    ppermute x70, waiting for transfers between devices, hop(): lax.ppermute(value, 'expert', [(ring[i], ring[(i + steps) % count]) for i...  122 us
    ppermute x70, starting transfers between devices, hop(): lax.ppermute(value, 'expert', [(ring[i], ring[(i + steps) % count]) for i...  71.5 us
    ppermute x7, starting transfers between devices, shifted(): lax.ppermute(value, 'section', [(source, (source + steps) % count) for so...  43.8 us
    pallas_call x2, Pallas kernels, rowpart_call(): pl.pallas_call(rowpart_kernel, grid=(steps,), in_specs=[whole(gate_cot),...  16 us
    pallas_call x1, Pallas kernels, cots_call(): pl.pallas_call(cots_kernel, grid=(hid // block,), in_specs=[whole(rows),...  12 us
    pallas_call x1, Pallas kernels, active_call(): pl.pallas_call(active_kernel, grid=(hid // block,), in_specs=[whole(rows)...  11.4 us
    pallas_call x2, Pallas kernels, outpart_call(): pl.pallas_call(outpart_kernel, grid=(steps,), in_specs=[whole(active), pl...  11.3 us
    ppermute x7, waiting for transfers between devices, shifted(): lax.ppermute(value, 'section', [(source, (source + steps) % count) for so...  8.45 us
  transfers between devices with their start and end apart: 77, of which 39 were waited for; matrix products, arithmetic and copies ran while one was open for 4% of the time, Pallas kernels for 18%

profile of v1, /device:TPU:1, one launch (start us, length us, event | category | flops | bytes accessed | tf_op | source)
XLA Modules:
  0.0 324.2 jit_solution(17347314459044512482)
XLA Ops:
  34.3 4.3 %collective-permute-done.34 = bf16[32,3072]{1,0:T(8,128)(2,1)S(1)} collective-permute-done((bf16[32,3072]{1,0:T(8,128)(2,1)S(1)}, bf16[32,3072]{1,0:T(8,128)(2,1)S(1)}, u32[]{:S(2)}, u32[]{:S(2)}) %collective-permute-start.34) | collective-permute-done | bytes 196640 | tf_op jit(solution)/shard_map/ppermute | solution.py:23
  39.8 5.5 %collective-permute-done.41 = bf16[32,3072]{1,0:T(8,128)(2,1)S(1)} collective-permute-done((bf16[32,3072]{1,0:T(8,128)(2,1)S(1)}, bf16[32,3072]{1,0:T(8,128)(2,1)S(1)}, u32[]{:S(2)}, u32[]{:S(2)}) %collective-permute-start.41) | collective-permute-done | bytes 196640 | tf_op jit(solution)/shard_map/ppermute | solution.py:23
  46.7 4.6 %collective-permute-done.48 = bf16[32,3072]{1,0:T(8,128)(2,1)S(1)} collective-permute-done((bf16[32,3072]{1,0:T(8,128)(2,1)S(1)}, bf16[32,3072]{1,0:T(8,128)(2,1)S(1)}, u32[]{:S(2)}, u32[]{:S(2)}) %collective-permute-start.48) | collective-permute-done | bytes 196640 | tf_op jit(solution)/shard_map/ppermute | solution.py:23
  52.7 3.6 %collective-permute-done.55 = bf16[32,3072]{1,0:T(8,128)(2,1)S(1)} collective-permute-done((bf16[32,3072]{1,0:T(8,128)(2,1)S(1)}, bf16[32,3072]{1,0:T(8,128)(2,1)S(1)}, u32[]{:S(2)}, u32[]{:S(2)}) %collective-permute-start.55) | collective-permute-done | bytes 196640 | tf_op jit(solution)/shard_map/ppermute | solution.py:23
  66.2 4.0 %collective-permute-done.35 = bf16[32,3072]{1,0:T(8,128)(2,1)S(1)} collective-permute-done((bf16[32,3072]{1,0:T(8,128)(2,1)S(1)}, bf16[32,3072]{1,0:T(8,128)(2,1)S(1)}, u32[]{:S(2)}, u32[]{:S(2)}) %collective-permute-start.35) | collective-permute-done | bytes 196640 | tf_op jit(solution)/shard_map/ppermute | solution.py:23
  71.6 4.3 %collective-permute-done.42 = bf16[32,3072]{1,0:T(8,128)(2,1)S(1)} collective-permute-done((bf16[32,3072]{1,0:T(8,128)(2,1)S(1)}, bf16[32,3072]{1,0:T(8,128)(2,1)S(1)}, u32[]{:S(2)}, u32[]{:S(2)}) %collective-permute-start.42) | collective-permute-done | bytes 196640 | tf_op jit(solution)/shard_map/ppermute | solution.py:23
  77.4 4.8 %collective-permute-done.49 = bf16[32,3072]{1,0:T(8,128)(2,1)S(1)} collective-permute-done((bf16[32,3072]{1,0:T(8,128)(2,1)S(1)}, bf16[32,3072]{1,0:T(8,128)(2,1)S(1)}, u32[]{:S(2)}, u32[]{:S(2)}) %collective-permute-start.49) | collective-permute-done | bytes 196640 | tf_op jit(solution)/shard_map/ppermute | solution.py:23
  83.6 4.7 %collective-permute-done.56 = bf16[32,3072]{1,0:T(8,128)(2,1)S(1)} collective-permute-done((bf16[32,3072]{1,0:T(8,128)(2,1)S(1)}, bf16[32,3072]{1,0:T(8,128)(2,1)S(1)}, u32[]{:S(2)}, u32[]{:S(2)}) %collective-permute-start.56) | collective-permute-done | bytes 196640 | tf_op jit(solution)/shard_map/ppermute | solution.py:23
  114.3 23.9 %collective-permute-start.76 = (bf16[128,6144]{1,0:T(8,128)(2,1)S(1)}, bf16[128,6144]{1,0:T(8,128)(2,1)}, u32[]{:S(2)}, u32[]{:S(2)}) collective-permute-start(bf16[128,6144]{1,0:T(8,128)(2,1)S(1)} %bitcast.71), channel_id=1, source_target_pairs={{0,24},{8,0},{16,8},{24,16},{1,25},{9,1},{17,9},{25,17},{2,26},{10... | collective-permute-start | bytes 4718600 | tf_op jit(solution)/shard_map/ppermute | solution.py:28
  142.6 15.4 %collective-permute-done.53 = bf16[32,3072]{1,0:T(8,128)(2,1)S(1)} collective-permute-done((bf16[32,3072]{1,0:T(8,128)(2,1)S(1)}, bf16[32,3072]{1,0:T(8,128)(2,1)S(1)}, u32[]{:S(2)}, u32[]{:S(2)}) %collective-permute-start.53) | collective-permute-done | bytes 196640 | tf_op jit(solution)/shard_map/ppermute | solution.py:23
  164.1 7.1 %shard_map.116.back_ref = f32[256,1024]{1,0:T(8,128)S(1)} custom-call(bf16[256,6144]{1,0:T(8,128)(2,1)S(1)} %pad_maximum_fusion.2.rows_ref, bf16[1024,6144]{1,0:T(8,128)(2,1)} %bitcast.68), custom_call_target="tpu_custom_call" | custom-call | flops 3221225472 | bytes 15728640 | tf_op jit(solution)/shard_map/pallas_call | solution.py:107
  171.2 12.0 %shard_map.117 = (bf16[256,1024]{1,0:T(8,128)(2,1)S(1)}, bf16[256,1024]{1,0:T(8,128)(2,1)S(1)}, f32[256,128]{1,0:T(8,128)S(1)}) custom-call(bf16[256,6144]{1,0:T(8,128)(2,1)S(1)} %pad_maximum_fusion.1.rows_ref, bf16[6144,1024]{1,0:T(8,128)(2,1)} %bitcast.60, bf16[6144,1024]{1,0:T(8,128)(2,1)} %bitcast.64, f32[256,1024]{1,0:T(8,128)S(1)} %shard_map.116.back_ref), custom_call_target="tpu_custom_call" | custom-call | flops 6442450944 | bytes 28311552 | tf_op jit(solution)/shard_map/pallas_call | solution.py:142
  185.2 8.0 %shard_map.118 = bf16[256,3072]{1,0:T(8,128)(2,1)S(1)} custom-call(bf16[256,1024]{1,0:T(8,128)(2,1)S(1)} %get-tuple-element.5.gate_cot_ref, bf16[256,1024]{1,0:T(8,128)(2,1)S(1)} %get-tuple-element.6.up_cot_ref, bf16[6144,1024]{1,0:T(8,128)(2,1)} %bitcast.61, bf16[6144,1024]{1,0:T(8,128)(2,1)} %bitcast.65), custom_call_target="tpu_custom_call" | custom-call | flops 3221225472 | bytes 12582912 | tf_op jit(solution)/shard_map/pallas_call | solution.py:169
  193.2 8.0 %shard_map.119 = bf16[256,3072]{1,0:T(8,128)(2,1)S(1)} custom-call(bf16[256,1024]{1,0:T(8,128)(2,1)S(1)} %get-tuple-element.5.gate_cot_ref, bf16[256,1024]{1,0:T(8,128)(2,1)S(1)} %get-tuple-element.6.up_cot_ref, bf16[6144,1024]{1,0:T(8,128)(2,1)} %bitcast.62, bf16[6144,1024]{1,0:T(8,128)(2,1)} %bitcast.66), custom_call_target="tpu_custom_call" | custom-call | flops 3221225472 | bytes 12582912 | tf_op jit(solution)/shard_map/pallas_call | solution.py:169
  203.4 11.4 %shard_map.113.active_ref = bf16[256,1024]{1,0:T(8,128)(2,1)S(1)} custom-call(bf16[256,6144]{1,0:T(8,128)(2,1)S(1)} %pad_maximum_fusion.rows_ref, bf16[6144,1024]{1,0:T(8,128)(2,1)} %bitcast.63, bf16[6144,1024]{1,0:T(8,128)(2,1)} %bitcast.67), custom_call_target="tpu_custom_call" | custom-call | flops 6442450944 | bytes 28311552 | tf_op jit(solution)/shard_map/pallas_call | solution.py:191
  214.8 5.7 %shard_map.115 = bf16[256,3072]{1,0:T(8,128)(2,1)S(1)} custom-call(bf16[256,1024]{1,0:T(8,128)(2,1)S(1)} %shard_map.113.active_ref, bf16[1024,6144]{1,0:T(8,128)(2,1)} %bitcast.69), custom_call_target="tpu_custom_call" | custom-call | flops 1610612736 | bytes 6291456 | tf_op jit(solution)/shard_map/pallas_call | solution.py:211
  220.4 5.6 %shard_map.114 = bf16[256,3072]{1,0:T(8,128)(2,1)S(1)} custom-call(bf16[256,1024]{1,0:T(8,128)(2,1)S(1)} %shard_map.113.active_ref, bf16[1024,6144]{1,0:T(8,128)(2,1)} %bitcast.70), custom_call_target="tpu_custom_call" | custom-call | flops 1610612736 | bytes 6291456 | tf_op jit(solution)/shard_map/pallas_call | solution.py:211
  230.9 5.6 %collective-permute-done.26 = bf16[32,3072]{1,0:T(8,128)(2,1)S(1)} collective-permute-done((bf16[32,3072]{1,0:T(8,128)(2,1)S(1)}, bf16[32,3072]{1,0:T(8,128)(2,1)S(1)}, u32[]{:S(2)}, u32[]{:S(2)}) %collective-permute-start.26) | collective-permute-done | bytes 196640 | tf_op jit(solution)/shard_map/ppermute | solution.py:23
  237.1 4.6 %collective-permute-done.15 = bf16[32,3072]{1,0:T(8,128)(2,1)S(1)} collective-permute-done((bf16[32,3072]{1,0:T(8,128)(2,1)S(1)}, bf16[32,3072]{1,0:T(8,128)(2,1)S(1)}, u32[]{:S(2)}, u32[]{:S(2)}) %collective-permute-start.15) | collective-permute-done | bytes 196640 | tf_op jit(solution)/shard_map/ppermute | solution.py:23
  245.0 5.3 %collective-permute-done.62 = bf16[32,3072]{1,0:T(8,128)(2,1)S(1)} collective-permute-done((bf16[32,3072]{1,0:T(8,128)(2,1)S(1)}, bf16[32,3072]{1,0:T(8,128)(2,1)S(1)}, u32[]{:S(2)}, u32[]{:S(2)}) %collective-permute-start.62) | collective-permute-done | bytes 196640 | tf_op jit(solution)/shard_map/ppermute | solution.py:23
  267.0 5.4 %collective-permute-done.17 = bf16[32,3072]{1,0:T(8,128)(2,1)S(1)} collective-permute-done((bf16[32,3072]{1,0:T(8,128)(2,1)S(1)}, bf16[32,3072]{1,0:T(8,128)(2,1)S(1)}, u32[]{:S(2)}, u32[]{:S(2)}) %collective-permute-start.17) | collective-permute-done | bytes 196640 | tf_op jit(solution)/shard_map/ppermute | solution.py:23
  280.2 10.6 %collective-permute-start.31 = (bf16[128,6144]{1,0:T(8,128)(2,1)S(1)}, bf16[128,6144]{1,0:T(8,128)(2,1)S(1)}, u32[]{:S(2)}, u32[]{:S(2)}) collective-permute-start(bf16[128,6144]{1,0:T(8,128)(2,1)S(1)} %bitcast.72), channel_id=1, source_target_pairs={{0,8},{8,16},{16,24},{24,0},{1,9},{9,17},{17,25},{25,1},{2,10},{10... | collective-permute-start | bytes 4718600 | tf_op jit(solution)/shard_map/ppermute | solution.py:28
  293.8 7.3 %collective-permute-done.64 = bf16[32,3072]{1,0:T(8,128)(2,1)S(1)} collective-permute-done((bf16[32,3072]{1,0:T(8,128)(2,1)S(1)}, bf16[32,3072]{1,0:T(8,128)(2,1)S(1)}, u32[]{:S(2)}, u32[]{:S(2)}) %collective-permute-start.64) | collective-permute-done | bytes 196640 | tf_op jit(solution)/shard_map/ppermute | solution.py:23
  314.1 6.9 %collective-permute-done.75 = bf16[32,6144]{1,0:T(8,128)(2,1)S(1)} collective-permute-done((bf16[32,6144]{1,0:T(8,128)(2,1)S(1)}, bf16[32,6144]{1,0:T(8,128)(2,1)S(1)}, u32[]{:S(2)}, u32[]{:S(2)}) %collective-permute-start.75) | collective-permute-done | bytes 393248 | tf_op jit(solution)/shard_map/ppermute | solution.py:28
  (279 shorter events, 144.2 us)
Async XLA Ops:
  6.4 51.5 %collective-permute-start.36 = (bf16[32,3072]{1,0:T(8,128)(2,1)S(1)}, bf16[32,3072]{1,0:T(8,128)(2,1)S(1)}, u32[]{:S(2)}, u32[]{:S(2)}) collective-permute-start(bf16[32,3072]{1,0:T(8,128)(2,1)S(1)} %get-tuple-element.45), channel_id=1, source_target_pairs={{0,2},{2,4},{4,6},{6,7},{7,5},{5,3},{3,1},{1,0},{8,10},{10,12},{12... | collective-permute-start | bytes 589832 | tf_op jit(solution)/shard_map/ppermute | solution.py:23
  7.8 92.9 %collective-permute-start.44 = (bf16[32,3072]{1,0:T(8,128)(2,1)S(1)}, bf16[32,3072]{1,0:T(8,128)(2,1)S(1)}, u32[]{:S(2)}, u32[]{:S(2)}) collective-permute-start(bf16[32,3072]{1,0:T(8,128)(2,1)S(1)} %get-tuple-element.48), channel_id=1, source_target_pairs={{0,2},{2,4},{4,6},{6,7},{7,5},{5,3},{3,1},{1,0},{8,10},{10,12},{12... | collective-permute-start | bytes 589832 | tf_op jit(solution)/shard_map/ppermute | solution.py:23
  16.0 86.1 %collective-permute-start.50 = (bf16[32,3072]{1,0:T(8,128)(2,1)S(1)}, bf16[32,3072]{1,0:T(8,128)(2,1)S(1)}, u32[]{:S(2)}, u32[]{:S(2)}) collective-permute-start(bf16[32,3072]{1,0:T(8,128)(2,1)S(1)} %get-tuple-element.41), channel_id=1, source_target_pairs={{0,2},{2,4},{4,6},{6,7},{7,5},{5,3},{3,1},{1,0},{8,10},{10,12},{12... | collective-permute-start | bytes 589832 | tf_op jit(solution)/shard_map/ppermute | solution.py:23
  19.6 86.5 %collective-permute-start.58 = (bf16[32,3072]{1,0:T(8,128)(2,1)S(1)}, bf16[32,3072]{1,0:T(8,128)(2,1)S(1)}, u32[]{:S(2)}, u32[]{:S(2)}) collective-permute-start(bf16[32,3072]{1,0:T(8,128)(2,1)S(1)} %get-tuple-element.44), channel_id=1, source_target_pairs={{0,2},{2,4},{4,6},{6,7},{7,5},{5,3},{3,1},{1,0},{8,10},{10,12},{12... | collective-permute-start | bytes 589832 | tf_op jit(solution)/shard_map/ppermute | solution.py:23
  60.9 28.8 %collective-permute-start.37 = (bf16[32,3072]{1,0:T(8,128)(2,1)S(1)}, bf16[32,3072]{1,0:T(8,128)(2,1)S(1)}, u32[]{:S(2)}, u32[]{:S(2)}) collective-permute-start(bf16[32,3072]{1,0:T(8,128)(2,1)S(1)} %collective-permute-done.36), channel_id=1, source_target_pairs={{0,2},{2,4},{4,6},{6,7},{7,5},{5,3},{3,1},{1,0},{8,10},{10,12},{12... | collective-permute-start | bytes 589832 | tf_op jit(solution)/shard_map/ppermute | solution.py:23
  107.8 30.4 %collective-permute-start.5 = (bf16[32,3072]{1,0:T(8,128)(2,1)S(1)}, bf16[32,3072]{1,0:T(8,128)(2,1)S(1)}, u32[]{:S(2)}, u32[]{:S(2)}) collective-permute-start(bf16[32,3072]{1,0:T(8,128)(2,1)S(1)} %collective-permute-done.4), channel_id=1, source_target_pairs={{0,2},{2,4},{4,6},{6,7},{7,5},{5,3},{3,1},{1,0},{8,10},{10,12},{12... | collective-permute-start | bytes 589832 | tf_op jit(solution)/shard_map/ppermute | solution.py:23
  109.1 30.4 %collective-permute-start.13 = (bf16[32,3072]{1,0:T(8,128)(2,1)S(1)}, bf16[32,3072]{1,0:T(8,128)(2,1)}, u32[]{:S(2)}, u32[]{:S(2)}) collective-permute-start(bf16[32,3072]{1,0:T(8,128)(2,1)S(1)} %collective-permute-done.12), channel_id=1, source_target_pairs={{0,2},{2,4},{4,6},{6,7},{7,5},{5,3},{3,1},{1,0},{8,10},{10,12},{12... | collective-permute-start | bytes 589832 | tf_op jit(solution)/shard_map/ppermute | solution.py:23
  111.2 29.5 %collective-permute-start.46 = (bf16[32,3072]{1,0:T(8,128)(2,1)S(1)}, bf16[32,3072]{1,0:T(8,128)(2,1)S(1)}, u32[]{:S(2)}, u32[]{:S(2)}) collective-permute-start(bf16[32,3072]{1,0:T(8,128)(2,1)S(1)} %collective-permute-done.45), channel_id=1, source_target_pairs={{0,2},{2,4},{4,6},{6,7},{7,5},{5,3},{3,1},{1,0},{8,10},{10,12},{12... | collective-permute-start | bytes 589832 | tf_op jit(solution)/shard_map/ppermute | solution.py:23
  112.7 28.3 %collective-permute-start.52 = (bf16[32,3072]{1,0:T(8,128)(2,1)S(1)}, bf16[32,3072]{1,0:T(8,128)(2,1)S(1)}, u32[]{:S(2)}, u32[]{:S(2)}) collective-permute-start(bf16[32,3072]{1,0:T(8,128)(2,1)S(1)} %collective-permute-done.51), channel_id=1, source_target_pairs={{0,2},{2,4},{4,6},{6,7},{7,5},{5,3},{3,1},{1,0},{8,10},{10,12},{12... | collective-permute-start | bytes 589832 | tf_op jit(solution)/shard_map/ppermute | solution.py:23
  114.3 199.8 %collective-permute-start.76 = (bf16[128,6144]{1,0:T(8,128)(2,1)S(1)}, bf16[128,6144]{1,0:T(8,128)(2,1)}, u32[]{:S(2)}, u32[]{:S(2)}) collective-permute-start(bf16[128,6144]{1,0:T(8,128)(2,1)S(1)} %bitcast.71), channel_id=1, source_target_pairs={{0,24},{8,0},{16,8},{24,16},{1,25},{9,1},{17,9},{25,17},{2,26},{10... | collective-permute-start | bytes 4718600 | tf_op jit(solution)/shard_map/ppermute | solution.py:28
  138.2 25.6 %collective-permute-start.60 = (bf16[32,3072]{1,0:T(8,128)(2,1)S(1)}, bf16[32,3072]{1,0:T(8,128)(2,1)S(1)}, u32[]{:S(2)}, u32[]{:S(2)}) collective-permute-start(bf16[32,3072]{1,0:T(8,128)(2,1)S(1)} %collective-permute-done.59), channel_id=1, source_target_pairs={{0,2},{2,4},{4,6},{6,7},{7,5},{5,3},{3,1},{1,0},{8,10},{10,12},{12... | collective-permute-start | bytes 589832 | tf_op jit(solution)/shard_map/ppermute | solution.py:23
  139.5 19.3 %collective-permute-start.6 = (bf16[32,3072]{1,0:T(8,128)(2,1)S(1)}, bf16[32,3072]{1,0:T(8,128)(2,1)}, u32[]{:S(2)}, u32[]{:S(2)}) collective-permute-start(bf16[32,3072]{1,0:T(8,128)(2,1)S(1)} %collective-permute-done.5), channel_id=1, source_target_pairs={{0,2},{2,4},{4,6},{6,7},{7,5},{5,3},{3,1},{1,0},{8,10},{10,12},{12... | collective-permute-start | bytes 589832 | tf_op jit(solution)/shard_map/ppermute | solution.py:23
  140.7 60.5 %collective-permute-start.14 = (bf16[32,3072]{1,0:T(8,128)(2,1)}, bf16[32,3072]{1,0:T(8,128)(2,1)}, u32[]{:S(2)}, u32[]{:S(2)}) collective-permute-start(bf16[32,3072]{1,0:T(8,128)(2,1)} %collective-permute-done.13), channel_id=1, source_target_pairs={{0,2},{2,4},{4,6},{6,7},{7,5},{5,3},{3,1},{1,0},{8,10},{10,12},{12... | collective-permute-start | bytes 589832 | tf_op jit(solution)/shard_map/ppermute | solution.py:23
  141.0 17.0 %collective-permute-start.53 = (bf16[32,3072]{1,0:T(8,128)(2,1)S(1)}, bf16[32,3072]{1,0:T(8,128)(2,1)S(1)}, u32[]{:S(2)}, u32[]{:S(2)}) collective-permute-start(bf16[32,3072]{1,0:T(8,128)(2,1)S(1)} %collective-permute-done.52), channel_id=1, source_target_pairs={{0,2},{2,4},{4,6},{6,7},{7,5},{5,3},{3,1},{1,0},{8,10},{10,12},{12... | collective-permute-start | bytes 589832 | tf_op jit(solution)/shard_map/ppermute | solution.py:23
  158.8 34.4 %collective-permute-start.11 = (bf16[32,3072]{1,0:T(8,128)(2,1)S(1)}, bf16[32,3072]{1,0:T(8,128)(2,1)S(1)}, u32[]{:S(2)}, u32[]{:S(2)}) collective-permute-start(bf16[32,3072]{1,0:T(8,128)(2,1)S(1)} %collective-permute-done.10), channel_id=1, source_target_pairs={{0,1},{2,0},{4,2},{6,4},{7,6},{5,7},{3,5},{1,3},{8,9},{10,8},{12,1... | collective-permute-start | bytes 589832 | tf_op jit(solution)/shard_map/ppermute | solution.py:23
  162.5 20.8 %collective-permute-start.7 = (bf16[32,3072]{1,0:T(8,128)(2,1)}, bf16[32,3072]{1,0:T(8,128)(2,1)}, u32[]{:S(2)}, u32[]{:S(2)}) collective-permute-start(bf16[32,3072]{1,0:T(8,128)(2,1)} %collective-permute-done.6), channel_id=1, source_target_pairs={{0,2},{2,4},{4,6},{6,7},{7,5},{5,3},{3,1},{1,0},{8,10},{10,12},{12... | collective-permute-start | bytes 589832 | tf_op jit(solution)/shard_map/ppermute | solution.py:23
  227.4 17.4 %collective-permute-start.65 = (bf16[32,3072]{1,0:T(8,128)(2,1)S(1)}, bf16[32,3072]{1,0:T(8,128)(2,1)S(1)}, u32[]{:S(2)}, u32[]{:S(2)}) collective-permute-start(bf16[32,3072]{1,0:T(8,128)(2,1)S(1)} %get-tuple-element.18), channel_id=1, source_target_pairs={{0,1},{2,0},{4,2},{6,4},{7,6},{5,7},{3,5},{1,3},{8,9},{10,8},{12,1... | collective-permute-start | bytes 589832 | tf_op jit(solution)/shard_map/ppermute | solution.py:23
  227.8 15.3 %collective-permute-start.68 = (bf16[32,3200]{1,0:T(8,128)(2,1)S(1)}, bf16[32,3200]{1,0:T(8,128)(2,1)S(1)}, u32[]{:S(2)}, u32[]{:S(2)}) collective-permute-start(bf16[32,3200]{1,0:T(8,128)(2,1)S(1)} %pad_maximum_fusion.3), channel_id=1, source_target_pairs={{0,2},{2,4},{4,6},{6,7},{7,5},{5,3},{3,1},{1,0},{8,10},{10,12},{12... | collective-permute-start | bytes 614408 | tf_op jit(solution)/shard_map/ppermute | solution.py:23
  253.4 21.8 %collective-permute-start.63 = (bf16[32,3072]{1,0:T(8,128)(2,1)S(1)}, bf16[32,3072]{1,0:T(8,128)(2,1)S(1)}, u32[]{:S(2)}, u32[]{:S(2)}) collective-permute-start(bf16[32,3072]{1,0:T(8,128)(2,1)S(1)} %get-tuple-element.15), channel_id=1, source_target_pairs={{0,2},{2,4},{4,6},{6,7},{7,5},{5,3},{3,1},{1,0},{8,10},{10,12},{12... | collective-permute-start | bytes 589832 | tf_op jit(solution)/shard_map/ppermute | solution.py:23
  255.9 19.3 %collective-permute-start.66 = (bf16[32,3072]{1,0:T(8,128)(2,1)S(1)}, bf16[32,3072]{1,0:T(8,128)(2,1)S(1)}, u32[]{:S(2)}, u32[]{:S(2)}) collective-permute-start(bf16[32,3072]{1,0:T(8,128)(2,1)S(1)} %get-tuple-element.16), channel_id=1, source_target_pairs={{0,1},{2,0},{4,2},{6,4},{7,6},{5,7},{3,5},{1,3},{8,9},{10,8},{12,1... | collective-permute-start | bytes 589832 | tf_op jit(solution)/shard_map/ppermute | solution.py:23
  275.1 15.7 %collective-permute-start.29 = (bf16[32,3072]{1,0:T(8,128)(2,1)S(1)}, bf16[32,3072]{1,0:T(8,128)(2,1)S(1)}, u32[]{:S(2)}, u32[]{:S(2)}) collective-permute-start(bf16[32,3072]{1,0:T(8,128)(2,1)S(1)} %get-tuple-element.34), channel_id=1, source_target_pairs={{0,1},{2,0},{4,2},{6,4},{7,6},{5,7},{3,5},{1,3},{8,9},{10,8},{12,1... | collective-permute-start | bytes 589832 | tf_op jit(solution)/shard_map/ppermute | solution.py:23
  275.2 16.9 %collective-permute-start.18 = (bf16[32,3072]{1,0:T(8,128)(2,1)S(1)}, bf16[32,3072]{1,0:T(8,128)(2,1)S(1)}, u32[]{:S(2)}, u32[]{:S(2)}) collective-permute-start(bf16[32,3072]{1,0:T(8,128)(2,1)S(1)} %get-tuple-element.27), channel_id=1, source_target_pairs={{0,2},{2,4},{4,6},{6,7},{7,5},{5,3},{3,1},{1,0},{8,10},{10,12},{12... | collective-permute-start | bytes 589832 | tf_op jit(solution)/shard_map/ppermute | solution.py:23
  278.1 14.9 %collective-permute-start.21 = (bf16[32,3072]{1,0:T(8,128)(2,1)S(1)}, bf16[32,3072]{1,0:T(8,128)(2,1)S(1)}, u32[]{:S(2)}, u32[]{:S(2)}) collective-permute-start(bf16[32,3072]{1,0:T(8,128)(2,1)S(1)} %get-tuple-element.28), channel_id=1, source_target_pairs={{0,1},{2,0},{4,2},{6,4},{7,6},{5,7},{3,5},{1,3},{8,9},{10,8},{12,1... | collective-permute-start | bytes 589832 | tf_op jit(solution)/shard_map/ppermute | solution.py:23
  280.2 32.1 %collective-permute-start.31 = (bf16[128,6144]{1,0:T(8,128)(2,1)S(1)}, bf16[128,6144]{1,0:T(8,128)(2,1)S(1)}, u32[]{:S(2)}, u32[]{:S(2)}) collective-permute-start(bf16[128,6144]{1,0:T(8,128)(2,1)S(1)} %bitcast.72), channel_id=1, source_target_pairs={{0,8},{8,16},{16,24},{24,0},{1,9},{9,17},{17,25},{25,1},{2,10},{10... | collective-permute-start | bytes 4718600 | tf_op jit(solution)/shard_map/ppermute | solution.py:28
  (69 other events, 520.9 us)

commit v2 on v1

v2 whole, which is shorter than its diff:
```python
import functools

import jax
import jax.numpy as jnp
from jax import lax
from jax.experimental import pallas as pl
from jax.experimental.pallas import tpu as pltpu
from jax.sharding import PartitionSpec as P

epsilon = 1e-05
highest = lax.Precision.HIGHEST
f32 = jnp.float32
bf16 = jnp.bfloat16
last_dims = (((1,), (1,)), ((), ()))


def ring_of(count):
    return list(range(0, count, 2)) + list(range(1, count, 2))[::-1]


def hop(value, steps):
    ring = ring_of(lax.axis_size("expert"))
    count = len(ring)
    return lax.ppermute(value, "expert", [(ring[i], ring[(i + steps) % count]) for i in range(count)])


def shifted(value, steps):
    count = lax.axis_size("section")
    return lax.ppermute(value, "section", [(source, (source + steps) % count) for source in range(count)])


def halves(value):
    middle = value.shape[1] // 2
    return [value[:, :middle], value[:, middle:]]


class Ring:

    def __init__(self):
        self.count = lax.axis_size("expert")
        self.full = (self.count - 1) // 2
        self.split = self.count % 2 == 0
        self.steps = self.full + self.split
        self.inbox = {}


class Gather(Ring):

    def begin(self, shard):
        self.held = [shard] + [None] * (self.count - 1)

    def send(self, step):
        ahead = self.held[-step % self.count]
        behind = self.held[step]
        if step == self.full:
            ahead, behind = halves(ahead)[0], halves(behind)[1]
        return [hop(ahead, 1), hop(behind, -1)]

    def receive(self, step, values):
        if step == self.full:
            self.held[step + 1] = jnp.concatenate(values, axis=1)
        else:
            self.held[-1 - step], self.held[step + 1] = values


class Scatter(Ring):

    def begin(self, part):
        self.parts = split_rows(part, self.count)

    def send(self, step):
        far = self.steps - step
        ahead, behind = self.parts[far], self.parts[-far]
        if self.split and step == 0:
            ahead, behind = halves(ahead)[0], halves(behind)[1]
        elif step > 0:
            ahead, behind = self.merged(ahead, 0, step), self.merged(behind, 1, step)
        return [hop(ahead, 1), hop(behind, -1)]

    def merged(self, own, way, step):
        value = self.inbox[way]
        if self.split and step == 1:
            pieces = halves(own)
            pieces[way] = (pieces[way].astype(f32) + value.astype(f32)).astype(bf16)
            return jnp.concatenate(pieces, axis=1)
        return (own.astype(f32) + value.astype(f32)).astype(bf16)

    def receive(self, step, values):
        self.inbox = dict(enumerate(values))

    def total(self):
        return sum(value.astype(f32) for value in (self.parts[0], *self.inbox.values()))


def fence(arrays):
    return pl.pallas_call(
        lambda *refs: None,
        in_specs=[pl.BlockSpec(memory_space=pl.ANY)] * len(arrays),
        out_specs=[pl.BlockSpec(memory_space=pl.ANY)] * len(arrays),
        out_shape=[jax.ShapeDtypeStruct(array.shape, array.dtype) for array in arrays],
        compiler_params=params(1),
        input_output_aliases={k: k for k in range(len(arrays))},
    )(*arrays)


class Shift:

    def __init__(self, array, steps, pieces):
        self.rows = split_rows(array, pieces)
        self.by = steps
        self.got = []

    def send(self, step):
        return [shifted(self.rows[step], self.by)]

    def receive(self, step, values):
        self.got += values

    def result(self):
        return jnp.concatenate(self.got, axis=0)


def run_windows(windows, pieces, env):
    flying, made = [], []
    for k, transfers in enumerate(windows):
        todo = pieces.get(k, [])
        names = list(made)
        for needs, _, _ in todo:
            names += [name for name in needs if name not in names]
        sources = [ring for ring, step in transfers if isinstance(ring, Gather) and step == 0]
        landed = [value for _, _, values in flying for value in values]
        passed = list(fence(landed + [env[name] for name in names] + [ring.held[0] for ring in sources]))
        for ring, step, values in flying:
            ring.receive(step, passed[: len(values)])
            passed = passed[len(values) :]
        for name in names:
            env[name] = passed.pop(0)
        for ring in sources:
            ring.held[0] = passed.pop(0)
        for ring, step in transfers:
            if isinstance(ring, Scatter) and step == 0:
                ring.begin(env[ring.source])
        with jax.named_scope(f"window_{k}"):
            flying = [(ring, step, ring.send(step)) for ring, step in transfers]
        made = []
        for needs, does, gives in todo:
            for name, value in zip(gives, does(*[env[name] for name in needs]), strict=True):
                env[name] = value
                made.append(name)
    for ring, step, values in flying:
        ring.receive(step, values)


def cost(flops, moved):
    return pl.CostEstimate(flops=int(flops), bytes_accessed=int(moved), transcendentals=0)


def params(mega):
    return pltpu.CompilerParams(vmem_limit_bytes=mega * 1024 * 1024)


def dot_t(left, right):
    return lax.dot_general(left, right, last_dims, preferred_element_type=f32)


def dot_n(left, right):
    return jnp.dot(left, right, preferred_element_type=f32)


in_hbm = pl.BlockSpec(memory_space=pltpu.HBM)
anywhere = pl.BlockSpec(memory_space=pl.ANY)
in_vmem = pl.BlockSpec(memory_space=pltpu.VMEM)


def pieces_of(length, most, grain):
    for number in range(most, 1, -1):
        if length % (number * grain) == 0:
            size = length // number
            return [slice(k * size, (k + 1) * size) for k in range(number)]
    return [slice(0, length)]


def row_copies(shards, rows_ref, sems):
    side = rows_ref.shape[0] // len(shards)
    return [
        pltpu.make_async_copy(shard, rows_ref.at[k * side : (k + 1) * side], sems.at[k])
        for k, shard in enumerate(shards)
    ]


def loads(source, target, parts, sems, columns=False):
    out = []
    for k, part in enumerate(parts):
        where = (slice(None), part) if columns else (part, slice(None))
        out.append(pltpu.make_async_copy(source.at[where], target.at[where], sems.at[k]))
    return out


def start_all(*lists):
    for group in zip(*lists, strict=True):
        for copy in group:
            copy.start()


def back_kernel(count, *refs):
    shards, (down_ref, out_ref, rows_ref, weight_ref, row_sems, sems) = refs[:count], refs[count:]
    parts = pieces_of(down_ref.shape[0], 4, 128)
    rows = row_copies(shards, rows_ref, row_sems)
    downs = loads(down_ref, weight_ref, parts, sems)
    start_all(rows)
    start_all(downs)
    for copy in rows:
        copy.wait()
    for part, copy in zip(parts, downs, strict=True):
        copy.wait()
        out_ref[:, part] = dot_t(rows_ref[...], weight_ref[part, :])


def back_call(shards, down):
    count, (side, width), hid = len(shards), shards[0].shape, down.shape[0]
    return pl.pallas_call(
        functools.partial(back_kernel, count),
        in_specs=[anywhere] * count + [in_hbm],
        out_specs=in_vmem,
        out_shape=jax.ShapeDtypeStruct((count * side, hid), f32),
        scratch_shapes=[
            pltpu.VMEM((count * side, width), bf16),
            pltpu.VMEM((hid, width), bf16),
            pltpu.SemaphoreType.DMA((count,)),
            pltpu.SemaphoreType.DMA((4,)),
        ],
        compiler_params=params(22),
        cost_estimate=cost(2 * count * side * width * hid, 2 * width * (hid + count * side)),
    )(*shards, down)


def gate_up(shards, gate_ref, up_ref, rows_ref, gate_w, up_w, gate_sum, up_sum, row_sems, gate_sems, up_sems):
    parts = pieces_of(gate_ref.shape[0], 6, 128)
    rows = row_copies(shards, rows_ref, row_sems)
    gates = loads(gate_ref, gate_w, parts, gate_sems)
    ups = loads(up_ref, up_w, parts, up_sems)
    start_all(rows)
    start_all(gates, ups)
    for copy in rows:
        copy.wait()
    for k, part in enumerate(parts):
        for copy, weight, total in ((gates[k], gate_w, gate_sum), (ups[k], up_w, up_sum)):
            copy.wait()
            product = dot_n(rows_ref[:, part], weight[part, :])
            total[...] = product if k == 0 else total[...] + product


def gate_up_scratch(count, side, width, hid):
    return [
        pltpu.VMEM((count * side, width), bf16),
        pltpu.VMEM((width, hid), bf16),
        pltpu.VMEM((width, hid), bf16),
        pltpu.VMEM((count * side, hid), f32),
        pltpu.VMEM((count * side, hid), f32),
        pltpu.SemaphoreType.DMA((count,)),
        pltpu.SemaphoreType.DMA((6,)),
        pltpu.SemaphoreType.DMA((6,)),
    ]


def cots_kernel(count, *refs):
    shards, (gate_ref, up_ref, back_ref, gate_cot_ref, up_cot_ref, slope_ref, *scratch) = refs[:count], refs[count:]
    gate_up(shards, gate_ref, up_ref, *scratch)
    gate_pre, up_pre = scratch[3][...], scratch[4][...]
    sig = jax.nn.sigmoid(gate_pre)
    silu = gate_pre * sig
    back = back_ref[...]
    active = (silu * up_pre).astype(bf16).astype(f32)
    slope_ref[...] = jnp.broadcast_to(
        jnp.sum(active * back, axis=1, keepdims=True), slope_ref.shape
    ).astype(slope_ref.dtype)
    gate_cot_ref[...] = (back * up_pre * sig * (1.0 + gate_pre * (1.0 - sig))).astype(bf16)
    up_cot_ref[...] = (back * silu).astype(bf16)


def cots_call(shards, gate, up, back):
    count, (side, width), hid = len(shards), shards[0].shape, gate.shape[1]
    return pl.pallas_call(
        functools.partial(cots_kernel, count),
        in_specs=[anywhere] * count + [in_hbm, in_hbm, in_vmem],
        out_specs=[in_vmem] * 3,
        out_shape=[
            jax.ShapeDtypeStruct((count * side, hid), bf16),
            jax.ShapeDtypeStruct((count * side, hid), bf16),
            jax.ShapeDtypeStruct((count * side, 128), bf16),
        ],
        scratch_shapes=gate_up_scratch(count, side, width, hid),
        compiler_params=params(44),
        cost_estimate=cost(4 * count * side * width * hid, 2 * width * (2 * hid + count * side)),
    )(*shards, gate, up, back)


def active_kernel(count, *refs):
    shards, (gate_ref, up_ref, out_ref, *scratch) = refs[:count], refs[count:]
    gate_up(shards, gate_ref, up_ref, *scratch)
    gate_pre = scratch[3][...]
    out_ref[...] = (gate_pre * jax.nn.sigmoid(gate_pre) * scratch[4][...]).astype(bf16)


def active_call(shards, gate, up):
    count, (side, width), hid = len(shards), shards[0].shape, gate.shape[1]
    return pl.pallas_call(
        functools.partial(active_kernel, count),
        in_specs=[anywhere] * count + [in_hbm, in_hbm],
        out_specs=in_vmem,
        out_shape=jax.ShapeDtypeStruct((count * side, hid), bf16),
        scratch_shapes=gate_up_scratch(count, side, width, hid),
        compiler_params=params(40),
        cost_estimate=cost(4 * count * side * width * hid, 2 * width * (2 * hid + count * side)),
    )(*shards, gate, up)


def rowpart_kernel(gate_cot_ref, up_cot_ref, slope_ref, gate_ref, up_ref, out_ref, gate_w, up_w, made, gate_sems, up_sems, out_sems):
    width = gate_ref.shape[0]
    parts = pieces_of(width, 6, 128)
    gates = loads(gate_ref, gate_w, parts, gate_sems)
    ups = loads(up_ref, up_w, parts, up_sems)
    start_all(gates, ups)
    made[:, width:] = slope_ref[...]
    outs = loads(made, out_ref, parts + [slice(width, made.shape[1])], out_sems, columns=True)
    outs[-1].start()
    for k, part in enumerate(parts):
        gates[k].wait()
        ups[k].wait()
        made[:, part] = (
            dot_t(gate_cot_ref[...], gate_w[part, :]) + dot_t(up_cot_ref[...], up_w[part, :])
        ).astype(bf16)
        outs[k].start()
    for copy in outs:
        copy.wait()


def rowpart_call(gate_cot, up_cot, slope, gate, up):
    count, hid = gate_cot.shape
    width, extra = gate.shape[0], slope.shape[1]
    return pl.pallas_call(
        rowpart_kernel,
        in_specs=[in_vmem] * 3 + [in_hbm] * 2,
        out_specs=anywhere,
        out_shape=jax.ShapeDtypeStruct((count, width + extra), bf16),
        scratch_shapes=[
            pltpu.VMEM((width, hid), bf16),
            pltpu.VMEM((width, hid), bf16),
            pltpu.VMEM((count, width + extra), bf16),
            pltpu.SemaphoreType.DMA((6,)),
            pltpu.SemaphoreType.DMA((6,)),
            pltpu.SemaphoreType.DMA((7,)),
        ],
        compiler_params=params(40),
        cost_estimate=cost(4 * count * width * hid, 4 * width * hid),
    )(gate_cot, up_cot, slope, gate, up)


def outpart_kernel(active_ref, down_ref, out_ref, down_w, made, sems, out_sems):
    parts = pieces_of(down_ref.shape[1], 6, 128)
    downs = loads(down_ref, down_w, parts, sems, columns=True)
    outs = loads(made, out_ref, parts, out_sems, columns=True)
    start_all(downs)
    for k, part in enumerate(parts):
        downs[k].wait()
        made[:, part] = dot_n(active_ref[...], down_w[:, part]).astype(bf16)
        outs[k].start()
    for copy in outs:
        copy.wait()


def outpart_call(active, down):
    count, hid = active.shape
    width = down.shape[1]
    return pl.pallas_call(
        outpart_kernel,
        in_specs=[in_vmem, in_hbm],
        out_specs=anywhere,
        out_shape=jax.ShapeDtypeStruct((count, width), bf16),
        scratch_shapes=[
            pltpu.VMEM((hid, width), bf16),
            pltpu.VMEM((count, width), bf16),
            pltpu.SemaphoreType.DMA((6,)),
            pltpu.SemaphoreType.DMA((6,)),
        ],
        compiler_params=params(22),
        cost_estimate=cost(2 * count * width * hid, 2 * width * hid),
    )(active, down)


def select_matrix(ids, capacity):
    tokens = ids.shape[0]
    named = jnp.sum((ids == 0).astype(bf16), axis=1)
    earlier = jnp.tril(jnp.ones((tokens, tokens), bf16), -1)
    rank = jnp.dot(earlier, named, preferred_element_type=f32)
    slot = jnp.where(named > 0, rank, float(capacity))
    return (slot[None, :] == jnp.arange(capacity, dtype=f32)[:, None]).astype(bf16)


def pick_ids(select, ids):
    return jnp.dot(select, ids.astype(bf16), preferred_element_type=f32).astype(jnp.int32)


def norm_route(inputs, gain_row, router_mat, chosen_ids):
    inverse = lax.rsqrt(jnp.mean(inputs * inputs, axis=1, keepdims=True) + epsilon)
    normed = inputs * inverse * gain_row[None, :]
    logits = jnp.dot(normed, router_mat, precision=highest)
    onehot = (
        chosen_ids[:, :, None] == jnp.arange(router_mat.shape[1], dtype=jnp.int32)[None, None, :]
    ).astype(f32)
    picked = jnp.sum(onehot * logits[:, None, :], axis=2)
    first_share = jax.nn.sigmoid(picked[:, 0] - picked[:, 1])
    shares = jnp.stack([first_share, 1.0 - first_share], axis=1)
    return (normed, jnp.sum(shares * (chosen_ids == 0).astype(f32), axis=1))


def split_rows(array, count):
    rows = array.shape[0] // count
    return [array[k * rows : (k + 1) * rows] for k in range(count)]


def place(select, rows, base):
    spread = lax.dot_general(select, rows, (((0,), (0,)), ((), ())), preferred_element_type=f32).astype(bf16)
    used = jnp.sum(select.astype(f32), axis=0) > 0
    return jnp.where(used[:, None], spread, base)


def local(
    act_in, saved_in, grad_in, fwd_routes, bwd_routes, w_gate, w_up, w_down, router, norm_gain
):
    count = lax.axis_size("expert")
    capacity = act_in.shape[1] // 4
    gate, up, down = w_gate[0], w_up[0], w_down[0]
    gain_row, router_mat = norm_gain[0], router[0]
    fwd_ids, bwd_ids = fwd_routes[0], bwd_routes[0]
    gather_u, gather_h, gather_f = Gather(), Gather(), Gather()
    scatter_r, scatter_o = Scatter(), Scatter()
    scatter_r.source, scatter_o.source = "row_part", "out_part"
    shift_act, shift_grad = Shift(act_in[0], 1, 4), Shift(grad_in[0], -1, 4)
    env = {}

    select_b = select_matrix(bwd_ids, capacity)
    env["select_b"], env["select_f"] = select_b, select_matrix(fwd_ids, capacity)
    rows_u = jnp.dot(select_b, grad_in[0], preferred_element_type=f32)
    gather_u.begin(rows_u.astype(bf16))

    def shifts(select_f, select_b):
        return (shifted(select_f, 1), shifted(select_b, -1))

    def front_b(select_b):
        rows_b = jnp.dot(select_b, saved_in[0], preferred_element_type=f32)
        ids_b = pick_ids(select_b, bwd_ids)
        (normed_b, weight_b), pullback = jax.vjp(
            lambda inputs: norm_route(inputs, gain_row, router_mat, ids_b), rows_b
        )
        env["pullback"] = pullback
        gather_h.begin(normed_b.astype(bf16))
        return (weight_b,)

    def front_f(select_f):
        rows_f = jnp.dot(select_f, act_in[0], preferred_element_type=f32)
        normed_f, weight_f = norm_route(rows_f, gain_row, router_mat, pick_ids(select_f, fwd_ids))
        gather_f.begin(normed_f.astype(bf16))
        return (rows_f, weight_f)

    def back():
        return (back_call(gather_u.held, down),)

    def active():
        return (active_call(gather_f.held, gate, up),)

    def outpart(active):
        return (outpart_call(active, down),)

    def cots(back):
        return cots_call(gather_h.held, gate, up, back)

    def rowpart(gate_cot, up_cot, slope):
        return (rowpart_call(gate_cot, up_cot, slope, gate, up),)

    windows = []
    for ring, merges in ((gather_u, False), (gather_f, True), (gather_h, True), (scatter_o, True), (scatter_r, True)):
        for step in range(ring.steps):
            if merges and step == 0:
                windows[-1].append((ring, step))
            else:
                windows.append([(ring, step)])
    start = {(ring, step): k for k, transfers in enumerate(windows) for ring, step in transfers}
    last = gather_u.steps - 1
    for k in range(4):
        windows[k] += [(shift_act, k), (shift_grad, k)]
    pieces = {}

    def put(window, needs, does, gives):
        pieces.setdefault(window, []).append((needs, does, gives))

    put(0, ("select_f",), front_f, ("rows_f", "weight_f"))
    put(1, ("select_b",), front_b, ("weight_b",))
    put(2, ("select_f", "select_b"), shifts, ("select_f_there", "select_b_there"))
    put(start[gather_u, last] + 1, (), back, ("back",))
    put(start[gather_f, last] + 1, (), active, ("active",))
    put(start[gather_h, last] - 1, ("active",), outpart, ("out_part",))
    put(start[gather_h, last] + 1, ("back",), cots, ("gate_cot", "up_cot", "slope"))
    put(start[scatter_o, last] - 1, ("gate_cot", "up_cot", "slope"), rowpart, ("row_part",))

    def act_rows(weight_f):
        return (shifted((env["rows_f"] + weight_f[:, None] * scatter_o.total()).astype(bf16), 1),)

    def act_place(select, rows):
        return (place(select, rows, shift_act.result()),)

    put(start[scatter_r, 0] + 1, ("weight_f",), act_rows, ("act_rows",))
    put(start[scatter_r, last], ("select_f_there", "act_rows"), act_place, ("act_out",))
    run_windows(windows, pieces, env)

    sums = scatter_r.total()
    width = gate.shape[0]
    scale = env["weight_b"].astype(bf16).astype(f32)[:, None]
    d_rows = env["pullback"]((sums[:, :width] * scale, sums[:, width]))[0]
    grad_rows = shifted((rows_u + d_rows).astype(bf16), -1)
    grad_out = place(env["select_b_there"], grad_rows, shift_grad.result())
    return (env["act_out"][None], grad_out[None])


def solution(mesh):
    in_specs = (
        P("section", "expert", None),
        P("section", "expert", None),
        P("section", "expert", None),
        P("section", "expert", None),
        P("section", "expert", None),
        P("section", None, "expert"),
        P("section", None, "expert"),
        P("section", "expert", None),
        P("section", None, None),
        P("section", None),
    )
    out_specs = (P("section", "expert", None), P("section", "expert", None))
    return jax.shard_map(local, mesh=mesh, in_specs=in_specs, out_specs=out_specs, check_vma=False)
```

time: 328 us -> 221 us (0.67); the launches traced: 324 us -> 221 us
  starting transfers between devices: 115 us -> 64.2 us
  waiting for transfers between devices: 130 us -> 89.5 us
  Pallas kernels: 57.7 us -> 49.7 us
  local copies, waits for them, and re-layouts: 5.2 us -> 1.64 us
    ppermute x70 -> x40, waiting for transfers between devices: 122 us -> 73 us  [hop(): lax.ppermute(value, 'expert', [(ring[i], ring[(i + steps) % count]) for i...]
    ppermute x70 -> x40, starting transfers between devices: 71.5 us -> 32.3 us  [hop(): lax.ppermute(value, 'expert', [(ring[i], ring[(i + steps) % count]) for i...]
    ppermute x7 -> x12, starting transfers between devices: 43.8 us -> 31.9 us  [shifted(): lax.ppermute(value, 'section', [(source, (source + steps) % count) for so...]
    pallas_call x7 -> x21, Pallas kernels: 57.7 us -> 49.7 us  [the longest x1 11.2 us: cots_call(): pl.pallas_call(functools.partial(cots_kernel, count), in_specs=[anywhere]...]
    ppermute x7 -> x12, waiting for transfers between devices: 8.45 us -> 16.5 us  [shifted(): lax.ppermute(value, 'section', [(source, (source + steps) % count) for so...]
    unnamed x68 -> x53, local copies, waits for them, and re-layouts: 4.58 us -> 0.95 us
  transfers between devices with their start and end apart: 77 -> 52, of which waited for: 39 -> 22; matrix products, arithmetic and copies ran while one was open for 4% -> 3% of each run, Pallas kernels for 18% -> 23%
where the time goes in v2:
time: 221 us
  waiting for transfers between devices  89.5 us (40%)
  starting transfers between devices  64.2 us (29%)
  Pallas kernels  49.7 us (22%)
  matrix products  10.4 us (5%)
  other arithmetic  4 us (2%)
    ppermute x40, waiting for transfers between devices, hop(): lax.ppermute(value, 'expert', [(ring[i], ring[(i + steps) % count]) for i...  73 us
    ppermute x40, starting transfers between devices, hop(): lax.ppermute(value, 'expert', [(ring[i], ring[(i + steps) % count]) for i...  32.3 us
    ppermute x12, starting transfers between devices, shifted(): lax.ppermute(value, 'section', [(source, (source + steps) % count) for so...  31.9 us
    ppermute x12, waiting for transfers between devices, shifted(): lax.ppermute(value, 'section', [(source, (source + steps) % count) for so...  16.5 us
    pallas_call x1, Pallas kernels, cots_call(): pl.pallas_call(functools.partial(cots_kernel, count), in_specs=[anywhere]...  11.2 us
    pallas_call x1, Pallas kernels, active_call(): pl.pallas_call(functools.partial(active_kernel, count), in_specs=[anywher...  10.7 us
    pallas_call x1, Pallas kernels, rowpart_call(): pl.pallas_call(rowpart_kernel, in_specs=[in_vmem] * 3 + [in_hbm] * 2, out...  10.3 us
    pallas_call x1, Pallas kernels, back_call(): pl.pallas_call(functools.partial(back_kernel, count), in_specs=[anywhere]...  9.66 us
  transfers between devices with their start and end apart: 52, of which 22 were waited for; matrix products, arithmetic and copies ran while one was open for 3% of the time, Pallas kernels for 23%

profile of v2, /device:TPU:1, one launch (start us, length us, event | category | flops | bytes accessed | tf_op | source)
XLA Modules:
  0.0 220.8 jit_solution(14562530006916952024)
XLA Ops:
  2.7 2.7 %fusion.60 = (bf16[32,6144]{1,0:T(8,128)(2,1)S(1)}, f32[32,6144]{1,0:T(8,128)}) fusion(bf16[1,128,6144]{2,1,0:T(8,128)(2,1)} %param.12, f32[128]{0:T(128)S(1)} %fusion.10), kind=kOutput, calls=%fused_computation.128 | convolution fusion | flops 50532352 | bytes 2753024 | tf_op jit(solution)/shard_map/dot_general | solution.py:444
  7.8 2.5 %collective-permute-start.2 = (bf16[32,6144]{1,0:T(8,128)(2,1)S(1)}, bf16[32,6144]{1,0:T(8,128)(2,1)S(1)}, u32[]{:S(2)}, u32[]{:S(2)}) collective-permute-start(bf16[32,6144]{1,0:T(8,128)(2,1)S(1)} %get-tuple-element.180), channel_id=1, source_target_pairs={{0,8},{8,16},{16,24},{24,0},{1,9},{9,17},{17,25},{25,1},{2,10},{10... | collective-permute-start | bytes 1179656 | tf_op jit(solution)/shard_map/window_0/ppermute | solution.py:29
  13.8 2.5 %collective-permute-done.refs_0_ = bf16[32,6144]{1,0:T(8,128)(2,1)S(1)} collective-permute-done((bf16[32,6144]{1,0:T(8,128)(2,1)S(1)}, bf16[32,6144]{1,0:T(8,128)(2,1)S(1)}, u32[]{:S(2)}, u32[]{:S(2)}) %collective-permute-start) | collective-permute-done | bytes 393248 | tf_op jit(solution)/shard_map/window_0/ppermute | solution.py:24
  17.6 2.6 %collective-permute-start.10 = (bf16[32,6144]{1,0:T(8,128)(2,1)S(1)}, bf16[32,6144]{1,0:T(8,128)(2,1)S(1)}, u32[]{:S(2)}, u32[]{:S(2)}) collective-permute-start(bf16[32,6144]{1,0:T(8,128)(2,1)S(1)} %get-tuple-element.181), channel_id=1, source_target_pairs={{0,8},{8,16},{16,24},{24,0},{1,9},{9,17},{17,25},{25,1},{2,10},{10... | collective-permute-start | bytes 1179656 | tf_op jit(solution)/shard_map/window_2/ppermute | solution.py:29
  28.0 2.8 %collective-permute-done.7.refs_3_ = bf16[32,6144]{1,0:T(8,128)(2,1)S(1)} collective-permute-done((bf16[32,6144]{1,0:T(8,128)(2,1)S(1)}, bf16[32,6144]{1,0:T(8,128)(2,1)S(1)}, u32[]{:S(2)}, u32[]{:S(2)}) %collective-permute-start.7) | collective-permute-done | bytes 393248 | tf_op jit(solution)/shard_map/window_1/ppermute | solution.py:29
  33.1 5.0 %collective-permute-done.5.refs_1_ = bf16[32,6144]{1,0:T(8,128)(2,1)S(1)} collective-permute-done((bf16[32,6144]{1,0:T(8,128)(2,1)S(1)}, bf16[32,6144]{1,0:T(8,128)(2,1)S(1)}, u32[]{:S(2)}, u32[]{:S(2)}) %collective-permute-start.5) | collective-permute-done | bytes 393248 | tf_op jit(solution)/shard_map/window_1/ppermute | solution.py:24
  43.6 5.0 %collective-permute-done.8.refs_0_ = bf16[32,6144]{1,0:T(8,128)(2,1)S(1)} collective-permute-done((bf16[32,6144]{1,0:T(8,128)(2,1)S(1)}, bf16[32,6144]{1,0:T(8,128)(2,1)S(1)}, u32[]{:S(2)}, u32[]{:S(2)}) %collective-permute-start.8) | collective-permute-done | bytes 393248 | tf_op jit(solution)/shard_map/window_2/ppermute | solution.py:24
  52.4 10.5 %collective-permute-done.14.refs_0_ = bf16[32,3072]{1,0:T(8,128)(2,1)S(1)} collective-permute-done((bf16[32,3072]{1,0:T(8,128)(2,1)S(1)}, bf16[32,3072]{1,0:T(8,128)(2,1)S(1)}, u32[]{:S(2)}, u32[]{:S(2)}) %collective-permute-start.14) | collective-permute-done | bytes 196640 | tf_op jit(solution)/shard_map/window_3/ppermute | solution.py:24
  64.6 9.7 %shard_map.118.refs_2_ = f32[256,1024]{1,0:T(8,128)S(1)} custom-call(bf16[32,6144]{1,0:T(8,128)(2,1)S(1)} %get-tuple-element.75.refs_0_, bf16[32,6144]{1,0:T(8,128)(2,1)S(1)} %get-tuple-element.78.refs_1_, bf16[32,6144]{1,0:T(8,128)(2,1)S(1)} %get-tuple-element.81.refs_2_, bf16[32,6144]{1,0:T(8,128)(2,1)S(1)} %get-tuple-element.85.refs_3_, ...), custom_call_target="tpu_custom_call" | custom-call | flops 3221225472 | bytes 15728640 | tf_op jit(solution)/shard_map/pallas_call | solution.py:221
  75.8 6.3 %collective-permute-done.22.refs_0_ = bf16[32,6144]{1,0:T(8,128)(2,1)S(1)} collective-permute-done((bf16[32,6144]{1,0:T(8,128)(2,1)S(1)}, bf16[32,6144]{1,0:T(8,128)(2,1)S(1)}, u32[]{:S(2)}, u32[]{:S(2)}) %collective-permute-start.22) | collective-permute-done | bytes 393248 | tf_op jit(solution)/shard_map/window_5/ppermute | solution.py:24
  85.2 7.8 %collective-permute-done.24.refs_0_ = bf16[32,3072]{1,0:T(8,128)(2,1)S(1)} collective-permute-done((bf16[32,3072]{1,0:T(8,128)(2,1)S(1)}, bf16[32,3072]{1,0:T(8,128)(2,1)S(1)}, u32[]{:S(2)}, u32[]{:S(2)}) %collective-permute-start.24) | collective-permute-done | bytes 196640 | tf_op jit(solution)/shard_map/window_6/ppermute | solution.py:24
  95.2 10.7 %shard_map.122.refs_2_ = bf16[256,1024]{1,0:T(8,128)(2,1)S(1)} custom-call(bf16[32,6144]{1,0:T(8,128)(2,1)S(1)} %get-tuple-element.86.refs_0_, bf16[32,6144]{1,0:T(8,128)(2,1)S(1)} %get-tuple-element.88.refs_1_, bf16[32,6144]{1,0:T(8,128)(2,1)S(1)} %get-tuple-element.92.refs_2_, bf16[32,6144]{1,0:T(8,128)(2,1)S(1)} %get-tuple-element.94.refs_3_, ...), custom_call_target="tpu_custom_call" | custom-call | flops 6442450944 | bytes 28311552 | tf_op jit(solution)/shard_map/pallas_call | solution.py:307
  107.5 7.8 %shard_map.124.refs_2_ = bf16[256,6144]{1,0:T(8,128)(2,1)S(1)} custom-call(bf16[256,1024]{1,0:T(8,128)(2,1)S(1)} %get-tuple-element.102.active_ref, bf16[1024,6144]{1,0:T(8,128)(2,1)S(1)} %bitcast.82), custom_call_target="tpu_custom_call" | custom-call | flops 3221225472 | bytes 12582912 | tf_op jit(solution)/shard_map/pallas_call | solution.py:375
  118.5 3.6 %collective-permute-done.34.refs_2_ = bf16[32,3072]{1,0:T(8,128)(2,1)S(1)} collective-permute-done((bf16[32,3072]{1,0:T(8,128)(2,1)S(1)}, bf16[32,3072]{1,0:T(8,128)(2,1)S(1)}, u32[]{:S(2)}, u32[]{:S(2)}) %collective-permute-start.34) | collective-permute-done | bytes 196640 | tf_op jit(solution)/shard_map/window_9/ppermute | solution.py:24
  123.1 3.2 %collective-permute-done.32.refs_0_ = bf16[32,3072]{1,0:T(8,128)(2,1)S(1)} collective-permute-done((bf16[32,3072]{1,0:T(8,128)(2,1)S(1)}, bf16[32,3072]{1,0:T(8,128)(2,1)S(1)}, u32[]{:S(2)}, u32[]{:S(2)}) %collective-permute-start.32) | collective-permute-done | bytes 196640 | tf_op jit(solution)/shard_map/window_9/ppermute | solution.py:24
  128.7 11.2 %shard_map.127 = (bf16[256,1024]{1,0:T(8,128)(2,1)S(1)}, bf16[256,1024]{1,0:T(8,128)(2,1)S(1)}, bf16[256,128]{1,0:T(8,128)(2,1)S(1)}) custom-call(bf16[32,6144]{1,0:T(8,128)(2,1)S(1)} %get-tuple-element.95.refs_0_, bf16[32,6144]{1,0:T(8,128)(2,1)S(1)} %get-tuple-element.97.refs_1_, bf16[32,6144]{1,0:T(8,128)(2,1)S(1)} %get-tuple-element.101.refs_2_, ...), custom_call_target="tpu_custom_call" | custom-call | flops 6442450944 | bytes 28311552 | tf_op jit(solution)/shard_map/pallas_call | solution.py:283
  141.6 10.3 %shard_map.129.refs_2_ = bf16[256,6272]{1,0:T(8,128)(2,1)S(1)} custom-call(bf16[256,1024]{1,0:T(8,128)(2,1)S(1)} %get-tuple-element.117.gate_cot_ref, bf16[256,1024]{1,0:T(8,128)(2,1)S(1)} %get-tuple-element.118.up_cot_ref, bf16[256,128]{1,0:T(8,128)(2,1)S(1)} %get-tuple-element.119.slope_ref, bf16[6144,1024]{1,0:T(8,128)(2,1)} %bitcast.85, ...), custom_call_target="tpu_custom_call" | custom-call | flops 6442450944 | bytes 25165824 | tf_op jit(solution)/shard_map/pallas_call | solution.py:341
  155.3 9.9 %collective-permute-done.42.refs_2_ = bf16[32,3136]{1,0:T(8,128)(2,1)S(1)} collective-permute-done((bf16[32,3136]{1,0:T(8,128)(2,1)S(1)}, bf16[32,3136]{1,0:T(8,128)(2,1)S(1)}, u32[]{:S(2)}, u32[]{:S(2)}) %collective-permute-start.42) | collective-permute-done | bytes 200736 | tf_op jit(solution)/shard_map/window_12/ppermute | solution.py:24
  167.7 12.8 %collective-permute-start.46 = (bf16[32,6144]{1,0:T(8,128)(2,1)S(1)}, bf16[32,6144]{1,0:T(8,128)(2,1)S(1)}, u32[]{:S(2)}, u32[]{:S(2)}) collective-permute-start(bf16[32,6144]{1,0:T(8,128)(2,1)S(1)} %add_convert_fusion.4), channel_id=1, source_target_pairs={{0,8},{8,16},{16,24},{24,0},{1,9},{9,17},{17,25},{25,1},{2,10},{10... | collective-permute-start | bytes 1179656 | tf_op jit(solution)/shard_map/ppermute | solution.py:29
  180.5 4.7 %collective-permute-done.46.refs_2_ = bf16[32,6144]{1,0:T(8,128)(2,1)S(1)} collective-permute-done((bf16[32,6144]{1,0:T(8,128)(2,1)S(1)}, bf16[32,6144]{1,0:T(8,128)(2,1)S(1)}, u32[]{:S(2)}, u32[]{:S(2)}) %collective-permute-start.46) | collective-permute-done | bytes 393248 | tf_op jit(solution)/shard_map/ppermute | solution.py:29
  186.9 6.8 %collective-permute-done.47.refs_0_ = bf16[32,6272]{1,0:T(8,128)(2,1)S(1)} collective-permute-done((bf16[32,6272]{1,0:T(8,128)(2,1)S(1)}, bf16[32,6272]{1,0:T(8,128)(2,1)S(1)}, u32[]{:S(2)}, u32[]{:S(2)}) %collective-permute-start.47) | collective-permute-done | bytes 401440 | tf_op jit(solution)/shard_map/window_14/ppermute | solution.py:24
  195.5 7.8 %collective-permute-done.49 = bf16[32,6272]{1,0:T(8,128)(2,1)S(1)} collective-permute-done((bf16[32,6272]{1,0:T(8,128)(2,1)S(1)}, bf16[32,6272]{1,0:T(8,128)(2,1)S(1)}, u32[]{:S(2)}, u32[]{:S(2)}) %collective-permute-start.49) | collective-permute-done | bytes 401440 | tf_op jit(solution)/shard_map/window_15/ppermute | solution.py:24
  205.2 7.6 %collective-permute-start.51 = (bf16[32,6144]{1,0:T(8,128)(2,1)S(1)}, bf16[32,6144]{1,0:T(8,128)(2,1)S(1)}, u32[]{:S(2)}, u32[]{:S(2)}) collective-permute-start(bf16[32,6144]{1,0:T(8,128)(2,1)S(1)} %fusion.13), channel_id=1, source_target_pairs={{0,24},{8,0},{16,8},{24,16},{1,25},{9,1},{17,9},{25,17},{2,26},{10... | collective-permute-start | bytes 1179656 | tf_op jit(solution)/shard_map/ppermute | solution.py:29
  214.6 4.5 %collective-permute-done.51 = bf16[32,6144]{1,0:T(8,128)(2,1)S(1)} collective-permute-done((bf16[32,6144]{1,0:T(8,128)(2,1)S(1)}, bf16[32,6144]{1,0:T(8,128)(2,1)S(1)}, u32[]{:S(2)}, u32[]{:S(2)}) %collective-permute-start.51) | collective-permute-done | bytes 393248 | tf_op jit(solution)/shard_map/ppermute | solution.py:29
  (218 shorter events, 61.1 us)
Async XLA Ops:
  7.8 12.4 %collective-permute-start.2 = (bf16[32,6144]{1,0:T(8,128)(2,1)S(1)}, bf16[32,6144]{1,0:T(8,128)(2,1)S(1)}, u32[]{:S(2)}, u32[]{:S(2)}) collective-permute-start(bf16[32,6144]{1,0:T(8,128)(2,1)S(1)} %get-tuple-element.180), channel_id=1, source_target_pairs={{0,8},{8,16},{16,24},{24,0},{1,9},{9,17},{17,25},{25,1},{2,10},{10... | collective-permute-start | bytes 1179656 | tf_op jit(solution)/shard_map/window_0/ppermute | solution.py:29
  10.5 11.8 %collective-permute-start.3 = (bf16[32,6144]{1,0:T(8,128)(2,1)S(1)}, bf16[32,6144]{1,0:T(8,128)(2,1)S(1)}, u32[]{:S(2)}, u32[]{:S(2)}) collective-permute-start(bf16[32,6144]{1,0:T(8,128)(2,1)S(1)} %get-tuple-element.176), channel_id=1, source_target_pairs={{0,24},{8,0},{16,8},{24,16},{1,25},{9,1},{17,9},{25,17},{2,26},{10... | collective-permute-start | bytes 1179656 | tf_op jit(solution)/shard_map/window_0/ppermute | solution.py:29
  10.5 16.6 %collective-permute-start.6 = (bf16[32,6144]{1,0:T(8,128)(2,1)S(1)}, bf16[32,6144]{1,0:T(8,128)(2,1)S(1)}, u32[]{:S(2)}, u32[]{:S(2)}) collective-permute-start(bf16[32,6144]{1,0:T(8,128)(2,1)S(1)} %get-tuple-element.179), channel_id=1, source_target_pairs={{0,8},{8,16},{16,24},{24,0},{1,9},{9,17},{17,25},{25,1},{2,10},{10... | collective-permute-start | bytes 1179656 | tf_op jit(solution)/shard_map/window_1/ppermute | solution.py:29
  16.4 14.3 %collective-permute-start.7 = (bf16[32,6144]{1,0:T(8,128)(2,1)S(1)}, bf16[32,6144]{1,0:T(8,128)(2,1)S(1)}, u32[]{:S(2)}, u32[]{:S(2)}) collective-permute-start(bf16[32,6144]{1,0:T(8,128)(2,1)S(1)} %get-tuple-element.175), channel_id=1, source_target_pairs={{0,24},{8,0},{16,8},{24,16},{1,25},{9,1},{17,9},{25,17},{2,26},{10... | collective-permute-start | bytes 1179656 | tf_op jit(solution)/shard_map/window_1/ppermute | solution.py:29
  17.6 22.0 %collective-permute-start.10 = (bf16[32,6144]{1,0:T(8,128)(2,1)S(1)}, bf16[32,6144]{1,0:T(8,128)(2,1)S(1)}, u32[]{:S(2)}, u32[]{:S(2)}) collective-permute-start(bf16[32,6144]{1,0:T(8,128)(2,1)S(1)} %get-tuple-element.181), channel_id=1, source_target_pairs={{0,8},{8,16},{16,24},{24,0},{1,9},{9,17},{17,25},{25,1},{2,10},{10... | collective-permute-start | bytes 1179656 | tf_op jit(solution)/shard_map/window_2/ppermute | solution.py:29
  20.2 19.4 %collective-permute-start.11 = (bf16[32,6144]{1,0:T(8,128)(2,1)S(1)}, bf16[32,6144]{1,0:T(8,128)(2,1)S(1)}, u32[]{:S(2)}, u32[]{:S(2)}) collective-permute-start(bf16[32,6144]{1,0:T(8,128)(2,1)S(1)} %get-tuple-element.177), channel_id=1, source_target_pairs={{0,24},{8,0},{16,8},{24,16},{1,25},{9,1},{17,9},{25,17},{2,26},{10... | collective-permute-start | bytes 1179656 | tf_op jit(solution)/shard_map/window_2/ppermute | solution.py:29
  30.7 20.3 %collective-permute-start.18 = (bf16[32,6144]{1,0:T(8,128)(2,1)S(1)}, bf16[32,6144]{1,0:T(8,128)(2,1)S(1)}, u32[]{:S(2)}, u32[]{:S(2)}) collective-permute-start(bf16[32,6144]{1,0:T(8,128)(2,1)S(1)} %get-tuple-element.178), channel_id=1, source_target_pairs={{0,8},{8,16},{16,24},{24,0},{1,9},{9,17},{17,25},{25,1},{2,10},{10... | collective-permute-start | bytes 1179656 | tf_op jit(solution)/shard_map/window_3/ppermute | solution.py:29
  49.4 13.6 %collective-permute-start.16 = (bf16[32,6144]{1,0:T(8,128)(2,1)S(1)}, bf16[32,6144]{1,0:T(8,128)(2,1)S(1)}, u32[]{:S(2)}, u32[]{:S(2)}) collective-permute-start(bf16[32,6144]{1,0:T(8,128)(2,1)S(1)} %get-tuple-element.86.refs_0_), channel_id=1, source_target_pairs={{0,2},{2,4},{4,6},{6,7},{7,5},{5,3},{3,1},{1,0},{8,10},{10,12},{12... | collective-permute-start | bytes 1179656 | tf_op jit(solution)/shard_map/window_3/ppermute | solution.py:24
  49.5 13.5 %collective-permute-start.17 = (bf16[32,6144]{1,0:T(8,128)(2,1)S(1)}, bf16[32,6144]{1,0:T(8,128)(2,1)S(1)}, u32[]{:S(2)}, u32[]{:S(2)}) collective-permute-start(bf16[32,6144]{1,0:T(8,128)(2,1)S(1)} %get-tuple-element.86.refs_0_), channel_id=1, source_target_pairs={{0,1},{2,0},{4,2},{6,4},{7,6},{5,7},{3,5},{1,3},{8,9},{10,8},{12,1... | collective-permute-start | bytes 1179656 | tf_op jit(solution)/shard_map/window_3/ppermute | solution.py:24
  50.8 12.1 %collective-permute-start.14 = (bf16[32,3072]{1,0:T(8,128)(2,1)S(1)}, bf16[32,3072]{1,0:T(8,128)(2,1)S(1)}, u32[]{:S(2)}, u32[]{:S(2)}) collective-permute-start(bf16[32,3072]{1,0:T(8,128)(2,1)S(1)} %slice.184), channel_id=1, source_target_pairs={{0,2},{2,4},{4,6},{6,7},{7,5},{5,3},{3,1},{1,0},{8,10},{10,12},{12... | collective-permute-start | bytes 589832 | tf_op jit(solution)/shard_map/window_3/ppermute | solution.py:24
  51.0 11.9 %collective-permute-start.15 = (bf16[32,3072]{1,0:T(8,128)(2,1)S(1)}, bf16[32,3072]{1,0:T(8,128)(2,1)S(1)}, u32[]{:S(2)}, u32[]{:S(2)}) collective-permute-start(bf16[32,3072]{1,0:T(8,128)(2,1)S(1)} %slice.185), channel_id=1, source_target_pairs={{0,1},{2,0},{4,2},{6,4},{7,6},{5,7},{3,5},{1,3},{8,9},{10,8},{12,1... | collective-permute-start | bytes 589832 | tf_op jit(solution)/shard_map/window_3/ppermute | solution.py:24
  93.0 12.9 %collective-permute-start.28 = (bf16[32,6144]{1,0:T(8,128)(2,1)S(1)}, bf16[32,6144]{1,0:T(8,128)(2,1)S(1)}, u32[]{:S(2)}, u32[]{:S(2)}) collective-permute-start(bf16[32,6144]{1,0:T(8,128)(2,1)S(1)} %get-tuple-element.96.refs_7_), channel_id=1, source_target_pairs={{0,2},{2,4},{4,6},{6,7},{7,5},{5,3},{3,1},{1,0},{8,10},{10,12},{12... | collective-permute-start | bytes 1179656 | tf_op jit(solution)/shard_map/window_7/ppermute | solution.py:24
  94.4 11.5 %collective-permute-start.29 = (bf16[32,6144]{1,0:T(8,128)(2,1)S(1)}, bf16[32,6144]{1,0:T(8,128)(2,1)S(1)}, u32[]{:S(2)}, u32[]{:S(2)}) collective-permute-start(bf16[32,6144]{1,0:T(8,128)(2,1)S(1)} %get-tuple-element.97.refs_1_), channel_id=1, source_target_pairs={{0,1},{2,0},{4,2},{6,4},{7,6},{5,7},{3,5},{1,3},{8,9},{10,8},{12,1... | collective-permute-start | bytes 1179656 | tf_op jit(solution)/shard_map/window_7/ppermute | solution.py:24
  127.0 12.8 %collective-permute-start.37 = (bf16[32,6144]{1,0:T(8,128)(2,1)S(1)}, bf16[32,6144]{1,0:T(8,128)(2,1)S(1)}, u32[]{:S(2)}, u32[]{:S(2)}) collective-permute-start(bf16[32,6144]{1,0:T(8,128)(2,1)S(1)} %pad_maximum_fusion.5), channel_id=1, source_target_pairs={{0,1},{2,0},{4,2},{6,4},{7,6},{5,7},{3,5},{1,3},{8,9},{10,8},{12,1... | collective-permute-start | bytes 1179656 | tf_op jit(solution)/shard_map/window_10/ppermute | solution.py:24
  127.8 12.0 %collective-permute-start.36 = (bf16[32,6144]{1,0:T(8,128)(2,1)S(1)}, bf16[32,6144]{1,0:T(8,128)(2,1)S(1)}, u32[]{:S(2)}, u32[]{:S(2)}) collective-permute-start(bf16[32,6144]{1,0:T(8,128)(2,1)S(1)} %pad_maximum_fusion.4), channel_id=1, source_target_pairs={{0,2},{2,4},{4,6},{6,7},{7,5},{5,3},{3,1},{1,0},{8,10},{10,12},{12... | collective-permute-start | bytes 1179656 | tf_op jit(solution)/shard_map/window_10/ppermute | solution.py:24
  140.0 11.8 %collective-permute-start.38 = (bf16[32,6144]{1,0:T(8,128)(2,1)S(1)}, bf16[32,6144]{1,0:T(8,128)(2,1)S(1)}, u32[]{:S(2)}, u32[]{:S(2)}) collective-permute-start(bf16[32,6144]{1,0:T(8,128)(2,1)S(1)} %get-tuple-element.167), channel_id=1, source_target_pairs={{0,2},{2,4},{4,6},{6,7},{7,5},{5,3},{3,1},{1,0},{8,10},{10,12},{12... | collective-permute-start | bytes 1179656 | tf_op jit(solution)/shard_map/window_11/ppermute | solution.py:24
  140.2 11.7 %collective-permute-start.39 = (bf16[32,6144]{1,0:T(8,128)(2,1)S(1)}, bf16[32,6144]{1,0:T(8,128)(2,1)S(1)}, u32[]{:S(2)}, u32[]{:S(2)}) collective-permute-start(bf16[32,6144]{1,0:T(8,128)(2,1)S(1)} %get-tuple-element.166), channel_id=1, source_target_pairs={{0,1},{2,0},{4,2},{6,4},{7,6},{5,7},{3,5},{1,3},{8,9},{10,8},{12,1... | collective-permute-start | bytes 1179656 | tf_op jit(solution)/shard_map/window_11/ppermute | solution.py:24
  152.1 13.4 %collective-permute-start.40 = (bf16[32,6144]{1,0:T(8,128)(2,1)S(1)}, bf16[32,6144]{1,0:T(8,128)(2,1)S(1)}, u32[]{:S(2)}, u32[]{:S(2)}) collective-permute-start(bf16[32,6144]{1,0:T(8,128)(2,1)S(1)} %get-tuple-element.165), channel_id=1, source_target_pairs={{0,2},{2,4},{4,6},{6,7},{7,5},{5,3},{3,1},{1,0},{8,10},{10,12},{12... | collective-permute-start | bytes 1179656 | tf_op jit(solution)/shard_map/window_12/ppermute | solution.py:24
  152.5 13.0 %collective-permute-start.41 = (bf16[32,6144]{1,0:T(8,128)(2,1)S(1)}, bf16[32,6144]{1,0:T(8,128)(2,1)S(1)}, u32[]{:S(2)}, u32[]{:S(2)}) collective-permute-start(bf16[32,6144]{1,0:T(8,128)(2,1)S(1)} %get-tuple-element.164), channel_id=1, source_target_pairs={{0,1},{2,0},{4,2},{6,4},{7,6},{5,7},{3,5},{1,3},{8,9},{10,8},{12,1... | collective-permute-start | bytes 1179656 | tf_op jit(solution)/shard_map/window_12/ppermute | solution.py:24
  153.8 11.4 %collective-permute-start.42 = (bf16[32,3136]{1,0:T(8,128)(2,1)S(1)}, bf16[32,3136]{1,0:T(8,128)(2,1)S(1)}, u32[]{:S(2)}, u32[]{:S(2)}) collective-permute-start(bf16[32,3136]{1,0:T(8,128)(2,1)S(1)} %get-tuple-element.161), channel_id=1, source_target_pairs={{0,2},{2,4},{4,6},{6,7},{7,5},{5,3},{3,1},{1,0},{8,10},{10,12},{12... | collective-permute-start | bytes 602120 | tf_op jit(solution)/shard_map/window_12/ppermute | solution.py:24
  165.8 19.4 %collective-permute-start.45 = (bf16[32,6272]{1,0:T(8,128)(2,1)S(1)}, bf16[32,6272]{1,0:T(8,128)(2,1)S(1)}, u32[]{:S(2)}, u32[]{:S(2)}) collective-permute-start(bf16[32,6272]{1,0:T(8,128)(2,1)S(1)} %pad_maximum_fusion.1), channel_id=1, source_target_pairs={{0,1},{2,0},{4,2},{6,4},{7,6},{5,7},{3,5},{1,3},{8,9},{10,8},{12,1... | collective-permute-start | bytes 1204232 | tf_op jit(solution)/shard_map/window_13/ppermute | solution.py:24
  167.1 18.1 %collective-permute-start.44 = (bf16[32,6272]{1,0:T(8,128)(2,1)S(1)}, bf16[32,6272]{1,0:T(8,128)(2,1)S(1)}, u32[]{:S(2)}, u32[]{:S(2)}) collective-permute-start(bf16[32,6272]{1,0:T(8,128)(2,1)S(1)} %pad_maximum_fusion), channel_id=1, source_target_pairs={{0,2},{2,4},{4,6},{6,7},{7,5},{5,3},{3,1},{1,0},{8,10},{10,12},{12... | collective-permute-start | bytes 1204232 | tf_op jit(solution)/shard_map/window_13/ppermute | solution.py:24
  167.7 17.5 %collective-permute-start.46 = (bf16[32,6144]{1,0:T(8,128)(2,1)S(1)}, bf16[32,6144]{1,0:T(8,128)(2,1)S(1)}, u32[]{:S(2)}, u32[]{:S(2)}) collective-permute-start(bf16[32,6144]{1,0:T(8,128)(2,1)S(1)} %add_convert_fusion.4), channel_id=1, source_target_pairs={{0,8},{8,16},{16,24},{24,0},{1,9},{9,17},{17,25},{25,1},{2,10},{10... | collective-permute-start | bytes 1179656 | tf_op jit(solution)/shard_map/ppermute | solution.py:29
  205.2 13.8 %collective-permute-start.51 = (bf16[32,6144]{1,0:T(8,128)(2,1)S(1)}, bf16[32,6144]{1,0:T(8,128)(2,1)S(1)}, u32[]{:S(2)}, u32[]{:S(2)}) collective-permute-start(bf16[32,6144]{1,0:T(8,128)(2,1)S(1)} %fusion.13), channel_id=1, source_target_pairs={{0,24},{8,0},{16,8},{24,16},{1,25},{9,1},{17,9},{25,17},{2,26},{10... | collective-permute-start | bytes 1179656 | tf_op jit(solution)/shard_map/ppermute | solution.py:29
  (54 other events, 639.5 us)

commit v3 on v0

v3 whole, which is shorter than its diff:
```python
import functools

import jax
import jax.numpy as jnp
from jax import lax
from jax.experimental import pallas as pl
from jax.experimental.pallas import tpu as pltpu
from jax.sharding import PartitionSpec as P

epsilon = 1e-05
highest = lax.Precision.HIGHEST
f32 = jnp.float32
bf16 = jnp.bfloat16
last_dims = (((1,), (1,)), ((), ()))
first_dims = (((0,), (0,)), ((), ()))
in_hbm = pl.BlockSpec(memory_space=pltpu.HBM)
anywhere = pl.BlockSpec(memory_space=pl.ANY)
in_vmem = pl.BlockSpec(memory_space=pltpu.VMEM)


def shape_of(rows, columns, dtype=bf16):
    return jax.ShapeDtypeStruct((rows, columns), dtype)


def params(mega):
    return pltpu.CompilerParams(vmem_limit_bytes=mega * 1024 * 1024)


def cost(flops, moved):
    return pl.CostEstimate(flops=int(flops), bytes_accessed=int(moved), transcendentals=0)


def dot_t(left, right):
    return lax.dot_general(left, right, last_dims, preferred_element_type=f32)


def dot_n(left, right):
    return jnp.dot(left, right, preferred_element_type=f32)


def hop(value, steps):
    count = lax.axis_size("expert")
    ring = list(range(0, count, 2)) + list(range(1, count, 2))[::-1]
    return lax.ppermute(value, "expert", [(ring[i], ring[(i + steps) % count]) for i in range(count)])


def shifted(value, steps):
    count = lax.axis_size("section")
    return lax.ppermute(value, "section", [(source, (source + steps) % count) for source in range(count)])


def halves(value):
    middle = value.shape[1] // 2
    return [value[:, :middle], value[:, middle:]]


class Ring:

    def __init__(self, name):
        self.name = name
        self.count = lax.axis_size("expert")
        self.full = (self.count - 1) // 2
        self.split = self.count % 2 == 0
        self.steps = self.full + self.split


class Gather(Ring):

    def begin(self, shard):
        self.held = [[shard]] + [None] * (self.count - 1)

    def send(self, step):
        ahead = self.held[-step % self.count][0]
        behind = self.held[step][0]
        if step == self.full:
            ahead, behind = halves(ahead)[0], halves(behind)[1]
        return [hop(ahead, 1), hop(behind, -1)]

    def receive(self, step, values):
        if step == self.full:
            self.held[step + 1] = values
        else:
            self.held[-1 - step], self.held[step + 1] = [values[0]], [values[1]]

    def sources(self, step):
        return [self.held[0]] if step == 0 else []


class Scatter(Ring):

    def begin(self, parts):
        self.parts = parts

    def send(self, step):
        far = self.steps - step
        if step > 0:
            ahead, behind = merge_call(self.parts[far][0], self.inbox[0], self.parts[-far][0], self.inbox[1])
        else:
            ahead, behind = self.parts[far][0], self.parts[-far][-1]
        return [hop(ahead, 1), hop(behind, -1)]

    def receive(self, step, values):
        self.inbox = values

    def sources(self, step):
        return [self.parts[self.steps]] + [self.parts[-self.steps]] * (1 - self.split) if step == 0 else []


def fence(arrays):
    return list(
        pl.pallas_call(
            lambda *refs: None,
            in_specs=[anywhere] * len(arrays),
            out_specs=[anywhere] * len(arrays),
            out_shape=[jax.ShapeDtypeStruct(array.shape, array.dtype) for array in arrays],
            compiler_params=params(1),
            cost_estimate=cost(0, 0),
            input_output_aliases={k: k for k in range(len(arrays))},
        )(*arrays)
    )


def run_windows(windows, pieces, env):
    flying, made = [], []
    for k, transfers in enumerate(windows):
        todo = pieces.get(k, [])
        names = list(made)
        for needs, _, _ in todo:
            names += [name for name in needs if name not in names]
        sources = env.pop("renewed", [])
        for ring, step, _ in transfers:
            sources += [held for held in ring.sources(step) if not any(held is other for other in sources)]
        landing = [flight for flight in flying if flight[2] <= k]
        flying = [flight for flight in flying if flight[2] > k]
        landed = [value for _, _, _, values in landing for value in values]
        passed = fence(landed + [env[name] for name in names] + [value for held in sources for value in held])
        for ring, step, _, values in landing:
            ring.receive(step, passed[: len(values)])
            passed = passed[len(values) :]
        for name in names:
            env[name] = passed.pop(0)
        for held in sources:
            held[:] = [passed.pop(0) for _ in held]
        with jax.named_scope(f"window_{k}"):
            flying += [(ring, step, k + stay, ring.send(step)) for ring, step, stay in transfers]
        made = []
        for needs, does, gives in todo:
            for name, value in zip(gives, does(*[env[name] for name in needs]), strict=True):
                env[name] = value
                made.append(name)
    for ring, step, _, values in flying:
        ring.receive(step, values)


def pieces_of(length, most, grain):
    for number in range(most, 1, -1):
        if length % (number * grain) == 0:
            size = length // number
            return [slice(k * size, (k + 1) * size) for k in range(number)]
    return [slice(0, length)]


def flat(held):
    return [value for shard in held for value in shard]


def row_copies(held_shape, shards, rows_ref, sems):
    side = rows_ref.shape[0] // len(held_shape)
    copies, at = [], 0
    for k, widths in enumerate(held_shape):
        first = 0
        for wide in widths:
            target = rows_ref.at[k * side : (k + 1) * side, first : first + wide]
            copies.append(pltpu.make_async_copy(shards[at], target, sems.at[at]))
            first, at = first + wide, at + 1
    return copies


def widths_of(held):
    return tuple(tuple(value.shape[1] for value in shard) for shard in held)


def start_all(*lists):
    for group in zip(*lists, strict=True):
        for copy in group:
            copy.start()


def merge_kernel(own_a_ref, value_a_ref, own_b_ref, value_b_ref, out_a_ref, out_b_ref):
    for own_ref, value_ref, out_ref, first in (
        (own_a_ref, value_a_ref, out_a_ref, 0),
        (own_b_ref, value_b_ref, out_b_ref, own_b_ref.shape[1] - value_b_ref.shape[1]),
    ):
        here = slice(first, first + value_ref.shape[1])
        if value_ref.shape != own_ref.shape:
            out_ref[...] = own_ref[...]
        out_ref[:, here] = (own_ref[:, here].astype(f32) + value_ref[...].astype(f32)).astype(bf16)


def merge_call(own_a, value_a, own_b, value_b):
    return pl.pallas_call(
        merge_kernel,
        in_specs=[in_vmem] * 4,
        out_specs=[in_vmem] * 2,
        out_shape=[shape_of(*own.shape) for own in (own_a, own_b)],
        compiler_params=params(4),
        cost_estimate=cost(0, 6 * own_a.size),
    )(own_a, value_a, own_b, value_b)


def load_kernel(after_ref, source, target, flag_ref, sems):
    copies = [
        pltpu.make_async_copy(source.at[part], target.at[part], sems.at[k])
        for k, part in enumerate(pieces_of(source.shape[0], 4, 128))
    ]
    start_all(copies)
    flag_ref[...] = jnp.zeros_like(flag_ref)
    for copy in copies:
        copy.wait()


def load_call(after, weight):
    return pl.pallas_call(
        load_kernel,
        in_specs=[anywhere, in_hbm],
        out_specs=[in_vmem, in_vmem],
        out_shape=[pltpu.VMEM(weight.shape, weight.dtype), shape_of(8, 128, f32)],
        scratch_shapes=[pltpu.SemaphoreType.DMA((4,))],
        compiler_params=params(1),
        cost_estimate=cost(0, 4 * weight.size),
    )(after, weight)


def back_kernel(held_shape, *refs):
    count = sum(len(widths) for widths in held_shape)
    shards, (down_ref, out_ref, rows_ref, weight_ref, row_sems, sems) = refs[:count], refs[count:]
    parts = pieces_of(out_ref.shape[1], 4, 128)
    rows = row_copies(held_shape, shards, rows_ref, row_sems)
    downs = [
        pltpu.make_async_copy(down_ref.at[part], weight_ref.at[part], sems.at[k])
        for k, part in enumerate(parts)
    ]
    start_all(rows)
    start_all(downs)
    for copy in rows:
        copy.wait()
    for part, copy in zip(parts, downs, strict=True):
        copy.wait()
        out_ref[:, part] = dot_t(rows_ref[...], weight_ref[part, :])


def back_call(held, down):
    count, side, width, hid = len(held), held[0][0].shape[0], sum(widths_of(held)[0]), down.shape[0]
    return pl.pallas_call(
        functools.partial(back_kernel, widths_of(held)),
        in_specs=[anywhere] * len(flat(held)) + [in_hbm],
        out_specs=in_vmem,
        out_shape=shape_of(count * side, hid, f32),
        scratch_shapes=[
            pltpu.VMEM((count * side, width), bf16),
            pltpu.VMEM((hid, width), bf16),
            pltpu.SemaphoreType.DMA((len(flat(held)),)),
            pltpu.SemaphoreType.DMA((4,)),
        ],
        compiler_params=params(22),
        cost_estimate=cost(2 * count * side * width * hid, 2 * width * (hid + count * side)),
    )(*flat(held), down)


def gate_up(held_shape, shards, gate_ref, up_ref, rows_ref, gate_sum, up_sum, row_sems):
    rows = row_copies(held_shape, shards, rows_ref, row_sems)
    start_all(rows)
    for copy in rows:
        copy.wait()
    for k, part in enumerate(pieces_of(gate_ref.shape[0], 6, 128)):
        for weight, total in ((gate_ref, gate_sum), (up_ref, up_sum)):
            product = dot_n(rows_ref[:, part], weight[part, :])
            total[...] = product if k == 0 else total[...] + product


def gate_up_scratch(copies, count, side, width, hid):
    return [
        pltpu.VMEM((count * side, width), bf16),
        pltpu.VMEM((count * side, hid), f32),
        pltpu.VMEM((count * side, hid), f32),
        pltpu.SemaphoreType.DMA((copies,)),
    ]


def gate_up_cost(count, side, width, hid):
    return cost(4 * count * side * width * hid, 2 * width * (2 * hid + count * side))


def active_kernel(held_shape, *refs):
    count = sum(len(widths) for widths in held_shape)
    shards, (gate_ref, up_ref, out_ref, *scratch) = refs[:count], refs[count:]
    gate_up(held_shape, shards, gate_ref, up_ref, *scratch)
    gate_pre = scratch[1][...]
    out_ref[...] = (gate_pre * jax.nn.sigmoid(gate_pre) * scratch[2][...]).astype(bf16)


def active_call(held, gate, up):
    count, side, width, hid = len(held), held[0][0].shape[0], sum(widths_of(held)[0]), gate.shape[1]
    return pl.pallas_call(
        functools.partial(active_kernel, widths_of(held)),
        in_specs=[anywhere] * len(flat(held)) + [in_vmem] * 2,
        out_specs=in_vmem,
        out_shape=shape_of(count * side, hid),
        scratch_shapes=gate_up_scratch(len(flat(held)), count, side, width, hid),
        compiler_params=params(12),
        cost_estimate=gate_up_cost(count, side, width, hid),
    )(*flat(held), gate, up)


def cots_kernel(held_shape, *refs):
    count = sum(len(widths) for widths in held_shape)
    shards, (gate_ref, up_ref, back_ref, gate_cot_ref, up_cot_ref, slope_ref, *scratch) = refs[:count], refs[count:]
    gate_up(held_shape, shards, gate_ref, up_ref, *scratch)
    gate_pre, up_pre = scratch[1][...], scratch[2][...]
    sig = jax.nn.sigmoid(gate_pre)
    silu = gate_pre * sig
    back = back_ref[...]
    active = (silu * up_pre).astype(bf16).astype(f32)
    slope_ref[...] = jnp.broadcast_to(jnp.sum(active * back, axis=1, keepdims=True), slope_ref.shape)
    gate_cot_ref[...] = (back * up_pre * sig * (1.0 + gate_pre * (1.0 - sig))).astype(bf16)
    up_cot_ref[...] = (back * silu).astype(bf16)


def cots_call(held, gate, up, back):
    count, side, width, hid = len(held), held[0][0].shape[0], sum(widths_of(held)[0]), gate.shape[1]
    return pl.pallas_call(
        functools.partial(cots_kernel, widths_of(held)),
        in_specs=[anywhere] * len(flat(held)) + [in_vmem] * 3,
        out_specs=[in_vmem] * 3,
        out_shape=[
            shape_of(count * side, hid),
            shape_of(count * side, hid),
            shape_of(count * side, 128, f32),
        ],
        scratch_shapes=gate_up_scratch(len(flat(held)), count, side, width, hid),
        compiler_params=params(14),
        cost_estimate=gate_up_cost(count, side, width, hid),
    )(*flat(held), gate, up, back)


def segments(count, width, extra):
    whole, pair = [(0, width + extra)], [(0, width // 2), (width // 2, width + extra)]
    return [pair if 2 * k == count else whole for k in range(count)]


def part_shapes(side, held):
    return [shape_of(side, last - first) for ranges in held for first, last in ranges]


def spread(made, held, first, value):
    side, last, at = value.shape[0] // len(held), first + value.shape[1], 0
    for k, ranges in enumerate(held):
        for low, high in ranges:
            begin, end = max(first, low), min(last, high)
            if begin < end:
                rows = value[k * side : (k + 1) * side, begin - first : end - first]
                made[at][:, begin - low : end - low] = rows
            at += 1


def send_out(made, out_refs, sems):
    copies = [
        pltpu.make_async_copy(source, target, sems.at[at])
        for at, (source, target) in enumerate(zip(made, out_refs, strict=True))
    ]
    start_all(copies)
    for copy in copies:
        copy.wait()


def made_scratch(shapes):
    return [pltpu.VMEM(shape.shape, shape.dtype) for shape in shapes] + [pltpu.SemaphoreType.DMA((len(shapes),))]


def regroup(held, arrays):
    arrays = list(arrays)
    return [[arrays.pop(0) for _ in ranges] for ranges in held]


def outpart_kernel(held, active_ref, down_ref, *refs):
    number = sum(len(ranges) for ranges in held)
    out_refs, made, (out_sems, down_w, sems) = refs[:number], refs[number : 2 * number], refs[2 * number :]
    width = down_ref.shape[1]
    parts = pieces_of(width, 6, 128)
    downs = [
        pltpu.make_async_copy(down_ref.at[:, part], down_w.at[:, part], sems.at[k]) for k, part in enumerate(parts)
    ]
    start_all(downs)
    for part, copy in zip(parts, downs, strict=True):
        copy.wait()
        value = dot_n(active_ref[...], down_w[:, part])
        spread(made, held, part.start, value.astype(bf16))
    send_out(made, out_refs, out_sems)


def outpart_call(count, active, down):
    rows, (hid, width) = active.shape[0], down.shape
    held = segments(count, width, 0)
    shapes = part_shapes(rows // count, held)
    arrays = pl.pallas_call(
        functools.partial(outpart_kernel, held),
        in_specs=[in_vmem, in_hbm],
        out_specs=[anywhere] * len(shapes),
        out_shape=shapes,
        scratch_shapes=made_scratch(shapes) + [pltpu.VMEM((hid, width), bf16), pltpu.SemaphoreType.DMA((6,))],
        compiler_params=params(22),
        cost_estimate=cost(2 * rows * width * hid, 2 * width * hid),
    )(active, down)
    return regroup(held, arrays)


def rowpart_kernel(held, gate_cot_ref, up_cot_ref, slope_ref, gate_ref, up_ref, *refs):
    out_refs, (up_w, up_sems) = refs[:-2], refs[-2:]
    width = gate_ref.shape[0]
    parts = pieces_of(width, 6, 128)

    ups = [pltpu.make_async_copy(up_ref.at[part], up_w.at[part], up_sems.at[k]) for k, part in enumerate(parts)]
    start_all(ups)
    spread(out_refs, held, width, slope_ref[...].astype(bf16))
    for part, copy in zip(parts, ups, strict=True):
        value = dot_t(gate_cot_ref[...], gate_ref[part, :])
        copy.wait()
        value = value + dot_t(up_cot_ref[...], up_w[part, :])
        spread(out_refs, held, part.start, value.astype(bf16))


def rowpart_call(count, gate_cot, up_cot, slope, gate, up):
    rows, (width, hid) = gate_cot.shape[0], gate.shape
    held = segments(count, width, slope.shape[1])
    shapes = part_shapes(rows // count, held)
    arrays = pl.pallas_call(
        functools.partial(rowpart_kernel, held),
        in_specs=[in_vmem] * 4 + [in_hbm],
        out_specs=[in_vmem] * len(shapes),
        out_shape=shapes,
        scratch_shapes=[pltpu.VMEM((width, hid), bf16), pltpu.SemaphoreType.DMA((6,))],
        compiler_params=params(20),
        cost_estimate=cost(4 * rows * width * hid, 4 * width * hid),
    )(gate_cot, up_cot, slope, gate, up)
    return regroup(held, arrays)


def select_of(ids):
    tokens = ids.shape[1]
    capacity = tokens // 4
    named = jnp.max((ids == 0).astype(f32), axis=0, keepdims=True)
    row = lax.broadcasted_iota(jnp.int32, (tokens, tokens), 0)
    column = lax.broadcasted_iota(jnp.int32, (tokens, tokens), 1)
    earlier = (row < column).astype(bf16)
    rank = dot_n(jnp.broadcast_to(named, (8, tokens)).astype(bf16), earlier)[:1]
    slot = jnp.where(named > 0, rank, float(capacity))
    places = lax.broadcasted_iota(jnp.int32, (capacity, tokens), 0).astype(f32)
    return (slot == places).astype(f32)


def pick(select, values):
    return dot_n(select.astype(bf16), values)


def pick_kernel(after_ref, ids_ref, values_ref, select_ref, rows_ref):
    select = select_of(ids_ref[...])
    select_ref[...] = select.astype(bf16)
    rows_ref[...] = pick(select, values_ref[...]).astype(bf16)


def norm_kernel(after_ref, ids_ref, values_ref, gain_ref, select_ref, rows_ref, *normed_refs):
    select = select_of(ids_ref[...])
    select_ref[...] = select.astype(bf16)
    rows = pick(select, values_ref[...])
    rows_ref[...] = rows.astype(bf16)
    inverse = lax.rsqrt(jnp.mean(rows * rows, axis=1, keepdims=True) + epsilon)
    normed = (rows * inverse * gain_ref[...]).astype(bf16)
    first = 0
    for normed_ref in normed_refs:
        last = first + normed_ref.shape[1]
        normed_ref[...] = normed[:, first:last]
        first = last


def front_call(after, ids, values, gain=None, cuts=0):
    tokens, width = values.shape
    capacity = tokens // 4
    more = [] if gain is None else [gain]
    return pl.pallas_call(
        pick_kernel if gain is None else norm_kernel,
        in_specs=[anywhere] + [in_vmem] * (2 + len(more)),
        out_specs=[in_vmem] * (2 + cuts),
        out_shape=[shape_of(capacity, tokens), shape_of(capacity, width)]
        + [shape_of(capacity, width // cuts) for _ in range(cuts)],
        compiler_params=params(8),
        cost_estimate=cost(0, 8 * values.size),
    )(after, ids, values, *more)


def act_kernel(rows_ref, weight_ref, own_ref, a_ref, b_ref, out_ref):
    total = own_ref[...].astype(f32) + a_ref[...].astype(f32) + b_ref[...].astype(f32)
    out_ref[...] = (rows_ref[...].astype(f32) + weight_ref[:, :1] * total).astype(bf16)


def act_call(rows, weight, own, a, b):
    return pl.pallas_call(
        act_kernel,
        in_specs=[in_vmem] * 5,
        out_specs=in_vmem,
        out_shape=shape_of(*rows.shape),
        compiler_params=params(6),
        cost_estimate=cost(0, 10 * rows.size),
    )(rows, weight, own, a, b)


def grad_kernel(rows_ref, above_ref, gain_ref, scale_ref, tilt_ref, own_ref, a_ref, b_ref, out_ref):
    width = rows_ref.shape[1]
    total = own_ref[...].astype(f32) + a_ref[...].astype(f32) + b_ref[...].astype(f32)
    rows = rows_ref[...].astype(f32)
    scale = scale_ref[:, :1].astype(bf16).astype(f32)
    cot = (total[:, :width] * scale + tilt_ref[...] * total[:, width : width + 1]) * gain_ref[...]
    inverse = lax.rsqrt(jnp.mean(rows * rows, axis=1, keepdims=True) + epsilon)
    along = jnp.mean(rows * cot, axis=1, keepdims=True) * (inverse * inverse * inverse)
    out_ref[...] = (above_ref[...].astype(f32) + (inverse * cot - rows * along)).astype(bf16)


def grad_call(rows, above, gain, scale, tilt, sums):
    return pl.pallas_call(
        grad_kernel,
        in_specs=[in_vmem] * (5 + len(sums)),
        out_specs=in_vmem,
        out_shape=shape_of(*rows.shape),
        compiler_params=params(16),
        cost_estimate=cost(0, 16 * rows.size),
    )(rows, above, gain, scale, tilt, *sums)


def place_kernel(select_ref, rows_ref, base_ref, out_ref):
    select = select_ref[...]
    one = jnp.ones((select.shape[0], 128), bf16)
    used = lax.dot_general(select, one, first_dims, preferred_element_type=f32)[:, :1] > 0
    for part in pieces_of(base_ref.shape[1], 6, 128):
        spread_rows = lax.dot_general(select, rows_ref[:, part], first_dims, preferred_element_type=f32)
        out_ref[:, part] = jnp.where(used, spread_rows.astype(bf16), base_ref[:, part])


def place_call(select, rows, base):
    return pl.pallas_call(
        place_kernel,
        in_specs=[in_vmem] * 3,
        out_specs=in_vmem,
        out_shape=shape_of(*base.shape),
        compiler_params=params(12),
        cost_estimate=cost(0, 4 * base.size),
    )(select, rows, base)


def route_kernel(after_ref, rows_ref, gain_ref, router_ref, ids_ref, weight_ref, *tilt_refs):
    ids, experts = ids_ref[...], router_ref.shape[0]
    select = select_of(ids).astype(bf16)
    rows = rows_ref[...].astype(f32)
    inverse = lax.rsqrt(jnp.mean(rows * rows, axis=1, keepdims=True) + epsilon)
    logits = lax.dot_general(
        rows * inverse * gain_ref[...], router_ref[...], last_dims, precision=highest, preferred_element_type=f32
    )
    expert = lax.broadcasted_iota(jnp.int32, (experts, ids.shape[1]), 0)
    first, second = (dot_t(select, (ids[k : k + 1] == expert).astype(bf16)) for k in (0, 1))
    share = jax.nn.sigmoid(jnp.sum((first - second) * logits, axis=1, keepdims=True))
    first_named, second_named = first[:, :1], second[:, :1]
    weight = share * first_named + (1.0 - share) * second_named
    weight_ref[...] = jnp.broadcast_to(weight, weight_ref.shape)
    for tilt_ref in tilt_refs:
        slant = share * (1.0 - share) * (first_named - second_named)
        tilt_ref[...] = jnp.dot(
            slant * (first - second), router_ref[...], precision=highest, preferred_element_type=f32
        )


def route_call(after, rows, gain, router_mat, ids, tilts):
    capacity, width = rows.shape
    return pl.pallas_call(
        route_kernel,
        in_specs=[anywhere] + [in_vmem] * 4,
        out_specs=[in_vmem] * (1 + tilts),
        out_shape=[shape_of(capacity, 128, f32)] + [shape_of(capacity, width, f32)] * tilts,
        compiler_params=params(20),
        cost_estimate=cost(0, 12 * rows.size),
    )(after, rows, gain, router_mat, ids)


def local(
    act_in, saved_in, grad_in, fwd_routes, bwd_routes, w_gate, w_up, w_down, router, norm_gain
):
    count = lax.axis_size("expert")
    gate, up, down = (pltpu.with_memory_space_constraint(array[0], pltpu.HBM) for array in (w_gate, w_up, w_down))
    router_mat = router[0].T
    fwd_ids, bwd_ids = fwd_routes[0].T, bwd_routes[0].T
    gather_f, gather_u, gather_h = Gather("f"), Gather("u"), Gather("h")
    scatter_o, scatter_r = Scatter("o"), Scatter("r")
    env = {"act_base": shifted(act_in[0], 1), "grad_base": shifted(grad_in[0], -1)}

    env["select_f"], env["rows_f"], normed_f = front_call(norm_gain, fwd_ids, act_in[0], norm_gain, 1)
    gather_f.begin(normed_f)

    def front_u(after):
        env["select_b"], rows = front_call(after, bwd_ids, grad_in[0])
        env["rows_u"] = rows
        gather_u.begin(rows)
        return (rows[:16, :128],)

    def front_b(after):
        _, env["rows_b"], normed = front_call(after, bwd_ids, saved_in[0], norm_gain, 1)
        gather_h.begin(normed)
        return (normed[:16, :128],)

    def shifts(select_f):
        env["select_f_there"], env["select_b_there"] = shifted(select_f, 1), shifted(env["select_b"], -1)
        return ()

    def route_f(select_f):
        return tuple(route_call(select_f, env["rows_f"], norm_gain, router_mat, fwd_ids, 0))

    def route_b(select_f):
        return tuple(route_call(select_f, env["rows_b"], norm_gain, router_mat, bwd_ids, 1))

    def load(name, weight):
        def does(after):
            env[name], flag = load_call(after, weight)
            return (flag,)

        return does

    def active(after):
        return (active_call(gather_f.held, env["gate"], env["up"]),)

    def outpart(active):
        parts = outpart_call(count, active, down)
        scatter_o.begin(parts)
        return (parts[0][0][:16, :128],)

    def back(after):
        return (back_call(gather_u.held, down),)

    def cots(back):
        return cots_call(gather_h.held, env["gate"], env["up"], back)

    def rowpart(gate_cot, up_cot, slope):
        parts = rowpart_call(count, gate_cot, up_cot, slope, env["gate"], up)
        scatter_r.begin(parts)
        env["renewed"] = list(parts)
        return ()

    def act_rows(weight_f):
        rows = act_call(env["rows_f"], weight_f, scatter_o.parts[0][0], *scatter_o.inbox)
        env["act_rows"] = shifted(rows, 1)
        return ()

    def act_place(select, rows, base):
        return (place_call(select, rows, base),)

    last = gather_u.steps - 1
    windows = [[(gather_f, step, 1)] for step in range(last + 1)]
    windows[-1].append((gather_u, 0, 2))
    for step in range(1, last):
        windows += [[(gather_h, step - 1, 2)], [(gather_u, step, 2)]]
    windows += [[(gather_h, last - 1, 2)], [(gather_u, last, 1), (scatter_o, 0, 1)]]
    windows += [[(gather_h, last, 1), (scatter_o, 1, 1)]]
    windows += [[(scatter_o, step, 1)] for step in range(2, last + 1)]
    windows += [[(scatter_r, step, 1)] for step in range(last + 1)]
    start = {(ring, step): k for k, transfers in enumerate(windows) for ring, step, _ in transfers}
    pieces = {}

    def put(window, needs, does, gives):
        pieces.setdefault(window, []).append((needs, does, gives))

    def nothing(*arrays):
        return ()

    f_done = start[gather_f, last] + 1
    h_done = start[gather_h, last] + 1
    out = start[scatter_o, last]
    put(0, ("select_f",), front_u, ("corner_u",))
    put(1, ("select_f",), front_b, ("corner_b",))
    put(1, ("select_f",), load("gate", gate), ("flag_g",))
    put(2, ("select_f",), load("up", up), ("flag_u",))
    put(f_done, ("select_f",), active, ("active",))
    put(f_done + 1, ("active",), outpart, ("corner_o",))
    put(h_done-1, ("act_base",), nothing, ())
    put(out+1, ("grad_base",), nothing, ())
    put(out+1, ("select_f",), shifts, ())
    put(h_done - 1, ("select_f",), back, ("back",))
    put(h_done, ("back",), cots, ("gate_cot", "up_cot", "slope"))
    put(h_done + 1, ("gate_cot", "up_cot", "slope"), rowpart, ())
    put(out + 1, ("select_f",), route_f, ("weight_f",))
    put(out + 2, ("weight_f",), act_rows, ())
    put(out + 3, ("select_f",), route_b, ("scale", "tilt"))
    put(out + 4, ("select_f_there", "act_rows", "act_base"), act_place, ("act_out",))
    run_windows(windows, pieces, env)

    sums = [scatter_r.parts[0][0], *scatter_r.inbox]
    grad_rows = grad_call(env["rows_b"], env["rows_u"], norm_gain, env["scale"], env["tilt"], sums)
    grad_out = place_call(env["select_b_there"], shifted(grad_rows, -1), env["grad_base"])
    return (env["act_out"][None], grad_out[None])


def solution(mesh):
    in_specs = (
        P("section", "expert", None),
        P("section", "expert", None),
        P("section", "expert", None),
        P("section", "expert", None),
        P("section", "expert", None),
        P("section", None, "expert"),
        P("section", None, "expert"),
        P("section", "expert", None),
        P("section", None, None),
        P("section", None),
    )
    out_specs = (P("section", "expert", None), P("section", "expert", None))
    return jax.shard_map(local, mesh=mesh, in_specs=in_specs, out_specs=out_specs, check_vma=False)
```

time: 398 us -> 191 us (0.48)
  waiting for transfers between devices: 234 us -> 67 us
  matrix products: 87.5 us -> 0 us
  Pallas kernels: 0 us -> 67.5 us
  starting transfers between devices: 4.47 us -> 52.7 us
  other arithmetic: 18.1 us -> 0.01 us
  local copies, waits for them, and re-layouts: 20.5 us -> 2.99 us
  blocking collectives: 17.3 us -> 0 us
  between operations: 15.5 us -> 1.06 us
    all_gather x3 -> x0, waiting for transfers between devices: 129 us -> none  [the longest x1 50.7 us: local(): gathered_f = lax.all_gather(send_f, 'expert', axis=0, tiled=True)]
    dot_general x10 -> x0, matrix products: 87.5 us -> none  [the longest x1 18.1 us: forward_part(): jnp.dot(active, down_rows, preferred_element_type=jnp.float32)]
    reduce_scatter x2 -> x0, waiting for transfers between devices: 85.6 us -> none  [the longest x1 66.3 us: local(): lax.psum_scatter(row_part.astype(jnp.float32).astype(jnp.bfloat16), 'expe...]
    pallas_call x0 -> x39, Pallas kernels: none -> 67.5 us  [the longest x1 11.3 us: back_call(): pl.pallas_call(functools.partial(back_kernel, widths_of(held)), in_specs=...]
    ppermute x2 -> x46, starting transfers between devices: 3.87 us -> 52.7 us  [the longest x40 30 us: hop(): lax.ppermute(value, 'expert', [(ring[i], ring[(i + steps) % count]) for i...]
    ppermute x2 -> x46, waiting for transfers between devices: 19.2 us -> 67 us  [the longest x40 60.5 us: hop(): lax.ppermute(value, 'expert', [(ring[i], ring[(i + steps) % count]) for i...]
    unnamed x1 -> x0, blocking collectives: 17.3 us -> none
    gather x7 -> x0, local copies, waits for them, and re-layouts: 14.9 us -> none  [the longest x3 7.58 us: unfill(): return jnp.take(padded, slot_of, axis=0)]
  transfers between devices with their start and end apart: 7 -> 46, of which waited for: 6 -> 25; matrix products, arithmetic and copies ran while one was open for 28% -> 0% of each run, Pallas kernels for 0% -> 33%
where the time goes in v3:
time: 191 us
  Pallas kernels  67.5 us (35%)
  waiting for transfers between devices  67 us (35%)
  starting transfers between devices  52.7 us (28%)
  local copies, waits for them, and re-layouts  2.99 us (2%)
    ppermute x40, waiting for transfers between devices, hop(): lax.ppermute(value, 'expert', [(ring[i], ring[(i + steps) % count]) for i...  60.5 us
    ppermute x40, starting transfers between devices, hop(): lax.ppermute(value, 'expert', [(ring[i], ring[(i + steps) % count]) for i...  30 us
    ppermute x6, starting transfers between devices, shifted(): lax.ppermute(value, 'section', [(source, (source + steps) % count) for so...  22.6 us
    pallas_call x1, Pallas kernels, back_call(): pl.pallas_call(functools.partial(back_kernel, widths_of(held)), in_specs=...  11.3 us
    pallas_call x1, Pallas kernels, rowpart_call(): pl.pallas_call(functools.partial(rowpart_kernel, held), in_specs=[in_vmem...  10.4 us
    pallas_call x2, Pallas kernels, load_call(): pl.pallas_call(load_kernel, in_specs=[anywhere, in_hbm], out_specs=[in_vm...  9.37 us
    pallas_call x1, Pallas kernels, cots_call(): pl.pallas_call(functools.partial(cots_kernel, widths_of(held)), in_specs=...  8.56 us
    pallas_call x1, Pallas kernels, active_call(): pl.pallas_call(functools.partial(active_kernel, widths_of(held)), in_spec...  8.17 us
  transfers between devices with their start and end apart: 46, of which 25 were waited for; matrix products, arithmetic and copies ran while one was open for 0% of the time, Pallas kernels for 33%

profile of v3, /device:TPU:1, one launch (start us, length us, event | category | flops | bytes accessed | tf_op | source)
XLA Modules:
  0.0 191.2 jit_solution(460968151854089374)
XLA Ops:
  6.8 8.3 %collective-permute-done.refs_0_ = bf16[32,6144]{1,0:T(8,128)(2,1)S(1)} collective-permute-done((bf16[32,6144]{1,0:T(8,128)(2,1)S(1)}, bf16[32,6144]{1,0:T(8,128)(2,1)S(1)}, u32[]{:S(2)}, u32[]{:S(2)}) %collective-permute-start) | collective-permute-done | bytes 393248 | tf_op jit(solution)/shard_map/window_0/ppermute | solution.py:44
  18.5 4.7 %shard_map.118 = (bf16[6144,1024]{1,0:T(8,128)(2,1)S(1)}, f32[8,128]{1,0:T(8,128)S(1)}) custom-call(bf16[32,128]{1,0:T(8,128)(2,1)S(1)} %get-tuple-element.127.after_ref.refs_4_, bf16[6144,1024]{1,0:T(8,128)(2,1)} %bitcast.35), custom_call_target="tpu_custom_call" | custom-call | bytes 25165824 | tf_op jit(solution)/shard_map/pallas_call | solution.py:223
  27.2 4.7 %shard_map.120 = (bf16[6144,1024]{1,0:T(8,128)(2,1)S(1)}, f32[8,128]{1,0:T(8,128)S(1)}) custom-call(bf16[32,128]{1,0:T(8,128)(2,1)S(1)} %get-tuple-element.132.after_ref.refs_2_, bf16[6144,1024]{1,0:T(8,128)(2,1)} %bitcast.33), custom_call_target="tpu_custom_call" | custom-call | bytes 25165824 | tf_op jit(solution)/shard_map/pallas_call | solution.py:223
  35.9 5.9 %collective-permute-start.24 = (bf16[128,6144]{1,0:T(8,128)(2,1)S(1)}, bf16[128,6144]{1,0:T(8,128)(2,1)S(1)}, u32[]{:S(2)}, u32[]{:S(2)}) collective-permute-start(bf16[128,6144]{1,0:T(8,128)(2,1)S(1)} %bitcast.21), channel_id=1, source_target_pairs={{0,8},{8,16},{16,24},{24,0},{1,9},{9,17},{17,25},{25,1},{2,10},{10... | collective-permute-start | bytes 4718600 | tf_op jit(solution)/shard_map/ppermute | solution.py:49
  45.0 8.2 %shard_map.123.refs_2_ = bf16[256,1024]{1,0:T(8,128)(2,1)S(1)} custom-call(bf16[32,6144]{1,0:T(8,128)(2,1)S(1)} %get-tuple-element.122.refs_0_, bf16[32,6144]{1,0:T(8,128)(2,1)S(1)} %get-tuple-element.126.refs_1_, bf16[32,6144]{1,0:T(8,128)(2,1)S(1)} %get-tuple-element.131.refs_2_, bf16[32,6144]{1,0:T(8,128)(2,1)S(1)} %get-tuple-element.135.refs_3_, ...), custom_call_target="tpu_custom_call" | custom-call | flops 6442450944 | bytes 28311552 | tf_op jit(solution)/shard_map/pallas_call | solution.py:304
  56.1 7.8 %shard_map.125 = (bf16[32,6144]{1,0:T(8,128)(2,1)S(1)}, bf16[32,6144]{1,0:T(8,128)(2,1)S(1)}, bf16[32,6144]{1,0:T(8,128)(2,1)S(1)}, bf16[32,6144]{1,0:T(8,128)(2...) custom-call(bf16[256,1024]{1,0:T(8,128)(2,1)S(1)} %get-tuple-element, ...), custom_call_target="tpu_custom_call" | custom-call | flops 3221225472 | bytes 12582912 | tf_op jit(solution)/shard_map/pallas_call | solution.py:405
  65.5 3.7 %collective-permute-done.16.refs_0_ = bf16[32,6144]{1,0:T(8,128)(2,1)S(1)} collective-permute-done((bf16[32,6144]{1,0:T(8,128)(2,1)S(1)}, bf16[32,6144]{1,0:T(8,128)(2,1)S(1)}, u32[]{:S(2)}, u32[]{:S(2)}) %collective-permute-start.16) | collective-permute-done | bytes 393248 | tf_op jit(solution)/shard_map/window_5/ppermute | solution.py:44
  69.2 2.3 %collective-permute-done.17.refs_1_ = bf16[32,6144]{1,0:T(8,128)(2,1)S(1)} collective-permute-done((bf16[32,6144]{1,0:T(8,128)(2,1)S(1)}, bf16[32,6144]{1,0:T(8,128)(2,1)S(1)}, u32[]{:S(2)}, u32[]{:S(2)}) %collective-permute-start.17) | collective-permute-done | bytes 393248 | tf_op jit(solution)/shard_map/window_5/ppermute | solution.py:44
  72.9 4.6 %collective-permute-done.12.refs_0_ = bf16[32,6144]{1,0:T(8,128)(2,1)S(1)} collective-permute-done((bf16[32,6144]{1,0:T(8,128)(2,1)S(1)}, bf16[32,6144]{1,0:T(8,128)(2,1)S(1)}, u32[]{:S(2)}, u32[]{:S(2)}) %collective-permute-start.12) | collective-permute-done | bytes 393248 | tf_op jit(solution)/shard_map/window_6/ppermute | solution.py:44
  77.5 2.4 %collective-permute-done.13.refs_1_ = bf16[32,6144]{1,0:T(8,128)(2,1)S(1)} collective-permute-done((bf16[32,6144]{1,0:T(8,128)(2,1)S(1)}, bf16[32,6144]{1,0:T(8,128)(2,1)S(1)}, u32[]{:S(2)}, u32[]{:S(2)}) %collective-permute-start.13) | collective-permute-done | bytes 393248 | tf_op jit(solution)/shard_map/window_6/ppermute | solution.py:44
  81.4 4.6 %collective-permute-done.18.refs_0_ = bf16[32,6144]{1,0:T(8,128)(2,1)S(1)} collective-permute-done((bf16[32,6144]{1,0:T(8,128)(2,1)S(1)}, bf16[32,6144]{1,0:T(8,128)(2,1)S(1)}, u32[]{:S(2)}, u32[]{:S(2)}) %collective-permute-start.18) | collective-permute-done | bytes 393248 | tf_op jit(solution)/shard_map/window_7/ppermute | solution.py:44
  85.9 2.4 %collective-permute-done.19.refs_1_ = bf16[32,6144]{1,0:T(8,128)(2,1)S(1)} collective-permute-done((bf16[32,6144]{1,0:T(8,128)(2,1)S(1)}, bf16[32,6144]{1,0:T(8,128)(2,1)S(1)}, u32[]{:S(2)}, u32[]{:S(2)}) %collective-permute-start.19) | collective-permute-done | bytes 393248 | tf_op jit(solution)/shard_map/window_7/ppermute | solution.py:44
  90.5 3.9 %collective-permute-done.14.refs_0_ = bf16[32,6144]{1,0:T(8,128)(2,1)S(1)} collective-permute-done((bf16[32,6144]{1,0:T(8,128)(2,1)S(1)}, bf16[32,6144]{1,0:T(8,128)(2,1)S(1)}, u32[]{:S(2)}, u32[]{:S(2)}) %collective-permute-start.14) | collective-permute-done | bytes 393248 | tf_op jit(solution)/shard_map/window_8/ppermute | solution.py:44
  94.4 2.4 %collective-permute-done.15.refs_1_ = bf16[32,6144]{1,0:T(8,128)(2,1)S(1)} collective-permute-done((bf16[32,6144]{1,0:T(8,128)(2,1)S(1)}, bf16[32,6144]{1,0:T(8,128)(2,1)S(1)}, u32[]{:S(2)}, u32[]{:S(2)}) %collective-permute-start.15) | collective-permute-done | bytes 393248 | tf_op jit(solution)/shard_map/window_8/ppermute | solution.py:44
  98.6 2.4 %collective-permute-done.21.refs_3_ = bf16[32,3072]{1,0:T(8,128)(2,1)S(1)} collective-permute-done((bf16[32,3072]{1,0:T(8,128)(2,1)S(1)}, bf16[32,3072]{1,0:T(8,128)(2,1)S(1)}, u32[]{:S(2)}, u32[]{:S(2)}) %collective-permute-start.21) | collective-permute-done | bytes 196640 | tf_op jit(solution)/shard_map/window_9/ppermute | solution.py:44
  108.7 11.3 %shard_map.131.refs_4_ = f32[256,1024]{1,0:T(8,128)S(1)} custom-call(bf16[32,6144]{1,0:T(8,128)(2,1)S(1)} %get-tuple-element.134.refs_0_, bf16[32,6144]{1,0:T(8,128)(2,1)S(1)} %get-tuple-element.151.refs_1_, bf16[32,6144]{1,0:T(8,128)(2,1)S(1)} %get-tuple-element.153.refs_2_, bf16[32,6144]{1,0:T(8,128)(2,1)S(1)} %get-tuple-element.157.refs_3_, ...), custom_call_target="tpu_custom_call" | custom-call | flops 3221225472 | bytes 15728640 | tf_op jit(solution)/shard_map/pallas_call | solution.py:254
  121.7 8.6 %shard_map.133 = (bf16[256,1024]{1,0:T(8,128)(2,1)S(1)}, bf16[256,1024]{1,0:T(8,128)(2,1)S(1)}, f32[256,128]{1,0:T(8,128)S(1)}) custom-call(bf16[32,6144]{1,0:T(8,128)(2,1)S(1)} %get-tuple-element.144.refs_0_, bf16[32,6144]{1,0:T(8,128)(2,1)S(1)} %get-tuple-element.147.refs_1_, bf16[32,6144]{1,0:T(8,128)(2,1)S(1)} %get-tuple-element.149.refs_2_, ...), custom_call_target="tpu_custom_call" | custom-call | flops 6442450944 | bytes 28311552 | tf_op jit(solution)/shard_map/pallas_call | solution.py:331
  132.1 10.4 %shard_map.135 = (bf16[32,6272]{1,0:T(8,128)(2,1)S(1)}, bf16[32,6272]{1,0:T(8,128)(2,1)S(1)}, bf16[32,6272]{1,0:T(8,128)(2,1)S(1)}, bf16[32,6272]{1,0:T(8,128)(2...) custom-call(bf16[256,1024]{1,0:T(8,128)(2,1)S(1)} %get-tuple-element, ...), custom_call_target="tpu_custom_call" | custom-call | flops 6442450944 | bytes 25165824 | tf_op jit(solution)/shard_map/pallas_call | solution.py:436
  145.2 2.7 %collective-permute-done.34.refs_0_ = bf16[32,3072]{1,0:T(8,128)(2,1)S(1)} collective-permute-done((bf16[32,3072]{1,0:T(8,128)(2,1)S(1)}, bf16[32,3072]{1,0:T(8,128)(2,1)S(1)}, u32[]{:S(2)}, u32[]{:S(2)}) %collective-permute-start.34) | collective-permute-done | bytes 196640 | tf_op jit(solution)/shard_map/window_13/ppermute | solution.py:44
  149.5 6.3 %collective-permute-start.40 = (bf16[32,128]{1,0:T(8,128)(2,1)S(1)}, bf16[32,128]{1,0:T(8,128)(2,1)S(1)}, u32[]{:S(2)}, u32[]{:S(2)}) collective-permute-start(bf16[32,128]{1,0:T(8,128)(2,1)S(1)} %get-tuple-element.204.after_ref.refs_2_), channel_id=1, source_target_pairs={{0,8},{8,16},{16,24},{24,0},{1,9},{9,17},{17,25},{25,1},{2,10},{10... | collective-permute-start | bytes 24584 | tf_op jit(solution)/shard_map/ppermute | solution.py:49
  158.7 7.2 %collective-permute-start.41 = (bf16[32,6144]{1,0:T(8,128)(2,1)S(1)}, bf16[32,6144]{1,0:T(8,128)(2,1)S(1)}, u32[]{:S(2)}, u32[]{:S(2)}) collective-permute-start(bf16[32,6144]{1,0:T(8,128)(2,1)S(1)} %shard_map.141), channel_id=1, source_target_pairs={{0,8},{8,16},{16,24},{24,0},{1,9},{9,17},{17,25},{25,1},{2,10},{10... | collective-permute-start | bytes 1179656 | tf_op jit(solution)/shard_map/ppermute | solution.py:49
  165.9 3.0 %shard_map.140 = (f32[32,128]{1,0:T(8,128)S(1)}, f32[32,6144]{1,0:T(8,128)S(1)}) custom-call(bf16[32,128]{1,0:T(8,128)(2,1)S(1)} %get-tuple-element.216.after_ref, bf16[32,6144]{1,0:T(8,128)(2,1)S(1)} %get-tuple-element.217.rows_ref, f32[1,6144]{1,0:T(1,128)S(1)} %copy-done.6, f32[8,6144]{1,0:T(8,128)S(1)} %bitcast.25, s32[2,128]{1,0:T(2,128)S(1)} %bitcast.28), custom_call_target="tpu_custom_call" | custom-call | bytes 2359296 | tf_op jit(solution)/shard_map/pallas_call | solution.py:581
  172.4 7.8 %collective-permute-done.43.a_ref = bf16[32,6272]{1,0:T(8,128)(2,1)S(1)} collective-permute-done((bf16[32,6272]{1,0:T(8,128)(2,1)S(1)}, bf16[32,6272]{1,0:T(8,128)(2,1)S(1)}, u32[]{:S(2)}, u32[]{:S(2)}) %collective-permute-start.43) | collective-permute-done | bytes 401440 | tf_op jit(solution)/shard_map/window_16/ppermute | solution.py:44
  185.6 3.9 %collective-permute-done.42.select_ref = bf16[32,128]{1,0:T(8,128)(2,1)S(1)} collective-permute-done((bf16[32,128]{1,0:T(8,128)(2,1)S(1)}, bf16[32,128]{1,0:T(8,128)(2,1)S(1)}, u32[]{:S(2)}, u32[]{:S(2)}) %collective-permute-start.42) | collective-permute-done | bytes 8224 | tf_op jit(solution)/shard_map/ppermute | solution.py:49
  (146 shorter events, 61.0 us)
Async XLA Ops:
  35.9 54.0 %collective-permute-start.24 = (bf16[128,6144]{1,0:T(8,128)(2,1)S(1)}, bf16[128,6144]{1,0:T(8,128)(2,1)S(1)}, u32[]{:S(2)}, u32[]{:S(2)}) collective-permute-start(bf16[128,6144]{1,0:T(8,128)(2,1)S(1)} %bitcast.21), channel_id=1, source_target_pairs={{0,8},{8,16},{16,24},{24,0},{1,9},{9,17},{17,25},{25,1},{2,10},{10... | collective-permute-start | bytes 4718600 | tf_op jit(solution)/shard_map/ppermute | solution.py:49
  41.8 11.3 %collective-permute-start.6 = (bf16[32,6144]{1,0:T(8,128)(2,1)S(1)}, bf16[32,6144]{1,0:T(8,128)(2,1)S(1)}, u32[]{:S(2)}, u32[]{:S(2)}) collective-permute-start(bf16[32,6144]{1,0:T(8,128)(2,1)S(1)} %get-tuple-element.134.refs_0_), channel_id=1, source_target_pairs={{0,2},{2,4},{4,6},{6,7},{7,5},{5,3},{3,1},{1,0},{8,10},{10,12},{12... | collective-permute-start | bytes 1179656 | tf_op jit(solution)/shard_map/window_3/ppermute | solution.py:44
  43.4 20.5 %collective-permute-start.10 = (bf16[32,6144]{1,0:T(8,128)(2,1)S(1)}, bf16[32,6144]{1,0:T(8,128)(2,1)S(1)}, u32[]{:S(2)}, u32[]{:S(2)}) collective-permute-start(bf16[32,6144]{1,0:T(8,128)(2,1)S(1)} %get-tuple-element.144.refs_0_), channel_id=1, source_target_pairs={{0,2},{2,4},{4,6},{6,7},{7,5},{5,3},{3,1},{1,0},{8,10},{10,12},{12... | collective-permute-start | bytes 1179656 | tf_op jit(solution)/shard_map/window_4/ppermute | solution.py:44
  44.9 19.0 %collective-permute-start.11 = (bf16[32,6144]{1,0:T(8,128)(2,1)S(1)}, bf16[32,6144]{1,0:T(8,128)(2,1)S(1)}, u32[]{:S(2)}, u32[]{:S(2)}) collective-permute-start(bf16[32,6144]{1,0:T(8,128)(2,1)S(1)} %get-tuple-element.144.refs_0_), channel_id=1, source_target_pairs={{0,1},{2,0},{4,2},{6,4},{7,6},{5,7},{3,5},{1,3},{8,9},{10,8},{12,1... | collective-permute-start | bytes 1179656 | tf_op jit(solution)/shard_map/window_4/ppermute | solution.py:44
  54.6 14.6 %collective-permute-start.16 = (bf16[32,6144]{1,0:T(8,128)(2,1)S(1)}, bf16[32,6144]{1,0:T(8,128)(2,1)S(1)}, u32[]{:S(2)}, u32[]{:S(2)}) collective-permute-start(bf16[32,6144]{1,0:T(8,128)(2,1)S(1)} %get-tuple-element.150.refs_8_), channel_id=1, source_target_pairs={{0,2},{2,4},{4,6},{6,7},{7,5},{5,3},{3,1},{1,0},{8,10},{10,12},{12... | collective-permute-start | bytes 1179656 | tf_op jit(solution)/shard_map/window_5/ppermute | solution.py:44
  55.2 16.3 %collective-permute-start.17 = (bf16[32,6144]{1,0:T(8,128)(2,1)S(1)}, bf16[32,6144]{1,0:T(8,128)(2,1)S(1)}, u32[]{:S(2)}, u32[]{:S(2)}) collective-permute-start(bf16[32,6144]{1,0:T(8,128)(2,1)S(1)} %get-tuple-element.151.refs_1_), channel_id=1, source_target_pairs={{0,1},{2,0},{4,2},{6,4},{7,6},{5,7},{3,5},{1,3},{8,9},{10,8},{12,1... | collective-permute-start | bytes 1179656 | tf_op jit(solution)/shard_map/window_5/ppermute | solution.py:44
  64.0 13.5 %collective-permute-start.12 = (bf16[32,6144]{1,0:T(8,128)(2,1)S(1)}, bf16[32,6144]{1,0:T(8,128)(2,1)S(1)}, u32[]{:S(2)}, u32[]{:S(2)}) collective-permute-start(bf16[32,6144]{1,0:T(8,128)(2,1)S(1)} %get-tuple-element.146.refs_8_), channel_id=1, source_target_pairs={{0,2},{2,4},{4,6},{6,7},{7,5},{5,3},{3,1},{1,0},{8,10},{10,12},{12... | collective-permute-start | bytes 1179656 | tf_op jit(solution)/shard_map/window_6/ppermute | solution.py:44
  64.5 15.4 %collective-permute-start.13 = (bf16[32,6144]{1,0:T(8,128)(2,1)S(1)}, bf16[32,6144]{1,0:T(8,128)(2,1)S(1)}, u32[]{:S(2)}, u32[]{:S(2)}) collective-permute-start(bf16[32,6144]{1,0:T(8,128)(2,1)S(1)} %get-tuple-element.147.refs_1_), channel_id=1, source_target_pairs={{0,1},{2,0},{4,2},{6,4},{7,6},{5,7},{3,5},{1,3},{8,9},{10,8},{12,1... | collective-permute-start | bytes 1179656 | tf_op jit(solution)/shard_map/window_6/ppermute | solution.py:44
  71.5 14.4 %collective-permute-start.18 = (bf16[32,6144]{1,0:T(8,128)(2,1)S(1)}, bf16[32,6144]{1,0:T(8,128)(2,1)S(1)}, u32[]{:S(2)}, u32[]{:S(2)}) collective-permute-start(bf16[32,6144]{1,0:T(8,128)(2,1)S(1)} %get-tuple-element.152.refs_7_), channel_id=1, source_target_pairs={{0,2},{2,4},{4,6},{6,7},{7,5},{5,3},{3,1},{1,0},{8,10},{10,12},{12... | collective-permute-start | bytes 1179656 | tf_op jit(solution)/shard_map/window_7/ppermute | solution.py:44
  72.0 16.3 %collective-permute-start.19 = (bf16[32,6144]{1,0:T(8,128)(2,1)S(1)}, bf16[32,6144]{1,0:T(8,128)(2,1)S(1)}, u32[]{:S(2)}, u32[]{:S(2)}) collective-permute-start(bf16[32,6144]{1,0:T(8,128)(2,1)S(1)} %get-tuple-element.153.refs_2_), channel_id=1, source_target_pairs={{0,1},{2,0},{4,2},{6,4},{7,6},{5,7},{3,5},{1,3},{8,9},{10,8},{12,1... | collective-permute-start | bytes 1179656 | tf_op jit(solution)/shard_map/window_7/ppermute | solution.py:44
  79.9 14.4 %collective-permute-start.14 = (bf16[32,6144]{1,0:T(8,128)(2,1)S(1)}, bf16[32,6144]{1,0:T(8,128)(2,1)S(1)}, u32[]{:S(2)}, u32[]{:S(2)}) collective-permute-start(bf16[32,6144]{1,0:T(8,128)(2,1)S(1)} %get-tuple-element.148.refs_7_), channel_id=1, source_target_pairs={{0,2},{2,4},{4,6},{6,7},{7,5},{5,3},{3,1},{1,0},{8,10},{10,12},{12... | collective-permute-start | bytes 1179656 | tf_op jit(solution)/shard_map/window_8/ppermute | solution.py:44
  80.4 16.3 %collective-permute-start.15 = (bf16[32,6144]{1,0:T(8,128)(2,1)S(1)}, bf16[32,6144]{1,0:T(8,128)(2,1)S(1)}, u32[]{:S(2)}, u32[]{:S(2)}) collective-permute-start(bf16[32,6144]{1,0:T(8,128)(2,1)S(1)} %get-tuple-element.149.refs_2_), channel_id=1, source_target_pairs={{0,1},{2,0},{4,2},{6,4},{7,6},{5,7},{3,5},{1,3},{8,9},{10,8},{12,1... | collective-permute-start | bytes 1179656 | tf_op jit(solution)/shard_map/window_8/ppermute | solution.py:44
  89.0 12.0 %collective-permute-start.21 = (bf16[32,3072]{1,0:T(8,128)(2,1)S(1)}, bf16[32,3072]{1,0:T(8,128)(2,1)S(1)}, u32[]{:S(2)}, u32[]{:S(2)}) collective-permute-start(bf16[32,3072]{1,0:T(8,128)(2,1)S(1)} %slice.33), channel_id=1, source_target_pairs={{0,1},{2,0},{4,2},{6,4},{7,6},{5,7},{3,5},{1,3},{8,9},{10,8},{12,1... | collective-permute-start | bytes 589832 | tf_op jit(solution)/shard_map/window_9/ppermute | solution.py:44
  89.9 12.5 %collective-permute-start.22 = (bf16[32,3072]{1,0:T(8,128)(2,1)S(1)}, bf16[32,3072]{1,0:T(8,128)(2,1)S(1)}, u32[]{:S(2)}, u32[]{:S(2)}) collective-permute-start(bf16[32,3072]{1,0:T(8,128)(2,1)S(1)} %get-tuple-element.158), channel_id=1, source_target_pairs={{0,2},{2,4},{4,6},{6,7},{7,5},{5,3},{3,1},{1,0},{8,10},{10,12},{12... | collective-permute-start | bytes 589832 | tf_op jit(solution)/shard_map/window_9/ppermute | solution.py:44
  104.6 15.3 %collective-permute-start.27 = (bf16[32,6144]{1,0:T(8,128)(2,1)S(1)}, bf16[32,6144]{1,0:T(8,128)(2,1)S(1)}, u32[]{:S(2)}, u32[]{:S(2)}) collective-permute-start(bf16[32,6144]{1,0:T(8,128)(2,1)S(1)} %get-tuple-element.167), channel_id=1, source_target_pairs={{0,2},{2,4},{4,6},{6,7},{7,5},{5,3},{3,1},{1,0},{8,10},{10,12},{12... | collective-permute-start | bytes 1179656 | tf_op jit(solution)/shard_map/window_10/ppermute | solution.py:44
  105.3 14.7 %collective-permute-start.28 = (bf16[32,6144]{1,0:T(8,128)(2,1)S(1)}, bf16[32,6144]{1,0:T(8,128)(2,1)S(1)}, u32[]{:S(2)}, u32[]{:S(2)}) collective-permute-start(bf16[32,6144]{1,0:T(8,128)(2,1)S(1)} %get-tuple-element.168), channel_id=1, source_target_pairs={{0,1},{2,0},{4,2},{6,4},{7,6},{5,7},{3,5},{1,3},{8,9},{10,8},{12,1... | collective-permute-start | bytes 1179656 | tf_op jit(solution)/shard_map/window_10/ppermute | solution.py:44
  106.2 36.3 %collective-permute-start.33 = (bf16[128,6144]{1,0:T(8,128)(2,1)S(1)}, bf16[128,6144]{1,0:T(8,128)(2,1)S(1)}, u32[]{:S(2)}, u32[]{:S(2)}) collective-permute-start(bf16[128,6144]{1,0:T(8,128)(2,1)S(1)} %bitcast.23), channel_id=1, source_target_pairs={{0,24},{8,0},{16,8},{24,16},{1,25},{9,1},{17,9},{25,17},{2,26},{10... | collective-permute-start | bytes 4718600 | tf_op jit(solution)/shard_map/ppermute | solution.py:49
  107.1 12.9 %collective-permute-start.25 = (bf16[32,3072]{1,0:T(8,128)(2,1)S(1)}, bf16[32,3072]{1,0:T(8,128)(2,1)S(1)}, u32[]{:S(2)}, u32[]{:S(2)}) collective-permute-start(bf16[32,3072]{1,0:T(8,128)(2,1)S(1)} %slice.34), channel_id=1, source_target_pairs={{0,2},{2,4},{4,6},{6,7},{7,5},{5,3},{3,1},{1,0},{8,10},{10,12},{12... | collective-permute-start | bytes 589832 | tf_op jit(solution)/shard_map/window_10/ppermute | solution.py:44
  107.7 12.3 %collective-permute-start.26 = (bf16[32,3072]{1,0:T(8,128)(2,1)S(1)}, bf16[32,3072]{1,0:T(8,128)(2,1)S(1)}, u32[]{:S(2)}, u32[]{:S(2)}) collective-permute-start(bf16[32,3072]{1,0:T(8,128)(2,1)S(1)} %slice.35), channel_id=1, source_target_pairs={{0,1},{2,0},{4,2},{6,4},{7,6},{5,7},{3,5},{1,3},{8,9},{10,8},{12,1... | collective-permute-start | bytes 589832 | tf_op jit(solution)/shard_map/window_10/ppermute | solution.py:44
  130.5 12.0 %collective-permute-start.31 = (bf16[32,6144]{1,0:T(8,128)(2,1)S(1)}, bf16[32,6144]{1,0:T(8,128)(2,1)S(1)}, u32[]{:S(2)}, u32[]{:S(2)}) collective-permute-start(bf16[32,6144]{1,0:T(8,128)(2,1)S(1)} %get-tuple-element.185), channel_id=1, source_target_pairs={{0,2},{2,4},{4,6},{6,7},{7,5},{5,3},{3,1},{1,0},{8,10},{10,12},{12... | collective-permute-start | bytes 1179656 | tf_op jit(solution)/shard_map/window_12/ppermute | solution.py:44
  131.2 11.3 %collective-permute-start.32 = (bf16[32,6144]{1,0:T(8,128)(2,1)S(1)}, bf16[32,6144]{1,0:T(8,128)(2,1)S(1)}, u32[]{:S(2)}, u32[]{:S(2)}) collective-permute-start(bf16[32,6144]{1,0:T(8,128)(2,1)S(1)} %get-tuple-element.186), channel_id=1, source_target_pairs={{0,1},{2,0},{4,2},{6,4},{7,6},{5,7},{3,5},{1,3},{8,9},{10,8},{12,1... | collective-permute-start | bytes 1179656 | tf_op jit(solution)/shard_map/window_12/ppermute | solution.py:44
  156.8 13.9 %collective-permute-start.38 = (bf16[32,6272]{1,0:T(8,128)(2,1)S(1)}, bf16[32,6272]{1,0:T(8,128)(2,1)S(1)}, u32[]{:S(2)}, u32[]{:S(2)}) collective-permute-start(bf16[32,6272]{1,0:T(8,128)(2,1)S(1)} %get-tuple-element.214), channel_id=1, source_target_pairs={{0,2},{2,4},{4,6},{6,7},{7,5},{5,3},{3,1},{1,0},{8,10},{10,12},{12... | collective-permute-start | bytes 1204232 | tf_op jit(solution)/shard_map/window_15/ppermute | solution.py:44
  157.4 13.3 %collective-permute-start.39 = (bf16[32,6272]{1,0:T(8,128)(2,1)S(1)}, bf16[32,6272]{1,0:T(8,128)(2,1)S(1)}, u32[]{:S(2)}, u32[]{:S(2)}) collective-permute-start(bf16[32,6272]{1,0:T(8,128)(2,1)S(1)} %get-tuple-element.215), channel_id=1, source_target_pairs={{0,1},{2,0},{4,2},{6,4},{7,6},{5,7},{3,5},{1,3},{8,9},{10,8},{12,1... | collective-permute-start | bytes 1204232 | tf_op jit(solution)/shard_map/window_15/ppermute | solution.py:44
  158.7 11.9 %collective-permute-start.41 = (bf16[32,6144]{1,0:T(8,128)(2,1)S(1)}, bf16[32,6144]{1,0:T(8,128)(2,1)S(1)}, u32[]{:S(2)}, u32[]{:S(2)}) collective-permute-start(bf16[32,6144]{1,0:T(8,128)(2,1)S(1)} %shard_map.141), channel_id=1, source_target_pairs={{0,8},{8,16},{16,24},{24,0},{1,9},{9,17},{17,25},{25,1},{2,10},{10... | collective-permute-start | bytes 1179656 | tf_op jit(solution)/shard_map/ppermute | solution.py:49
  (36 other events, 296.0 us)

commit v4 on v3

--- a/solution.py
+++ b/solution.py
@@ -233,49 +233,47 @@
 
 def back_kernel(held_shape, *refs):
     count = sum(len(widths) for widths in held_shape)
-    shards, (down_ref, out_ref, rows_ref, weight_ref, row_sems, sems) = refs[:count], refs[count:]
+    shards, (down_ref, out_ref, rows_ref, row_sems) = refs[:count], refs[count:]
     parts = pieces_of(out_ref.shape[1], 4, 128)
     rows = row_copies(held_shape, shards, rows_ref, row_sems)
-    downs = [
-        pltpu.make_async_copy(down_ref.at[part], weight_ref.at[part], sems.at[k])
-        for k, part in enumerate(parts)
-    ]
     start_all(rows)
-    start_all(downs)
     for copy in rows:
         copy.wait()
-    for part, copy in zip(parts, downs, strict=True):
-        copy.wait()
-        out_ref[:, part] = dot_t(rows_ref[...], weight_ref[part, :])
+    for part in parts:
+        out_ref[:, part] = dot_t(rows_ref[...], down_ref[part, :])
 
 
 def back_call(held, down):
     count, side, width, hid = len(held), held[0][0].shape[0], sum(widths_of(held)[0]), down.shape[0]
     return pl.pallas_call(
         functools.partial(back_kernel, widths_of(held)),
-        in_specs=[anywhere] * len(flat(held)) + [in_hbm],
+        in_specs=[anywhere] * len(flat(held)) + [in_vmem],
         out_specs=in_vmem,
         out_shape=shape_of(count * side, hid, f32),
         scratch_shapes=[
             pltpu.VMEM((count * side, width), bf16),
-            pltpu.VMEM((hid, width), bf16),
             pltpu.SemaphoreType.DMA((len(flat(held)),)),
-            pltpu.SemaphoreType.DMA((4,)),
         ],
-        compiler_params=params(22),
+        compiler_params=params(8),
         cost_estimate=cost(2 * count * side * width * hid, 2 * width * (hid + count * side)),
     )(*flat(held), down)
 
 
-def gate_up(held_shape, shards, gate_ref, up_ref, rows_ref, gate_sum, up_sum, row_sems):
+def gate_up(held_shape, shards, gate_ref, up_ref, rows_ref, gate_sum, up_sum, up_w, row_sems, up_sems):
+    parts = pieces_of(gate_ref.shape[0], 6, 128)
     rows = row_copies(held_shape, shards, rows_ref, row_sems)
+    ups = [pltpu.make_async_copy(up_ref.at[part], up_w.at[part], up_sems.at[k]) for k, part in enumerate(parts)]
     start_all(rows)
+    start_all(ups)
     for copy in rows:
         copy.wait()
-    for k, part in enumerate(pieces_of(gate_ref.shape[0], 6, 128)):
-        for weight, total in ((gate_ref, gate_sum), (up_ref, up_sum)):
-            product = dot_n(rows_ref[:, part], weight[part, :])
-            total[...] = product if k == 0 else total[...] + product
+    for k, part in enumerate(parts):
+        product = dot_n(rows_ref[:, part], gate_ref[part, :])
+        gate_sum[...] = product if k == 0 else gate_sum[...] + product
+    for k, part in enumerate(parts):
+        ups[k].wait()
+        product = dot_n(rows_ref[:, part], up_w[part, :])
+        up_sum[...] = product if k == 0 else up_sum[...] + product
 
 
 def gate_up_scratch(copies, count, side, width, hid):
@@ -283,7 +281,9 @@
         pltpu.VMEM((count * side, width), bf16),
         pltpu.VMEM((count * side, hid), f32),
         pltpu.VMEM((count * side, hid), f32),
+        pltpu.VMEM((width, hid), bf16),
         pltpu.SemaphoreType.DMA((copies,)),
+        pltpu.SemaphoreType.DMA((6,)),
     ]
 
 
@@ -303,11 +303,11 @@
     count, side, width, hid = len(held), held[0][0].shape[0], sum(widths_of(held)[0]), gate.shape[1]
     return pl.pallas_call(
         functools.partial(active_kernel, widths_of(held)),
-        in_specs=[anywhere] * len(flat(held)) + [in_vmem] * 2,
+        in_specs=[anywhere] * len(flat(held)) + [in_vmem, in_hbm],
         out_specs=in_vmem,
         out_shape=shape_of(count * side, hid),
         scratch_shapes=gate_up_scratch(len(flat(held)), count, side, width, hid),
-        compiler_params=params(12),
+        compiler_params=params(24),
         cost_estimate=gate_up_cost(count, side, width, hid),
     )(*flat(held), gate, up)
 
@@ -330,7 +330,7 @@
     count, side, width, hid = len(held), held[0][0].shape[0], sum(widths_of(held)[0]), gate.shape[1]
     return pl.pallas_call(
         functools.partial(cots_kernel, widths_of(held)),
-        in_specs=[anywhere] * len(flat(held)) + [in_vmem] * 3,
+        in_specs=[anywhere] * len(flat(held)) + [in_vmem, in_hbm, in_vmem],
         out_specs=[in_vmem] * 3,
         out_shape=[
             shape_of(count * side, hid),
@@ -338,7 +338,7 @@
             shape_of(count * side, 128, f32),
         ],
         scratch_shapes=gate_up_scratch(len(flat(held)), count, side, width, hid),
-        compiler_params=params(14),
+        compiler_params=params(26),
         cost_estimate=gate_up_cost(count, side, width, hid),
     )(*flat(held), gate, up, back)
 
@@ -384,16 +384,11 @@
 
 def outpart_kernel(held, active_ref, down_ref, *refs):
     number = sum(len(ranges) for ranges in held)
-    out_refs, made, (out_sems, down_w, sems) = refs[:number], refs[number : 2 * number], refs[2 * number :]
+    out_refs, made, (out_sems,) = refs[:number], refs[number : 2 * number], refs[2 * number :]
     width = down_ref.shape[1]
     parts = pieces_of(width, 6, 128)
-    downs = [
-        pltpu.make_async_copy(down_ref.at[:, part], down_w.at[:, part], sems.at[k]) for k, part in enumerate(parts)
-    ]
-    start_all(downs)
-    for part, copy in zip(parts, downs, strict=True):
-        copy.wait()
-        value = dot_n(active_ref[...], down_w[:, part])
+    for part in parts:
+        value = dot_n(active_ref[...], down_ref[:, part])
         spread(made, held, part.start, value.astype(bf16))
     send_out(made, out_refs, out_sems)
 
@@ -404,11 +399,11 @@
     shapes = part_shapes(rows // count, held)
     arrays = pl.pallas_call(
         functools.partial(outpart_kernel, held),
-        in_specs=[in_vmem, in_hbm],
+        in_specs=[in_vmem] * 2,
         out_specs=[anywhere] * len(shapes),
         out_shape=shapes,
-        scratch_shapes=made_scratch(shapes) + [pltpu.VMEM((hid, width), bf16), pltpu.SemaphoreType.DMA((6,))],
-        compiler_params=params(22),
+        scratch_shapes=made_scratch(shapes),
+        compiler_params=params(6),
         cost_estimate=cost(2 * rows * width * hid, 2 * width * hid),
     )(active, down)
     return regroup(held, arrays)
@@ -422,11 +417,13 @@
     ups = [pltpu.make_async_copy(up_ref.at[part], up_w.at[part], up_sems.at[k]) for k, part in enumerate(parts)]
     start_all(ups)
     spread(out_refs, held, width, slope_ref[...].astype(bf16))
-    for part, copy in zip(parts, ups, strict=True):
-        value = dot_t(gate_cot_ref[...], gate_ref[part, :])
-        copy.wait()
-        value = value + dot_t(up_cot_ref[...], up_w[part, :])
+    ahead = [dot_t(gate_cot_ref[...], gate_ref[part, :]) for part in parts[:2]]
+    for k, part in enumerate(parts):
+        ups[k].wait()
+        value = ahead.pop(0) + dot_t(up_cot_ref[...], up_w[part, :])
         spread(out_refs, held, part.start, value.astype(bf16))
+        if k + 2 < len(parts):
+            ahead.append(dot_t(gate_cot_ref[...], gate_ref[parts[k + 2], :]))
 
 
 def rowpart_call(count, gate_cot, up_cot, slope, gate, up):
@@ -462,39 +459,46 @@
     return dot_n(select.astype(bf16), values)
 
 
-def pick_kernel(after_ref, ids_ref, values_ref, select_ref, rows_ref):
+def front_kernel(after_ref, ids_hbm, values_hbm, gain_hbm, *refs):
+    select_ref, rows_ref, *normed_refs = refs[:-4]
+    ids_ref, values_ref, gain_ref, sems = refs[-4:]
+    copies = [
+        pltpu.make_async_copy(source, target, sems.at[k])
+        for k, (source, target) in enumerate(
+            ((ids_hbm, ids_ref), (values_hbm, values_ref), (gain_hbm, gain_ref))
+        )
+    ]
+    start_all(copies)
+    copies[0].wait()
     select = select_of(ids_ref[...])
     select_ref[...] = select.astype(bf16)
-    rows_ref[...] = pick(select, values_ref[...]).astype(bf16)
-
-
-def norm_kernel(after_ref, ids_ref, values_ref, gain_ref, select_ref, rows_ref, *normed_refs):
-    select = select_of(ids_ref[...])
-    select_ref[...] = select.astype(bf16)
+    copies[1].wait()
     rows = pick(select, values_ref[...])
     rows_ref[...] = rows.astype(bf16)
-    inverse = lax.rsqrt(jnp.mean(rows * rows, axis=1, keepdims=True) + epsilon)
-    normed = (rows * inverse * gain_ref[...]).astype(bf16)
-    first = 0
+    copies[2].wait()
     for normed_ref in normed_refs:
-        last = first + normed_ref.shape[1]
-        normed_ref[...] = normed[:, first:last]
-        first = last
-
-
-def front_call(after, ids, values, gain=None, cuts=0):
+        inverse = lax.rsqrt(jnp.mean(rows * rows, axis=1, keepdims=True) + epsilon)
+        normed_ref[...] = (rows * inverse * gain_ref[...]).astype(bf16)
+
+
+def front_call(after, ids, values, gain, normed):
     tokens, width = values.shape
     capacity = tokens // 4
-    more = [] if gain is None else [gain]
-    return pl.pallas_call(
-        pick_kernel if gain is None else norm_kernel,
-        in_specs=[anywhere] + [in_vmem] * (2 + len(more)),
-        out_specs=[in_vmem] * (2 + cuts),
-        out_shape=[shape_of(capacity, tokens), shape_of(capacity, width)]
-        + [shape_of(capacity, width // cuts) for _ in range(cuts)],
+    ids, values, gain = (pltpu.with_memory_space_constraint(array, pltpu.HBM) for array in (ids, values, gain))
+    return pl.pallas_call(
+        front_kernel,
+        in_specs=[anywhere] + [in_hbm] * 3,
+        out_specs=[in_vmem] * (2 + normed),
+        out_shape=[shape_of(capacity, tokens)] + [shape_of(capacity, width)] * (1 + normed),
+        scratch_shapes=[
+            pltpu.VMEM(ids.shape, ids.dtype),
+            pltpu.VMEM(values.shape, values.dtype),
+            pltpu.VMEM(gain.shape, gain.dtype),
+            pltpu.SemaphoreType.DMA((3,)),
+        ],
         compiler_params=params(8),
         cost_estimate=cost(0, 8 * values.size),
-    )(after, ids, values, *more)
+    )(after, ids, values, gain)
 
 
 def act_kernel(rows_ref, weight_ref, own_ref, a_ref, b_ref, out_ref):
@@ -603,7 +607,7 @@
     gather_f.begin(normed_f)
 
     def front_u(after):
-        env["select_b"], rows = front_call(after, bwd_ids, grad_in[0])
+        env["select_b"], rows = front_call(after, bwd_ids, grad_in[0], norm_gain, 0)
         env["rows_u"] = rows
         gather_u.begin(rows)
         return (rows[:16, :128],)
@@ -631,18 +635,18 @@
         return does
 
     def active(after):
-        return (active_call(gather_f.held, env["gate"], env["up"]),)
+        return (active_call(gather_f.held, env["gate"], up),)
 
     def outpart(active):
-        parts = outpart_call(count, active, down)
+        parts = outpart_call(count, active, env["down"])
         scatter_o.begin(parts)
         return (parts[0][0][:16, :128],)
 
     def back(after):
-        return (back_call(gather_u.held, down),)
+        return (back_call(gather_u.held, env["down"]),)
 
     def cots(back):
-        return cots_call(gather_h.held, env["gate"], env["up"], back)
+        return cots_call(gather_h.held, env["gate"], up, back)
 
     def rowpart(gate_cot, up_cot, slope):
         parts = rowpart_call(count, gate_cot, up_cot, slope, env["gate"], up)
@@ -655,19 +659,27 @@
         env["act_rows"] = shifted(rows, 1)
         return ()
 
-    def act_place(select, rows, base):
+    def act_place(select, rows, base, other):
         return (place_call(select, rows, base),)
 
     last = gather_u.steps - 1
-    windows = [[(gather_f, step, 1)] for step in range(last + 1)]
-    windows[-1].append((gather_u, 0, 2))
-    for step in range(1, last):
-        windows += [[(gather_h, step - 1, 2)], [(gather_u, step, 2)]]
-    windows += [[(gather_h, last - 1, 2)], [(gather_u, last, 1), (scatter_o, 0, 1)]]
-    windows += [[(gather_h, last, 1), (scatter_o, 1, 1)]]
-    windows += [[(scatter_o, step, 1)] for step in range(2, last + 1)]
-    windows += [[(scatter_r, step, 1)] for step in range(last + 1)]
-    start = {(ring, step): k for k, transfers in enumerate(windows) for ring, step, _ in transfers}
+    turns = []
+    for step in range(last):
+        turns += [(gather_f, step), (gather_u, step) if step + 1 < last else (gather_h, 0)]
+    turns += [(gather_f, last), (gather_u, last - 1), (gather_h, 1), (gather_u, last)]
+    turns += [(gather_h, step) for step in range(2, last)]
+    windows = [[turn] for turn in turns]
+    windows += [[(scatter_o, 0)], [(gather_h, last), (scatter_o, 1)]]
+    windows += [[(scatter_o, step)] for step in range(2, last + 1)]
+    windows += [[(scatter_r, step)] for step in range(last + 1)]
+    start = {turn: k for k, turns in enumerate(windows) for turn in turns}
+
+    def stay(ring, step):
+        return min(2, start.get((ring, step + 1), start[ring, step] + 2) - start[ring, step])
+
+    windows = [[(ring, step, stay(ring, step)) for ring, step in turns] for turns in windows]
+    windows[start[gather_h, last]] = [(gather_h, last, 1), (scatter_o, 1, 1)]
+    windows[start[scatter_o, last]] = [(scatter_o, last, 1)]
     pieces = {}
 
     def put(window, needs, does, gives):
@@ -676,25 +688,25 @@
     def nothing(*arrays):
         return ()
 
-    f_done = start[gather_f, last] + 1
+    f_done = start[gather_f, last] + 2
     h_done = start[gather_h, last] + 1
     out = start[scatter_o, last]
     put(0, ("select_f",), front_u, ("corner_u",))
     put(1, ("select_f",), front_b, ("corner_b",))
-    put(1, ("select_f",), load("gate", gate), ("flag_g",))
-    put(2, ("select_f",), load("up", up), ("flag_u",))
+    put(2, ("select_f",), load("gate", gate), ("flag_g",))
+    put(3, ("select_f",), load("down", down), ("flag_d",))
     put(f_done, ("select_f",), active, ("active",))
     put(f_done + 1, ("active",), outpart, ("corner_o",))
-    put(h_done-1, ("act_base",), nothing, ())
+    put(h_done-3, ("act_base",), nothing, ())
     put(out+1, ("grad_base",), nothing, ())
-    put(out+1, ("select_f",), shifts, ())
-    put(h_done - 1, ("select_f",), back, ("back",))
+    put(h_done - 2, ("select_f",), back, ("back",))
     put(h_done, ("back",), cots, ("gate_cot", "up_cot", "slope"))
     put(h_done + 1, ("gate_cot", "up_cot", "slope"), rowpart, ())
+    put(out + 1, ("select_f",), shifts, ())
     put(out + 1, ("select_f",), route_f, ("weight_f",))
     put(out + 2, ("weight_f",), act_rows, ())
     put(out + 3, ("select_f",), route_b, ("scale", "tilt"))
-    put(out + 4, ("select_f_there", "act_rows", "act_base"), act_place, ("act_out",))
+    put(out + 4, ("select_f_there", "act_rows", "act_base", "select_b_there"), act_place, ("act_out",))
     run_windows(windows, pieces, env)
 
     sums = [scatter_r.parts[0][0], *scatter_r.inbox]

time: 191 us -> 185 us (0.969)
  waiting for transfers between devices: 67 us -> 59.5 us
  starting transfers between devices: 52.7 us -> 59.9 us
  Pallas kernels: 67.5 us -> 63.9 us
  local copies, waits for them, and re-layouts: 2.99 us -> 0.15 us
    ppermute x40, waiting for transfers between devices: 60.5 us -> 53.2 us  [hop(): lax.ppermute(value, 'expert', [(ring[i], ring[(i + steps) % count]) for i...]
    ppermute x6, starting transfers between devices: 22.6 us -> 29.1 us  [shifted(): lax.ppermute(value, 'section', [(source, (source + steps) % count) for so...]
    pallas_call x1, Pallas kernels: 11.3 us -> 4.96 us  [back_call(): pl.pallas_call(functools.partial(back_kernel, widths_of(held)), in_specs=...]
    pallas_call x3, Pallas kernels: 2.17 us -> 6.31 us  [front_call(): pl.pallas_call(front_kernel, in_specs=[anywhere] + [in_hbm] * 3, out_spec...]
    unnamed x29 -> x13, local copies, waits for them, and re-layouts: 2.9 us -> 0.06 us
    pallas_call x1, Pallas kernels: 7.81 us -> 5.32 us  [outpart_call(): pl.pallas_call(functools.partial(outpart_kernel, held), in_specs=[in_vmem...]
  transfers between devices with their start and end apart: 46 -> 46, of which waited for: 25 -> 24; matrix products, arithmetic and copies ran while one was open for 0% -> 0% of each run, Pallas kernels for 33% -> 32%
where the time goes in v4:
time: 185 us
  Pallas kernels  63.9 us (35%)
  starting transfers between devices  59.9 us (32%)
  waiting for transfers between devices  59.5 us (32%)
    ppermute x40, waiting for transfers between devices, hop(): lax.ppermute(value, 'expert', [(ring[i], ring[(i + steps) % count]) for i...  53.2 us
    ppermute x40, starting transfers between devices, hop(): lax.ppermute(value, 'expert', [(ring[i], ring[(i + steps) % count]) for i...  30.8 us
    ppermute x6, starting transfers between devices, shifted(): lax.ppermute(value, 'section', [(source, (source + steps) % count) for so...  29.1 us
    pallas_call x1, Pallas kernels, rowpart_call(): pl.pallas_call(functools.partial(rowpart_kernel, held), in_specs=[in_vmem...  10.4 us
    pallas_call x2, Pallas kernels, load_call(): pl.pallas_call(load_kernel, in_specs=[anywhere, in_hbm], out_specs=[in_vm...  9.48 us
    pallas_call x1, Pallas kernels, cots_call(): pl.pallas_call(functools.partial(cots_kernel, widths_of(held)), in_specs=...  9.08 us
    pallas_call x1, Pallas kernels, active_call(): pl.pallas_call(functools.partial(active_kernel, widths_of(held)), in_spec...  8.67 us
    pallas_call x3, Pallas kernels, front_call(): pl.pallas_call(front_kernel, in_specs=[anywhere] + [in_hbm] * 3, out_spec...  6.31 us
  transfers between devices with their start and end apart: 46, of which 24 were waited for; matrix products, arithmetic and copies ran while one was open for 0% of the time, Pallas kernels for 32%

profile of v4, /device:TPU:1, one launch (start us, length us, event | category | flops | bytes accessed | tf_op | source)
XLA Modules:
  0.0 184.6 jit_solution(7861605292387816165)
XLA Ops:
  2.7 2.2 %collective-permute-start.2 = (bf16[32,6144]{1,0:T(8,128)(2,1)S(1)}, bf16[32,6144]{1,0:T(8,128)(2,1)S(1)}, u32[]{:S(2)}, u32[]{:S(2)}) collective-permute-start(bf16[32,6144]{1,0:T(8,128)(2,1)S(1)} %get-tuple-element.128.refs_0_), channel_id=1, source_target_pairs={{0,2},{2,4},{4,6},{6,7},{7,5},{5,3},{3,1},{1,0},{8,10},{10,12},{12... | collective-permute-start | bytes 1179656 | tf_op jit(solution)/shard_map/window_0/ppermute | solution.py:44
  8.3 2.4 %shard_map.117 = (bf16[32,128]{1,0:T(8,128)(2,1)}, bf16[32,6144]{1,0:T(8,128)(2,1)S(1)}, bf16[32,6144]{1,0:T(8,128)(2,1)S(1)}) custom-call(bf16[32,128]{1,0:T(8,128)(2,1)S(1)} %get-tuple-element.129.after_ref.refs_3_, s32[2,128]{1,0:T(2,128)} %bitcast.20, bf16[128,6144]{1,0:T(8,128)(2,1)} %bitcast.31, f32[1,6144]{1,0:T(1,128)} %gain_ref.5), custom_call_target="tpu_custom_call" | custom-call | bytes 6291456 | tf_op jit(solution)/shard_map/pallas_call | solution.py:488
  10.7 3.0 %collective-permute-done.2.refs_0_ = bf16[32,6144]{1,0:T(8,128)(2,1)S(1)} collective-permute-done((bf16[32,6144]{1,0:T(8,128)(2,1)S(1)}, bf16[32,6144]{1,0:T(8,128)(2,1)S(1)}, u32[]{:S(2)}, u32[]{:S(2)}) %collective-permute-start.2) | collective-permute-done | bytes 393248 | tf_op jit(solution)/shard_map/window_0/ppermute | solution.py:44
  16.0 4.8 %shard_map.119 = (bf16[6144,1024]{1,0:T(8,128)(2,1)S(1)}, f32[8,128]{1,0:T(8,128)S(1)}) custom-call(bf16[32,128]{1,0:T(8,128)(2,1)S(1)} %get-tuple-element.131.after_ref.refs_3_, bf16[6144,1024]{1,0:T(8,128)(2,1)} %bitcast.27), custom_call_target="tpu_custom_call" | custom-call | bytes 25165824 | tf_op jit(solution)/shard_map/pallas_call | solution.py:223
  24.5 5.0 %collective-permute-start.18 = (bf16[128,6144]{1,0:T(8,128)(2,1)S(1)}, bf16[128,6144]{1,0:T(8,128)(2,1)S(1)}, u32[]{:S(2)}, u32[]{:S(2)}) collective-permute-start(bf16[128,6144]{1,0:T(8,128)(2,1)S(1)} %bitcast.33), channel_id=1, source_target_pairs={{0,8},{8,16},{16,24},{24,0},{1,9},{9,17},{17,25},{25,1},{2,10},{10... | collective-permute-start | bytes 4718600 | tf_op jit(solution)/shard_map/ppermute | solution.py:49
  29.5 4.7 %shard_map.122 = (bf16[1024,6144]{1,0:T(8,128)(2,1)S(1)}, f32[8,128]{1,0:T(8,128)S(1)}) custom-call(bf16[32,128]{1,0:T(8,128)(2,1)S(1)} %get-tuple-element.139.after_ref.refs_2_, bf16[1024,6144]{1,0:T(8,128)(2,1)} %bitcast.28), custom_call_target="tpu_custom_call" | custom-call | bytes 25165824 | tf_op jit(solution)/shard_map/pallas_call | solution.py:223
  35.7 3.3 %collective-permute-done.4.refs_0_ = bf16[32,6144]{1,0:T(8,128)(2,1)S(1)} collective-permute-done((bf16[32,6144]{1,0:T(8,128)(2,1)S(1)}, bf16[32,6144]{1,0:T(8,128)(2,1)S(1)}, u32[]{:S(2)}, u32[]{:S(2)}) %collective-permute-start.4) | collective-permute-done | bytes 393248 | tf_op jit(solution)/shard_map/window_3/ppermute | solution.py:44
  41.3 6.1 %collective-permute-done.10.refs_0_ = bf16[32,6144]{1,0:T(8,128)(2,1)S(1)} collective-permute-done((bf16[32,6144]{1,0:T(8,128)(2,1)S(1)}, bf16[32,6144]{1,0:T(8,128)(2,1)S(1)}, u32[]{:S(2)}, u32[]{:S(2)}) %collective-permute-start.10) | collective-permute-done | bytes 393248 | tf_op jit(solution)/shard_map/window_4/ppermute | solution.py:44
  49.9 5.9 %collective-permute-done.14.refs_0_ = bf16[32,6144]{1,0:T(8,128)(2,1)S(1)} collective-permute-done((bf16[32,6144]{1,0:T(8,128)(2,1)S(1)}, bf16[32,6144]{1,0:T(8,128)(2,1)S(1)}, u32[]{:S(2)}, u32[]{:S(2)}) %collective-permute-start.14) | collective-permute-done | bytes 393248 | tf_op jit(solution)/shard_map/window_5/ppermute | solution.py:44
  57.3 2.7 %collective-permute-done.12.refs_0_ = bf16[32,3072]{1,0:T(8,128)(2,1)S(1)} collective-permute-done((bf16[32,3072]{1,0:T(8,128)(2,1)S(1)}, bf16[32,3072]{1,0:T(8,128)(2,1)S(1)}, u32[]{:S(2)}, u32[]{:S(2)}) %collective-permute-start.12) | collective-permute-done | bytes 196640 | tf_op jit(solution)/shard_map/window_6/ppermute | solution.py:44
  61.5 8.7 %shard_map.126.refs_2_ = bf16[256,1024]{1,0:T(8,128)(2,1)S(1)} custom-call(bf16[32,6144]{1,0:T(8,128)(2,1)S(1)} %get-tuple-element.128.refs_0_, bf16[32,6144]{1,0:T(8,128)(2,1)S(1)} %get-tuple-element.137.refs_1_, bf16[32,6144]{1,0:T(8,128)(2,1)S(1)} %get-tuple-element.141.refs_2_, bf16[32,6144]{1,0:T(8,128)(2,1)S(1)} %get-tuple-element.143.refs_3_, ...), custom_call_target="tpu_custom_call" | custom-call | flops 6442450944 | bytes 28311552 | tf_op jit(solution)/shard_map/pallas_call | solution.py:304
  71.8 5.3 %shard_map.128 = (bf16[32,6144]{1,0:T(8,128)(2,1)S(1)}, bf16[32,6144]{1,0:T(8,128)(2,1)S(1)}, bf16[32,6144]{1,0:T(8,128)(2,1)S(1)}, bf16[32,6144]{1,0:T(8,128)(2...) custom-call(bf16[256,1024]{1,0:T(8,128)(2,1)S(1)} %get-tuple-element, ...), custom_call_target="tpu_custom_call" | custom-call | flops 3221225472 | bytes 12582912 | tf_op jit(solution)/shard_map/pallas_call | solution.py:400
  83.5 5.0 %shard_map.132.refs_4_ = f32[256,1024]{1,0:T(8,128)S(1)} custom-call(bf16[32,6144]{1,0:T(8,128)(2,1)S(1)} %get-tuple-element.127.refs_0_, bf16[32,6144]{1,0:T(8,128)(2,1)S(1)} %get-tuple-element.134.refs_1_, bf16[32,6144]{1,0:T(8,128)(2,1)S(1)} %get-tuple-element.136.refs_2_, bf16[32,6144]{1,0:T(8,128)(2,1)S(1)} %get-tuple-element.159.refs_3_, ...), custom_call_target="tpu_custom_call" | custom-call | flops 3221225472 | bytes 15728640 | tf_op jit(solution)/shard_map/pallas_call | solution.py:248
  88.4 3.7 %collective-permute-done.23.refs_2_ = bf16[32,3072]{1,0:T(8,128)(2,1)S(1)} collective-permute-done((bf16[32,3072]{1,0:T(8,128)(2,1)S(1)}, bf16[32,3072]{1,0:T(8,128)(2,1)S(1)}, u32[]{:S(2)}, u32[]{:S(2)}) %collective-permute-start.23) | collective-permute-done | bytes 196640 | tf_op jit(solution)/shard_map/window_11/ppermute | solution.py:44
  95.3 3.4 %collective-permute-start.33 = (bf16[128,6144]{1,0:T(8,128)(2,1)S(1)}, bf16[128,6144]{1,0:T(8,128)(2,1)S(1)}, u32[]{:S(2)}, u32[]{:S(2)}) collective-permute-start(bf16[128,6144]{1,0:T(8,128)(2,1)S(1)} %bitcast.35), channel_id=1, source_target_pairs={{0,24},{8,0},{16,8},{24,16},{1,25},{9,1},{17,9},{25,17},{2,26},{10... | collective-permute-start | bytes 4718600 | tf_op jit(solution)/shard_map/ppermute | solution.py:49
  100.3 5.5 %collective-permute-done.25.refs_0_ = bf16[32,3072]{1,0:T(8,128)(2,1)S(1)} collective-permute-done((bf16[32,3072]{1,0:T(8,128)(2,1)S(1)}, bf16[32,3072]{1,0:T(8,128)(2,1)S(1)}, u32[]{:S(2)}, u32[]{:S(2)}) %collective-permute-start.25) | collective-permute-done | bytes 196640 | tf_op jit(solution)/shard_map/window_12/ppermute | solution.py:44
  108.8 9.1 %shard_map.135 = (bf16[256,1024]{1,0:T(8,128)(2,1)S(1)}, bf16[256,1024]{1,0:T(8,128)(2,1)S(1)}, f32[256,128]{1,0:T(8,128)S(1)}) custom-call(bf16[32,6144]{1,0:T(8,128)(2,1)S(1)} %get-tuple-element.152.refs_0_, bf16[32,6144]{1,0:T(8,128)(2,1)S(1)} %get-tuple-element.154.refs_1_, bf16[32,6144]{1,0:T(8,128)(2,1)S(1)} %get-tuple-element.157.refs_2_, ...), custom_call_target="tpu_custom_call" | custom-call | flops 6442450944 | bytes 28311552 | tf_op jit(solution)/shard_map/pallas_call | solution.py:331
  119.6 10.4 %shard_map.137 = (bf16[32,6272]{1,0:T(8,128)(2,1)S(1)}, bf16[32,6272]{1,0:T(8,128)(2,1)S(1)}, bf16[32,6272]{1,0:T(8,128)(2,1)S(1)}, bf16[32,6272]{1,0:T(8,128)(2...) custom-call(bf16[256,1024]{1,0:T(8,128)(2,1)S(1)} %get-tuple-element, ...), custom_call_target="tpu_custom_call" | custom-call | flops 6442450944 | bytes 25165824 | tf_op jit(solution)/shard_map/pallas_call | solution.py:433
  132.7 2.1 %collective-permute-done.34.refs_0_ = bf16[32,3072]{1,0:T(8,128)(2,1)S(1)} collective-permute-done((bf16[32,3072]{1,0:T(8,128)(2,1)S(1)}, bf16[32,3072]{1,0:T(8,128)(2,1)S(1)}, u32[]{:S(2)}, u32[]{:S(2)}) %collective-permute-start.34) | collective-permute-done | bytes 196640 | tf_op jit(solution)/shard_map/window_15/ppermute | solution.py:44
  136.5 10.0 %collective-permute-start.40 = (bf16[32,128]{1,0:T(8,128)(2,1)S(1)}, bf16[32,128]{1,0:T(8,128)(2,1)S(1)}, u32[]{:S(2)}, u32[]{:S(2)}) collective-permute-start(bf16[32,128]{1,0:T(8,128)(2,1)S(1)} %get-tuple-element.209.after_ref.refs_2_), channel_id=1, source_target_pairs={{0,8},{8,16},{16,24},{24,0},{1,9},{9,17},{17,25},{25,1},{2,10},{10... | collective-permute-start | bytes 24584 | tf_op jit(solution)/shard_map/ppermute | solution.py:49
  149.4 9.0 %collective-permute-start.41 = (bf16[32,6144]{1,0:T(8,128)(2,1)S(1)}, bf16[32,6144]{1,0:T(8,128)(2,1)S(1)}, u32[]{:S(2)}, u32[]{:S(2)}) collective-permute-start(bf16[32,6144]{1,0:T(8,128)(2,1)S(1)} %shard_map.143), channel_id=1, source_target_pairs={{0,8},{8,16},{16,24},{24,0},{1,9},{9,17},{17,25},{25,1},{2,10},{10... | collective-permute-start | bytes 1179656 | tf_op jit(solution)/shard_map/ppermute | solution.py:49
  158.4 3.0 %shard_map.142 = (f32[32,128]{1,0:T(8,128)S(1)}, f32[32,6144]{1,0:T(8,128)S(1)}) custom-call(bf16[32,128]{1,0:T(8,128)(2,1)S(1)} %get-tuple-element.221.after_ref, bf16[32,6144]{1,0:T(8,128)(2,1)S(1)} %get-tuple-element.222.rows_ref, f32[1,6144]{1,0:T(1,128)S(1)} %copy-done, f32[8,6144]{1,0:T(8,128)S(1)} %bitcast.18, s32[2,128]{1,0:T(2,128)S(1)} %bitcast.21), custom_call_target="tpu_custom_call" | custom-call | bytes 2359296 | tf_op jit(solution)/shard_map/pallas_call | solution.py:585
  164.8 8.9 %collective-permute-done.43.a_ref = bf16[32,6272]{1,0:T(8,128)(2,1)S(1)} collective-permute-done((bf16[32,6272]{1,0:T(8,128)(2,1)S(1)}, bf16[32,6272]{1,0:T(8,128)(2,1)S(1)}, u32[]{:S(2)}, u32[]{:S(2)}) %collective-permute-start.43) | collective-permute-done | bytes 401440 | tf_op jit(solution)/shard_map/window_18/ppermute | solution.py:44
  179.0 3.7 %collective-permute-done.45.rows_ref = bf16[32,6144]{1,0:T(8,128)(2,1)S(1)} collective-permute-done((bf16[32,6144]{1,0:T(8,128)(2,1)S(1)}, bf16[32,6144]{1,0:T(8,128)(2,1)S(1)}, u32[]{:S(2)}, u32[]{:S(2)}) %collective-permute-start.45) | collective-permute-done | bytes 393248 | tf_op jit(solution)/shard_map/ppermute | solution.py:49
  (131 shorter events, 55.8 us)
Async XLA Ops:
  6.8 15.3 %collective-permute-start = (bf16[32,6144]{1,0:T(8,128)(2,1)S(1)}, bf16[32,6144]{1,0:T(8,128)(2,1)S(1)}, u32[]{:S(2)}, u32[]{:S(2)}) collective-permute-start(bf16[32,6144]{1,0:T(8,128)(2,1)S(1)} %get-tuple-element.127.refs_0_), channel_id=1, source_target_pairs={{0,2},{2,4},{4,6},{6,7},{7,5},{5,3},{3,1},{1,0},{8,10},{10,12},{12... | collective-permute-start | bytes 1179656 | tf_op jit(solution)/shard_map/window_1/ppermute | solution.py:44
  8.3 14.7 %collective-permute-start.1 = (bf16[32,6144]{1,0:T(8,128)(2,1)S(1)}, bf16[32,6144]{1,0:T(8,128)(2,1)S(1)}, u32[]{:S(2)}, u32[]{:S(2)}) collective-permute-start(bf16[32,6144]{1,0:T(8,128)(2,1)S(1)} %get-tuple-element.127.refs_0_), channel_id=1, source_target_pairs={{0,1},{2,0},{4,2},{6,4},{7,6},{5,7},{3,5},{1,3},{8,9},{10,8},{12,1... | collective-permute-start | bytes 1179656 | tf_op jit(solution)/shard_map/window_1/ppermute | solution.py:44
  14.6 19.6 %collective-permute-start.8 = (bf16[32,6144]{1,0:T(8,128)(2,1)S(1)}, bf16[32,6144]{1,0:T(8,128)(2,1)S(1)}, u32[]{:S(2)}, u32[]{:S(2)}) collective-permute-start(bf16[32,6144]{1,0:T(8,128)(2,1)S(1)} %get-tuple-element.138.refs_8_), channel_id=1, source_target_pairs={{0,2},{2,4},{4,6},{6,7},{7,5},{5,3},{3,1},{1,0},{8,10},{10,12},{12... | collective-permute-start | bytes 1179656 | tf_op jit(solution)/shard_map/window_2/ppermute | solution.py:44
  15.9 18.3 %collective-permute-start.9 = (bf16[32,6144]{1,0:T(8,128)(2,1)S(1)}, bf16[32,6144]{1,0:T(8,128)(2,1)S(1)}, u32[]{:S(2)}, u32[]{:S(2)}) collective-permute-start(bf16[32,6144]{1,0:T(8,128)(2,1)S(1)} %get-tuple-element.137.refs_1_), channel_id=1, source_target_pairs={{0,1},{2,0},{4,2},{6,4},{7,6},{5,7},{3,5},{1,3},{8,9},{10,8},{12,1... | collective-permute-start | bytes 1179656 | tf_op jit(solution)/shard_map/window_2/ppermute | solution.py:44
  23.0 16.0 %collective-permute-start.4 = (bf16[32,6144]{1,0:T(8,128)(2,1)S(1)}, bf16[32,6144]{1,0:T(8,128)(2,1)S(1)}, u32[]{:S(2)}, u32[]{:S(2)}) collective-permute-start(bf16[32,6144]{1,0:T(8,128)(2,1)S(1)} %get-tuple-element.133.refs_8_), channel_id=1, source_target_pairs={{0,2},{2,4},{4,6},{6,7},{7,5},{5,3},{3,1},{1,0},{8,10},{10,12},{12... | collective-permute-start | bytes 1179656 | tf_op jit(solution)/shard_map/window_3/ppermute | solution.py:44
  24.3 15.6 %collective-permute-start.5 = (bf16[32,6144]{1,0:T(8,128)(2,1)S(1)}, bf16[32,6144]{1,0:T(8,128)(2,1)S(1)}, u32[]{:S(2)}, u32[]{:S(2)}) collective-permute-start(bf16[32,6144]{1,0:T(8,128)(2,1)S(1)} %get-tuple-element.134.refs_1_), channel_id=1, source_target_pairs={{0,1},{2,0},{4,2},{6,4},{7,6},{5,7},{3,5},{1,3},{8,9},{10,8},{12,1... | collective-permute-start | bytes 1179656 | tf_op jit(solution)/shard_map/window_3/ppermute | solution.py:44
  24.5 53.3 %collective-permute-start.18 = (bf16[128,6144]{1,0:T(8,128)(2,1)S(1)}, bf16[128,6144]{1,0:T(8,128)(2,1)S(1)}, u32[]{:S(2)}, u32[]{:S(2)}) collective-permute-start(bf16[128,6144]{1,0:T(8,128)(2,1)S(1)} %bitcast.33), channel_id=1, source_target_pairs={{0,8},{8,16},{16,24},{24,0},{1,9},{9,17},{17,25},{25,1},{2,10},{10... | collective-permute-start | bytes 4718600 | tf_op jit(solution)/shard_map/ppermute | solution.py:49
  34.2 13.2 %collective-permute-start.10 = (bf16[32,6144]{1,0:T(8,128)(2,1)S(1)}, bf16[32,6144]{1,0:T(8,128)(2,1)S(1)}, u32[]{:S(2)}, u32[]{:S(2)}) collective-permute-start(bf16[32,6144]{1,0:T(8,128)(2,1)S(1)} %get-tuple-element.142.refs_7_), channel_id=1, source_target_pairs={{0,2},{2,4},{4,6},{6,7},{7,5},{5,3},{3,1},{1,0},{8,10},{10,12},{12... | collective-permute-start | bytes 1179656 | tf_op jit(solution)/shard_map/window_4/ppermute | solution.py:44
  35.5 12.8 %collective-permute-start.11 = (bf16[32,6144]{1,0:T(8,128)(2,1)S(1)}, bf16[32,6144]{1,0:T(8,128)(2,1)S(1)}, u32[]{:S(2)}, u32[]{:S(2)}) collective-permute-start(bf16[32,6144]{1,0:T(8,128)(2,1)S(1)} %get-tuple-element.141.refs_2_), channel_id=1, source_target_pairs={{0,1},{2,0},{4,2},{6,4},{7,6},{5,7},{3,5},{1,3},{8,9},{10,8},{12,1... | collective-permute-start | bytes 1179656 | tf_op jit(solution)/shard_map/window_4/ppermute | solution.py:44
  39.9 16.0 %collective-permute-start.14 = (bf16[32,6144]{1,0:T(8,128)(2,1)S(1)}, bf16[32,6144]{1,0:T(8,128)(2,1)S(1)}, u32[]{:S(2)}, u32[]{:S(2)}) collective-permute-start(bf16[32,6144]{1,0:T(8,128)(2,1)S(1)} %get-tuple-element.152.refs_0_), channel_id=1, source_target_pairs={{0,2},{2,4},{4,6},{6,7},{7,5},{5,3},{3,1},{1,0},{8,10},{10,12},{12... | collective-permute-start | bytes 1179656 | tf_op jit(solution)/shard_map/window_5/ppermute | solution.py:44
  41.2 15.9 %collective-permute-start.15 = (bf16[32,6144]{1,0:T(8,128)(2,1)S(1)}, bf16[32,6144]{1,0:T(8,128)(2,1)S(1)}, u32[]{:S(2)}, u32[]{:S(2)}) collective-permute-start(bf16[32,6144]{1,0:T(8,128)(2,1)S(1)} %get-tuple-element.152.refs_0_), channel_id=1, source_target_pairs={{0,1},{2,0},{4,2},{6,4},{7,6},{5,7},{3,5},{1,3},{8,9},{10,8},{12,1... | collective-permute-start | bytes 1179656 | tf_op jit(solution)/shard_map/window_5/ppermute | solution.py:44
  55.8 14.4 %collective-permute-start.6 = (bf16[32,6144]{1,0:T(8,128)(2,1)S(1)}, bf16[32,6144]{1,0:T(8,128)(2,1)S(1)}, u32[]{:S(2)}, u32[]{:S(2)}) collective-permute-start(bf16[32,6144]{1,0:T(8,128)(2,1)S(1)} %get-tuple-element.135.refs_7_), channel_id=1, source_target_pairs={{0,2},{2,4},{4,6},{6,7},{7,5},{5,3},{3,1},{1,0},{8,10},{10,12},{12... | collective-permute-start | bytes 1179656 | tf_op jit(solution)/shard_map/window_7/ppermute | solution.py:44
  57.0 13.2 %collective-permute-start.7 = (bf16[32,6144]{1,0:T(8,128)(2,1)S(1)}, bf16[32,6144]{1,0:T(8,128)(2,1)S(1)}, u32[]{:S(2)}, u32[]{:S(2)}) collective-permute-start(bf16[32,6144]{1,0:T(8,128)(2,1)S(1)} %get-tuple-element.136.refs_2_), channel_id=1, source_target_pairs={{0,1},{2,0},{4,2},{6,4},{7,6},{5,7},{3,5},{1,3},{8,9},{10,8},{12,1... | collective-permute-start | bytes 1179656 | tf_op jit(solution)/shard_map/window_7/ppermute | solution.py:44
  60.0 17.1 %collective-permute-start.16 = (bf16[32,6144]{1,0:T(8,128)(2,1)S(1)}, bf16[32,6144]{1,0:T(8,128)(2,1)S(1)}, u32[]{:S(2)}, u32[]{:S(2)}) collective-permute-start(bf16[32,6144]{1,0:T(8,128)(2,1)S(1)} %get-tuple-element.153.refs_8_), channel_id=1, source_target_pairs={{0,2},{2,4},{4,6},{6,7},{7,5},{5,3},{3,1},{1,0},{8,10},{10,12},{12... | collective-permute-start | bytes 1179656 | tf_op jit(solution)/shard_map/window_8/ppermute | solution.py:44
  61.2 16.5 %collective-permute-start.17 = (bf16[32,6144]{1,0:T(8,128)(2,1)S(1)}, bf16[32,6144]{1,0:T(8,128)(2,1)S(1)}, u32[]{:S(2)}, u32[]{:S(2)}) collective-permute-start(bf16[32,6144]{1,0:T(8,128)(2,1)S(1)} %get-tuple-element.154.refs_1_), channel_id=1, source_target_pairs={{0,1},{2,0},{4,2},{6,4},{7,6},{5,7},{3,5},{1,3},{8,9},{10,8},{12,1... | collective-permute-start | bytes 1179656 | tf_op jit(solution)/shard_map/window_8/ppermute | solution.py:44
  77.8 15.9 %collective-permute-start.19 = (bf16[32,6144]{1,0:T(8,128)(2,1)S(1)}, bf16[32,6144]{1,0:T(8,128)(2,1)S(1)}, u32[]{:S(2)}, u32[]{:S(2)}) collective-permute-start(bf16[32,6144]{1,0:T(8,128)(2,1)S(1)} %get-tuple-element.156.refs_7_), channel_id=1, source_target_pairs={{0,2},{2,4},{4,6},{6,7},{7,5},{5,3},{3,1},{1,0},{8,10},{10,12},{12... | collective-permute-start | bytes 1179656 | tf_op jit(solution)/shard_map/window_10/ppermute | solution.py:44
  79.1 14.6 %collective-permute-start.20 = (bf16[32,6144]{1,0:T(8,128)(2,1)S(1)}, bf16[32,6144]{1,0:T(8,128)(2,1)S(1)}, u32[]{:S(2)}, u32[]{:S(2)}) collective-permute-start(bf16[32,6144]{1,0:T(8,128)(2,1)S(1)} %get-tuple-element.157.refs_2_), channel_id=1, source_target_pairs={{0,1},{2,0},{4,2},{6,4},{7,6},{5,7},{3,5},{1,3},{8,9},{10,8},{12,1... | collective-permute-start | bytes 1179656 | tf_op jit(solution)/shard_map/window_10/ppermute | solution.py:44
  93.7 13.4 %collective-permute-start.27 = (bf16[32,6144]{1,0:T(8,128)(2,1)S(1)}, bf16[32,6144]{1,0:T(8,128)(2,1)S(1)}, u32[]{:S(2)}, u32[]{:S(2)}) collective-permute-start(bf16[32,6144]{1,0:T(8,128)(2,1)S(1)} %get-tuple-element.173), channel_id=1, source_target_pairs={{0,2},{2,4},{4,6},{6,7},{7,5},{5,3},{3,1},{1,0},{8,10},{10,12},{12... | collective-permute-start | bytes 1179656 | tf_op jit(solution)/shard_map/window_12/ppermute | solution.py:44
  95.1 12.0 %collective-permute-start.28 = (bf16[32,6144]{1,0:T(8,128)(2,1)S(1)}, bf16[32,6144]{1,0:T(8,128)(2,1)S(1)}, u32[]{:S(2)}, u32[]{:S(2)}) collective-permute-start(bf16[32,6144]{1,0:T(8,128)(2,1)S(1)} %get-tuple-element.174), channel_id=1, source_target_pairs={{0,1},{2,0},{4,2},{6,4},{7,6},{5,7},{3,5},{1,3},{8,9},{10,8},{12,1... | collective-permute-start | bytes 1179656 | tf_op jit(solution)/shard_map/window_12/ppermute | solution.py:44
  95.3 34.7 %collective-permute-start.33 = (bf16[128,6144]{1,0:T(8,128)(2,1)S(1)}, bf16[128,6144]{1,0:T(8,128)(2,1)S(1)}, u32[]{:S(2)}, u32[]{:S(2)}) collective-permute-start(bf16[128,6144]{1,0:T(8,128)(2,1)S(1)} %bitcast.35), channel_id=1, source_target_pairs={{0,24},{8,0},{16,8},{24,16},{1,25},{9,1},{17,9},{25,17},{2,26},{10... | collective-permute-start | bytes 4718600 | tf_op jit(solution)/shard_map/ppermute | solution.py:49
  135.0 12.3 %collective-permute-start.36 = (bf16[32,6272]{1,0:T(8,128)(2,1)S(1)}, bf16[32,6272]{1,0:T(8,128)(2,1)S(1)}, u32[]{:S(2)}, u32[]{:S(2)}) collective-permute-start(bf16[32,6272]{1,0:T(8,128)(2,1)S(1)} %get-tuple-element.214), channel_id=1, source_target_pairs={{0,2},{2,4},{4,6},{6,7},{7,5},{5,3},{3,1},{1,0},{8,10},{10,12},{12... | collective-permute-start | bytes 1204232 | tf_op jit(solution)/shard_map/window_16/ppermute | solution.py:44
  147.5 15.6 %collective-permute-start.38 = (bf16[32,6272]{1,0:T(8,128)(2,1)S(1)}, bf16[32,6272]{1,0:T(8,128)(2,1)S(1)}, u32[]{:S(2)}, u32[]{:S(2)}) collective-permute-start(bf16[32,6272]{1,0:T(8,128)(2,1)S(1)} %get-tuple-element.219), channel_id=1, source_target_pairs={{0,2},{2,4},{4,6},{6,7},{7,5},{5,3},{3,1},{1,0},{8,10},{10,12},{12... | collective-permute-start | bytes 1204232 | tf_op jit(solution)/shard_map/window_17/ppermute | solution.py:44
  148.9 14.3 %collective-permute-start.39 = (bf16[32,6272]{1,0:T(8,128)(2,1)S(1)}, bf16[32,6272]{1,0:T(8,128)(2,1)S(1)}, u32[]{:S(2)}, u32[]{:S(2)}) collective-permute-start(bf16[32,6272]{1,0:T(8,128)(2,1)S(1)} %get-tuple-element.220), channel_id=1, source_target_pairs={{0,1},{2,0},{4,2},{6,4},{7,6},{5,7},{3,5},{1,3},{8,9},{10,8},{12,1... | collective-permute-start | bytes 1204232 | tf_op jit(solution)/shard_map/window_17/ppermute | solution.py:44
  149.4 13.7 %collective-permute-start.41 = (bf16[32,6144]{1,0:T(8,128)(2,1)S(1)}, bf16[32,6144]{1,0:T(8,128)(2,1)S(1)}, u32[]{:S(2)}, u32[]{:S(2)}) collective-permute-start(bf16[32,6144]{1,0:T(8,128)(2,1)S(1)} %shard_map.143), channel_id=1, source_target_pairs={{0,8},{8,16},{16,24},{24,0},{1,9},{9,17},{17,25},{25,1},{2,10},{10... | collective-permute-start | bytes 1179656 | tf_op jit(solution)/shard_map/ppermute | solution.py:49
  (28 other events, 235.6 us)

commit v5 on v4

--- a/solution.py
+++ b/solution.py
@@ -276,15 +276,22 @@
         up_sum[...] = product if k == 0 else up_sum[...] + product
 
 
-def gate_up_scratch(copies, count, side, width, hid):
-    return [
-        pltpu.VMEM((count * side, width), bf16),
-        pltpu.VMEM((count * side, hid), f32),
-        pltpu.VMEM((count * side, hid), f32),
-        pltpu.VMEM((width, hid), bf16),
-        pltpu.SemaphoreType.DMA((copies,)),
-        pltpu.SemaphoreType.DMA((6,)),
-    ]
+def gate_up_held(held_shape, shards, gate_ref, up_ref, rows_ref, gate_sum, up_sum, row_sems):
+    rows = row_copies(held_shape, shards, rows_ref, row_sems)
+    start_all(rows)
+    for copy in rows:
+        copy.wait()
+    for k, part in enumerate(pieces_of(gate_ref.shape[0], 6, 128)):
+        for weight, total in ((gate_ref, gate_sum), (up_ref, up_sum)):
+            product = dot_n(rows_ref[:, part], weight[part, :])
+            total[...] = product if k == 0 else total[...] + product
+
+
+def gate_up_scratch(copies, count, side, width, hid, held=False):
+    sums = [pltpu.VMEM((count * side, hid), f32)] * 2
+    loads = [] if held else [pltpu.VMEM((width, hid), bf16)]
+    sems = [pltpu.SemaphoreType.DMA((copies,))] + [pltpu.SemaphoreType.DMA((6,))] * (not held)
+    return [pltpu.VMEM((count * side, width), bf16), *sums, *loads, *sems]
 
 
 def gate_up_cost(count, side, width, hid):
@@ -315,7 +322,7 @@
 def cots_kernel(held_shape, *refs):
     count = sum(len(widths) for widths in held_shape)
     shards, (gate_ref, up_ref, back_ref, gate_cot_ref, up_cot_ref, slope_ref, *scratch) = refs[:count], refs[count:]
-    gate_up(held_shape, shards, gate_ref, up_ref, *scratch)
+    gate_up_held(held_shape, shards, gate_ref, up_ref, *scratch)
     gate_pre, up_pre = scratch[1][...], scratch[2][...]
     sig = jax.nn.sigmoid(gate_pre)
     silu = gate_pre * sig
@@ -330,15 +337,15 @@
     count, side, width, hid = len(held), held[0][0].shape[0], sum(widths_of(held)[0]), gate.shape[1]
     return pl.pallas_call(
         functools.partial(cots_kernel, widths_of(held)),
-        in_specs=[anywhere] * len(flat(held)) + [in_vmem, in_hbm, in_vmem],
+        in_specs=[anywhere] * len(flat(held)) + [in_vmem] * 3,
         out_specs=[in_vmem] * 3,
         out_shape=[
             shape_of(count * side, hid),
             shape_of(count * side, hid),
             shape_of(count * side, 128, f32),
         ],
-        scratch_shapes=gate_up_scratch(len(flat(held)), count, side, width, hid),
-        compiler_params=params(26),
+        scratch_shapes=gate_up_scratch(len(flat(held)), count, side, width, hid, True),
+        compiler_params=params(14),
         cost_estimate=gate_up_cost(count, side, width, hid),
     )(*flat(held), gate, up, back)
 
@@ -409,21 +416,14 @@
     return regroup(held, arrays)
 
 
-def rowpart_kernel(held, gate_cot_ref, up_cot_ref, slope_ref, gate_ref, up_ref, *refs):
-    out_refs, (up_w, up_sems) = refs[:-2], refs[-2:]
+def rowpart_kernel(held, gate_cot_ref, up_cot_ref, slope_ref, gate_ref, up_ref, *out_refs):
     width = gate_ref.shape[0]
     parts = pieces_of(width, 6, 128)
 
-    ups = [pltpu.make_async_copy(up_ref.at[part], up_w.at[part], up_sems.at[k]) for k, part in enumerate(parts)]
-    start_all(ups)
     spread(out_refs, held, width, slope_ref[...].astype(bf16))
-    ahead = [dot_t(gate_cot_ref[...], gate_ref[part, :]) for part in parts[:2]]
-    for k, part in enumerate(parts):
-        ups[k].wait()
-        value = ahead.pop(0) + dot_t(up_cot_ref[...], up_w[part, :])
+    for part in parts:
+        value = dot_t(gate_cot_ref[...], gate_ref[part, :]) + dot_t(up_cot_ref[...], up_ref[part, :])
         spread(out_refs, held, part.start, value.astype(bf16))
-        if k + 2 < len(parts):
-            ahead.append(dot_t(gate_cot_ref[...], gate_ref[parts[k + 2], :]))
 
 
 def rowpart_call(count, gate_cot, up_cot, slope, gate, up):
@@ -432,11 +432,10 @@
     shapes = part_shapes(rows // count, held)
     arrays = pl.pallas_call(
         functools.partial(rowpart_kernel, held),
-        in_specs=[in_vmem] * 4 + [in_hbm],
+        in_specs=[in_vmem] * 5,
         out_specs=[in_vmem] * len(shapes),
         out_shape=shapes,
-        scratch_shapes=[pltpu.VMEM((width, hid), bf16), pltpu.SemaphoreType.DMA((6,))],
-        compiler_params=params(20),
+        compiler_params=params(6),
         cost_estimate=cost(4 * rows * width * hid, 4 * width * hid),
     )(gate_cot, up_cot, slope, gate, up)
     return regroup(held, arrays)
@@ -646,10 +645,10 @@
         return (back_call(gather_u.held, env["down"]),)
 
     def cots(back):
-        return cots_call(gather_h.held, env["gate"], up, back)
+        return cots_call(gather_h.held, env["gate"], env["up"], back)
 
     def rowpart(gate_cot, up_cot, slope):
-        parts = rowpart_call(count, gate_cot, up_cot, slope, env["gate"], up)
+        parts = rowpart_call(count, gate_cot, up_cot, slope, env["gate"], env["up"])
         scatter_r.begin(parts)
         env["renewed"] = list(parts)
         return ()
@@ -700,6 +699,7 @@
     put(h_done-3, ("act_base",), nothing, ())
     put(out+1, ("grad_base",), nothing, ())
     put(h_done - 2, ("select_f",), back, ("back",))
+    put(h_done - 1, ("select_f",), load("up", up), ("flag_u",))
     put(h_done, ("back",), cots, ("gate_cot", "up_cot", "slope"))
     put(h_done + 1, ("gate_cot", "up_cot", "slope"), rowpart, ())
     put(out + 1, ("select_f",), shifts, ())

time: 185 us -> 183 us (0.989)
  waiting for transfers between devices: 59.5 us -> 57.1 us
    pallas_call x2 -> x3, Pallas kernels: 9.48 us -> 14.2 us  [load_call(): pl.pallas_call(load_kernel, in_specs=[anywhere, in_hbm], out_specs=[in_vm...]
    pallas_call x1, Pallas kernels: 10.4 us -> 6.68 us  [rowpart_call(): pl.pallas_call(functools.partial(rowpart_kernel, held), in_specs=[in_vmem...]
    ppermute x40, waiting for transfers between devices: 53.2 us -> 50.8 us  [hop(): lax.ppermute(value, 'expert', [(ring[i], ring[(i + steps) % count]) for i...]
  transfers between devices with their start and end apart: 46 -> 46, of which waited for: 24 -> 25; matrix products, arithmetic and copies ran while one was open for 0% -> 0% of each run, Pallas kernels for 32% -> 32%
where the time goes in v5:
time: 183 us
  Pallas kernels  64.4 us (35%)
  starting transfers between devices  60.3 us (33%)
  waiting for transfers between devices  57.1 us (31%)
    ppermute x40, waiting for transfers between devices, hop(): lax.ppermute(value, 'expert', [(ring[i], ring[(i + steps) % count]) for i...  50.8 us
    ppermute x40, starting transfers between devices, hop(): lax.ppermute(value, 'expert', [(ring[i], ring[(i + steps) % count]) for i...  30.8 us
    ppermute x6, starting transfers between devices, shifted(): lax.ppermute(value, 'section', [(source, (source + steps) % count) for so...  29.5 us
    pallas_call x3, Pallas kernels, load_call(): pl.pallas_call(load_kernel, in_specs=[anywhere, in_hbm], out_specs=[in_vm...  14.2 us
    pallas_call x1, Pallas kernels, active_call(): pl.pallas_call(functools.partial(active_kernel, widths_of(held)), in_spec...  8.67 us
    pallas_call x1, Pallas kernels, cots_call(): pl.pallas_call(functools.partial(cots_kernel, widths_of(held)), in_specs=...  8.55 us
    pallas_call x1, Pallas kernels, rowpart_call(): pl.pallas_call(functools.partial(rowpart_kernel, held), in_specs=[in_vmem...  6.68 us
    pallas_call x3, Pallas kernels, front_call(): pl.pallas_call(front_kernel, in_specs=[anywhere] + [in_hbm] * 3, out_spec...  6.31 us
  transfers between devices with their start and end apart: 46, of which 25 were waited for; matrix products, arithmetic and copies ran while one was open for 0% of the time, Pallas kernels for 32%

profile of v5, /device:TPU:1, one launch (start us, length us, event | category | flops | bytes accessed | tf_op | source)
XLA Modules:
  0.0 183.0 jit_solution(9271516871083398455)
XLA Ops:
  2.7 2.2 %collective-permute-start.2 = (bf16[32,6144]{1,0:T(8,128)(2,1)S(1)}, bf16[32,6144]{1,0:T(8,128)(2,1)S(1)}, u32[]{:S(2)}, u32[]{:S(2)}) collective-permute-start(bf16[32,6144]{1,0:T(8,128)(2,1)S(1)} %get-tuple-element.131.refs_0_), channel_id=1, source_target_pairs={{0,2},{2,4},{4,6},{6,7},{7,5},{5,3},{3,1},{1,0},{8,10},{10,12},{12... | collective-permute-start | bytes 1179656 | tf_op jit(solution)/shard_map/window_0/ppermute | solution.py:44
  8.3 2.4 %shard_map.117 = (bf16[32,128]{1,0:T(8,128)(2,1)}, bf16[32,6144]{1,0:T(8,128)(2,1)S(1)}, bf16[32,6144]{1,0:T(8,128)(2,1)S(1)}) custom-call(bf16[32,128]{1,0:T(8,128)(2,1)S(1)} %get-tuple-element.132.after_ref.refs_3_, s32[2,128]{1,0:T(2,128)} %bitcast.20, bf16[128,6144]{1,0:T(8,128)(2,1)} %bitcast.30, f32[1,6144]{1,0:T(1,128)} %gain_ref.5), custom_call_target="tpu_custom_call" | custom-call | bytes 6291456 | tf_op jit(solution)/shard_map/pallas_call | solution.py:487
  10.7 3.0 %collective-permute-done.2.refs_0_ = bf16[32,6144]{1,0:T(8,128)(2,1)S(1)} collective-permute-done((bf16[32,6144]{1,0:T(8,128)(2,1)S(1)}, bf16[32,6144]{1,0:T(8,128)(2,1)S(1)}, u32[]{:S(2)}, u32[]{:S(2)}) %collective-permute-start.2) | collective-permute-done | bytes 393248 | tf_op jit(solution)/shard_map/window_0/ppermute | solution.py:44
  16.0 4.8 %shard_map.119 = (bf16[6144,1024]{1,0:T(8,128)(2,1)S(1)}, f32[8,128]{1,0:T(8,128)S(1)}) custom-call(bf16[32,128]{1,0:T(8,128)(2,1)S(1)} %get-tuple-element.134.after_ref.refs_3_, bf16[6144,1024]{1,0:T(8,128)(2,1)} %bitcast.26), custom_call_target="tpu_custom_call" | custom-call | bytes 25165824 | tf_op jit(solution)/shard_map/pallas_call | solution.py:223
  24.5 5.0 %collective-permute-start.18 = (bf16[128,6144]{1,0:T(8,128)(2,1)S(1)}, bf16[128,6144]{1,0:T(8,128)(2,1)S(1)}, u32[]{:S(2)}, u32[]{:S(2)}) collective-permute-start(bf16[128,6144]{1,0:T(8,128)(2,1)S(1)} %bitcast.32), channel_id=1, source_target_pairs={{0,8},{8,16},{16,24},{24,0},{1,9},{9,17},{17,25},{25,1},{2,10},{10... | collective-permute-start | bytes 4718600 | tf_op jit(solution)/shard_map/ppermute | solution.py:49
  29.5 4.7 %shard_map.122 = (bf16[1024,6144]{1,0:T(8,128)(2,1)S(1)}, f32[8,128]{1,0:T(8,128)S(1)}) custom-call(bf16[32,128]{1,0:T(8,128)(2,1)S(1)} %get-tuple-element.142.after_ref.refs_2_, bf16[1024,6144]{1,0:T(8,128)(2,1)} %bitcast.27), custom_call_target="tpu_custom_call" | custom-call | bytes 25165824 | tf_op jit(solution)/shard_map/pallas_call | solution.py:223
  35.7 3.3 %collective-permute-done.4.refs_0_ = bf16[32,6144]{1,0:T(8,128)(2,1)S(1)} collective-permute-done((bf16[32,6144]{1,0:T(8,128)(2,1)S(1)}, bf16[32,6144]{1,0:T(8,128)(2,1)S(1)}, u32[]{:S(2)}, u32[]{:S(2)}) %collective-permute-start.4) | collective-permute-done | bytes 393248 | tf_op jit(solution)/shard_map/window_3/ppermute | solution.py:44
  41.3 6.1 %collective-permute-done.10.refs_0_ = bf16[32,6144]{1,0:T(8,128)(2,1)S(1)} collective-permute-done((bf16[32,6144]{1,0:T(8,128)(2,1)S(1)}, bf16[32,6144]{1,0:T(8,128)(2,1)S(1)}, u32[]{:S(2)}, u32[]{:S(2)}) %collective-permute-start.10) | collective-permute-done | bytes 393248 | tf_op jit(solution)/shard_map/window_4/ppermute | solution.py:44
  49.9 5.9 %collective-permute-done.14.refs_0_ = bf16[32,6144]{1,0:T(8,128)(2,1)S(1)} collective-permute-done((bf16[32,6144]{1,0:T(8,128)(2,1)S(1)}, bf16[32,6144]{1,0:T(8,128)(2,1)S(1)}, u32[]{:S(2)}, u32[]{:S(2)}) %collective-permute-start.14) | collective-permute-done | bytes 393248 | tf_op jit(solution)/shard_map/window_5/ppermute | solution.py:44
  57.3 2.7 %collective-permute-done.12.refs_0_ = bf16[32,3072]{1,0:T(8,128)(2,1)S(1)} collective-permute-done((bf16[32,3072]{1,0:T(8,128)(2,1)S(1)}, bf16[32,3072]{1,0:T(8,128)(2,1)S(1)}, u32[]{:S(2)}, u32[]{:S(2)}) %collective-permute-start.12) | collective-permute-done | bytes 196640 | tf_op jit(solution)/shard_map/window_6/ppermute | solution.py:44
  61.5 8.7 %shard_map.126.refs_2_ = bf16[256,1024]{1,0:T(8,128)(2,1)S(1)} custom-call(bf16[32,6144]{1,0:T(8,128)(2,1)S(1)} %get-tuple-element.131.refs_0_, bf16[32,6144]{1,0:T(8,128)(2,1)S(1)} %get-tuple-element.140.refs_1_, bf16[32,6144]{1,0:T(8,128)(2,1)S(1)} %get-tuple-element.144.refs_2_, bf16[32,6144]{1,0:T(8,128)(2,1)S(1)} %get-tuple-element.146.refs_3_, ...), custom_call_target="tpu_custom_call" | custom-call | flops 6442450944 | bytes 28311552 | tf_op jit(solution)/shard_map/pallas_call | solution.py:311
  71.8 5.3 %shard_map.128 = (bf16[32,6144]{1,0:T(8,128)(2,1)S(1)}, bf16[32,6144]{1,0:T(8,128)(2,1)S(1)}, bf16[32,6144]{1,0:T(8,128)(2,1)S(1)}, bf16[32,6144]{1,0:T(8,128)(2...) custom-call(bf16[256,1024]{1,0:T(8,128)(2,1)S(1)} %get-tuple-element, ...), custom_call_target="tpu_custom_call" | custom-call | flops 3221225472 | bytes 12582912 | tf_op jit(solution)/shard_map/pallas_call | solution.py:407
  83.5 5.0 %shard_map.132.refs_4_ = f32[256,1024]{1,0:T(8,128)S(1)} custom-call(bf16[32,6144]{1,0:T(8,128)(2,1)S(1)} %get-tuple-element.130.refs_0_, bf16[32,6144]{1,0:T(8,128)(2,1)S(1)} %get-tuple-element.137.refs_1_, bf16[32,6144]{1,0:T(8,128)(2,1)S(1)} %get-tuple-element.139.refs_2_, bf16[32,6144]{1,0:T(8,128)(2,1)S(1)} %get-tuple-element.162.refs_3_, ...), custom_call_target="tpu_custom_call" | custom-call | flops 3221225472 | bytes 15728640 | tf_op jit(solution)/shard_map/pallas_call | solution.py:248
  88.4 3.7 %collective-permute-done.23.refs_2_ = bf16[32,3072]{1,0:T(8,128)(2,1)S(1)} collective-permute-done((bf16[32,3072]{1,0:T(8,128)(2,1)S(1)}, bf16[32,3072]{1,0:T(8,128)(2,1)S(1)}, u32[]{:S(2)}, u32[]{:S(2)}) %collective-permute-start.23) | collective-permute-done | bytes 196640 | tf_op jit(solution)/shard_map/window_11/ppermute | solution.py:44
  95.3 3.4 %collective-permute-start.33 = (bf16[128,6144]{1,0:T(8,128)(2,1)S(1)}, bf16[128,6144]{1,0:T(8,128)(2,1)S(1)}, u32[]{:S(2)}, u32[]{:S(2)}) collective-permute-start(bf16[128,6144]{1,0:T(8,128)(2,1)S(1)} %bitcast.34), channel_id=1, source_target_pairs={{0,24},{8,0},{16,8},{24,16},{1,25},{9,1},{17,9},{25,17},{2,26},{10... | collective-permute-start | bytes 4718600 | tf_op jit(solution)/shard_map/ppermute | solution.py:49
  100.3 4.7 %shard_map.134 = (bf16[6144,1024]{1,0:T(8,128)(2,1)S(1)}, f32[8,128]{1,0:T(8,128)S(1)}) custom-call(bf16[32,128]{1,0:T(8,128)(2,1)S(1)} %get-tuple-element.179.after_ref.refs_3_, bf16[6144,1024]{1,0:T(8,128)(2,1)} %bitcast.25), custom_call_target="tpu_custom_call" | custom-call | bytes 25165824 | tf_op jit(solution)/shard_map/pallas_call | solution.py:223
  108.9 8.6 %shard_map.136 = (bf16[256,1024]{1,0:T(8,128)(2,1)S(1)}, bf16[256,1024]{1,0:T(8,128)(2,1)S(1)}, f32[256,128]{1,0:T(8,128)S(1)}) custom-call(bf16[32,6144]{1,0:T(8,128)(2,1)S(1)} %get-tuple-element.155.refs_0_, bf16[32,6144]{1,0:T(8,128)(2,1)S(1)} %get-tuple-element.157.refs_1_, bf16[32,6144]{1,0:T(8,128)(2,1)S(1)} %get-tuple-element.160.refs_2_, ...), custom_call_target="tpu_custom_call" | custom-call | flops 6442450944 | bytes 28311552 | tf_op jit(solution)/shard_map/pallas_call | solution.py:338
  119.2 6.7 %shard_map.138 = (bf16[32,6272]{1,0:T(8,128)(2,1)S(1)}, bf16[32,6272]{1,0:T(8,128)(2,1)S(1)}, bf16[32,6272]{1,0:T(8,128)(2,1)S(1)}, bf16[32,6272]{1,0:T(8,128)(2...) custom-call(bf16[256,1024]{1,0:T(8,128)(2,1)S(1)} %get-tuple-element, ...), custom_call_target="tpu_custom_call" | custom-call | flops 6442450944 | bytes 25165824 | tf_op jit(solution)/shard_map/pallas_call | solution.py:433
  128.5 2.9 %collective-permute-done.34.refs_0_ = bf16[32,3072]{1,0:T(8,128)(2,1)S(1)} collective-permute-done((bf16[32,3072]{1,0:T(8,128)(2,1)S(1)}, bf16[32,3072]{1,0:T(8,128)(2,1)S(1)}, u32[]{:S(2)}, u32[]{:S(2)}) %collective-permute-start.34) | collective-permute-done | bytes 196640 | tf_op jit(solution)/shard_map/window_15/ppermute | solution.py:44
  134.8 10.4 %collective-permute-start.40 = (bf16[32,128]{1,0:T(8,128)(2,1)S(1)}, bf16[32,128]{1,0:T(8,128)(2,1)S(1)}, u32[]{:S(2)}, u32[]{:S(2)}) collective-permute-start(bf16[32,128]{1,0:T(8,128)(2,1)S(1)} %get-tuple-element.215.after_ref.refs_2_), channel_id=1, source_target_pairs={{0,8},{8,16},{16,24},{24,0},{1,9},{9,17},{17,25},{25,1},{2,10},{10... | collective-permute-start | bytes 24584 | tf_op jit(solution)/shard_map/ppermute | solution.py:49
  148.1 9.0 %collective-permute-start.41 = (bf16[32,6144]{1,0:T(8,128)(2,1)S(1)}, bf16[32,6144]{1,0:T(8,128)(2,1)S(1)}, u32[]{:S(2)}, u32[]{:S(2)}) collective-permute-start(bf16[32,6144]{1,0:T(8,128)(2,1)S(1)} %shard_map.144), channel_id=1, source_target_pairs={{0,8},{8,16},{16,24},{24,0},{1,9},{9,17},{17,25},{25,1},{2,10},{10... | collective-permute-start | bytes 1179656 | tf_op jit(solution)/shard_map/ppermute | solution.py:49
  157.1 3.0 %shard_map.143 = (f32[32,128]{1,0:T(8,128)S(1)}, f32[32,6144]{1,0:T(8,128)S(1)}) custom-call(bf16[32,128]{1,0:T(8,128)(2,1)S(1)} %get-tuple-element.227.after_ref, bf16[32,6144]{1,0:T(8,128)(2,1)S(1)} %get-tuple-element.228.rows_ref, f32[1,6144]{1,0:T(1,128)S(1)} %copy-done, f32[8,6144]{1,0:T(8,128)S(1)} %bitcast.18, s32[2,128]{1,0:T(2,128)S(1)} %bitcast.21), custom_call_target="tpu_custom_call" | custom-call | bytes 2359296 | tf_op jit(solution)/shard_map/pallas_call | solution.py:584
  163.5 8.9 %collective-permute-done.43.a_ref = bf16[32,6272]{1,0:T(8,128)(2,1)S(1)} collective-permute-done((bf16[32,6272]{1,0:T(8,128)(2,1)S(1)}, bf16[32,6272]{1,0:T(8,128)(2,1)S(1)}, u32[]{:S(2)}, u32[]{:S(2)}) %collective-permute-start.43) | collective-permute-done | bytes 401440 | tf_op jit(solution)/shard_map/window_18/ppermute | solution.py:44
  177.4 3.7 %collective-permute-done.45.rows_ref = bf16[32,6144]{1,0:T(8,128)(2,1)S(1)} collective-permute-done((bf16[32,6144]{1,0:T(8,128)(2,1)S(1)}, bf16[32,6144]{1,0:T(8,128)(2,1)S(1)}, u32[]{:S(2)}, u32[]{:S(2)}) %collective-permute-start.45) | collective-permute-done | bytes 393248 | tf_op jit(solution)/shard_map/ppermute | solution.py:49
  (132 shorter events, 58.1 us)
Async XLA Ops:
  6.8 15.3 %collective-permute-start = (bf16[32,6144]{1,0:T(8,128)(2,1)S(1)}, bf16[32,6144]{1,0:T(8,128)(2,1)S(1)}, u32[]{:S(2)}, u32[]{:S(2)}) collective-permute-start(bf16[32,6144]{1,0:T(8,128)(2,1)S(1)} %get-tuple-element.130.refs_0_), channel_id=1, source_target_pairs={{0,2},{2,4},{4,6},{6,7},{7,5},{5,3},{3,1},{1,0},{8,10},{10,12},{12... | collective-permute-start | bytes 1179656 | tf_op jit(solution)/shard_map/window_1/ppermute | solution.py:44
  8.3 14.7 %collective-permute-start.1 = (bf16[32,6144]{1,0:T(8,128)(2,1)S(1)}, bf16[32,6144]{1,0:T(8,128)(2,1)S(1)}, u32[]{:S(2)}, u32[]{:S(2)}) collective-permute-start(bf16[32,6144]{1,0:T(8,128)(2,1)S(1)} %get-tuple-element.130.refs_0_), channel_id=1, source_target_pairs={{0,1},{2,0},{4,2},{6,4},{7,6},{5,7},{3,5},{1,3},{8,9},{10,8},{12,1... | collective-permute-start | bytes 1179656 | tf_op jit(solution)/shard_map/window_1/ppermute | solution.py:44
  14.6 19.6 %collective-permute-start.8 = (bf16[32,6144]{1,0:T(8,128)(2,1)S(1)}, bf16[32,6144]{1,0:T(8,128)(2,1)S(1)}, u32[]{:S(2)}, u32[]{:S(2)}) collective-permute-start(bf16[32,6144]{1,0:T(8,128)(2,1)S(1)} %get-tuple-element.141.refs_8_), channel_id=1, source_target_pairs={{0,2},{2,4},{4,6},{6,7},{7,5},{5,3},{3,1},{1,0},{8,10},{10,12},{12... | collective-permute-start | bytes 1179656 | tf_op jit(solution)/shard_map/window_2/ppermute | solution.py:44
  15.9 18.3 %collective-permute-start.9 = (bf16[32,6144]{1,0:T(8,128)(2,1)S(1)}, bf16[32,6144]{1,0:T(8,128)(2,1)S(1)}, u32[]{:S(2)}, u32[]{:S(2)}) collective-permute-start(bf16[32,6144]{1,0:T(8,128)(2,1)S(1)} %get-tuple-element.140.refs_1_), channel_id=1, source_target_pairs={{0,1},{2,0},{4,2},{6,4},{7,6},{5,7},{3,5},{1,3},{8,9},{10,8},{12,1... | collective-permute-start | bytes 1179656 | tf_op jit(solution)/shard_map/window_2/ppermute | solution.py:44
  23.0 16.0 %collective-permute-start.4 = (bf16[32,6144]{1,0:T(8,128)(2,1)S(1)}, bf16[32,6144]{1,0:T(8,128)(2,1)S(1)}, u32[]{:S(2)}, u32[]{:S(2)}) collective-permute-start(bf16[32,6144]{1,0:T(8,128)(2,1)S(1)} %get-tuple-element.136.refs_8_), channel_id=1, source_target_pairs={{0,2},{2,4},{4,6},{6,7},{7,5},{5,3},{3,1},{1,0},{8,10},{10,12},{12... | collective-permute-start | bytes 1179656 | tf_op jit(solution)/shard_map/window_3/ppermute | solution.py:44
  24.3 15.6 %collective-permute-start.5 = (bf16[32,6144]{1,0:T(8,128)(2,1)S(1)}, bf16[32,6144]{1,0:T(8,128)(2,1)S(1)}, u32[]{:S(2)}, u32[]{:S(2)}) collective-permute-start(bf16[32,6144]{1,0:T(8,128)(2,1)S(1)} %get-tuple-element.137.refs_1_), channel_id=1, source_target_pairs={{0,1},{2,0},{4,2},{6,4},{7,6},{5,7},{3,5},{1,3},{8,9},{10,8},{12,1... | collective-permute-start | bytes 1179656 | tf_op jit(solution)/shard_map/window_3/ppermute | solution.py:44
  24.5 53.3 %collective-permute-start.18 = (bf16[128,6144]{1,0:T(8,128)(2,1)S(1)}, bf16[128,6144]{1,0:T(8,128)(2,1)S(1)}, u32[]{:S(2)}, u32[]{:S(2)}) collective-permute-start(bf16[128,6144]{1,0:T(8,128)(2,1)S(1)} %bitcast.32), channel_id=1, source_target_pairs={{0,8},{8,16},{16,24},{24,0},{1,9},{9,17},{17,25},{25,1},{2,10},{10... | collective-permute-start | bytes 4718600 | tf_op jit(solution)/shard_map/ppermute | solution.py:49
  34.2 13.2 %collective-permute-start.10 = (bf16[32,6144]{1,0:T(8,128)(2,1)S(1)}, bf16[32,6144]{1,0:T(8,128)(2,1)S(1)}, u32[]{:S(2)}, u32[]{:S(2)}) collective-permute-start(bf16[32,6144]{1,0:T(8,128)(2,1)S(1)} %get-tuple-element.145.refs_7_), channel_id=1, source_target_pairs={{0,2},{2,4},{4,6},{6,7},{7,5},{5,3},{3,1},{1,0},{8,10},{10,12},{12... | collective-permute-start | bytes 1179656 | tf_op jit(solution)/shard_map/window_4/ppermute | solution.py:44
  35.5 12.8 %collective-permute-start.11 = (bf16[32,6144]{1,0:T(8,128)(2,1)S(1)}, bf16[32,6144]{1,0:T(8,128)(2,1)S(1)}, u32[]{:S(2)}, u32[]{:S(2)}) collective-permute-start(bf16[32,6144]{1,0:T(8,128)(2,1)S(1)} %get-tuple-element.144.refs_2_), channel_id=1, source_target_pairs={{0,1},{2,0},{4,2},{6,4},{7,6},{5,7},{3,5},{1,3},{8,9},{10,8},{12,1... | collective-permute-start | bytes 1179656 | tf_op jit(solution)/shard_map/window_4/ppermute | solution.py:44
  39.9 16.0 %collective-permute-start.14 = (bf16[32,6144]{1,0:T(8,128)(2,1)S(1)}, bf16[32,6144]{1,0:T(8,128)(2,1)S(1)}, u32[]{:S(2)}, u32[]{:S(2)}) collective-permute-start(bf16[32,6144]{1,0:T(8,128)(2,1)S(1)} %get-tuple-element.155.refs_0_), channel_id=1, source_target_pairs={{0,2},{2,4},{4,6},{6,7},{7,5},{5,3},{3,1},{1,0},{8,10},{10,12},{12... | collective-permute-start | bytes 1179656 | tf_op jit(solution)/shard_map/window_5/ppermute | solution.py:44
  41.2 15.9 %collective-permute-start.15 = (bf16[32,6144]{1,0:T(8,128)(2,1)S(1)}, bf16[32,6144]{1,0:T(8,128)(2,1)S(1)}, u32[]{:S(2)}, u32[]{:S(2)}) collective-permute-start(bf16[32,6144]{1,0:T(8,128)(2,1)S(1)} %get-tuple-element.155.refs_0_), channel_id=1, source_target_pairs={{0,1},{2,0},{4,2},{6,4},{7,6},{5,7},{3,5},{1,3},{8,9},{10,8},{12,1... | collective-permute-start | bytes 1179656 | tf_op jit(solution)/shard_map/window_5/ppermute | solution.py:44
  55.8 14.4 %collective-permute-start.6 = (bf16[32,6144]{1,0:T(8,128)(2,1)S(1)}, bf16[32,6144]{1,0:T(8,128)(2,1)S(1)}, u32[]{:S(2)}, u32[]{:S(2)}) collective-permute-start(bf16[32,6144]{1,0:T(8,128)(2,1)S(1)} %get-tuple-element.138.refs_7_), channel_id=1, source_target_pairs={{0,2},{2,4},{4,6},{6,7},{7,5},{5,3},{3,1},{1,0},{8,10},{10,12},{12... | collective-permute-start | bytes 1179656 | tf_op jit(solution)/shard_map/window_7/ppermute | solution.py:44
  57.0 13.2 %collective-permute-start.7 = (bf16[32,6144]{1,0:T(8,128)(2,1)S(1)}, bf16[32,6144]{1,0:T(8,128)(2,1)S(1)}, u32[]{:S(2)}, u32[]{:S(2)}) collective-permute-start(bf16[32,6144]{1,0:T(8,128)(2,1)S(1)} %get-tuple-element.139.refs_2_), channel_id=1, source_target_pairs={{0,1},{2,0},{4,2},{6,4},{7,6},{5,7},{3,5},{1,3},{8,9},{10,8},{12,1... | collective-permute-start | bytes 1179656 | tf_op jit(solution)/shard_map/window_7/ppermute | solution.py:44
  60.0 17.1 %collective-permute-start.16 = (bf16[32,6144]{1,0:T(8,128)(2,1)S(1)}, bf16[32,6144]{1,0:T(8,128)(2,1)S(1)}, u32[]{:S(2)}, u32[]{:S(2)}) collective-permute-start(bf16[32,6144]{1,0:T(8,128)(2,1)S(1)} %get-tuple-element.156.refs_8_), channel_id=1, source_target_pairs={{0,2},{2,4},{4,6},{6,7},{7,5},{5,3},{3,1},{1,0},{8,10},{10,12},{12... | collective-permute-start | bytes 1179656 | tf_op jit(solution)/shard_map/window_8/ppermute | solution.py:44
  61.2 16.5 %collective-permute-start.17 = (bf16[32,6144]{1,0:T(8,128)(2,1)S(1)}, bf16[32,6144]{1,0:T(8,128)(2,1)S(1)}, u32[]{:S(2)}, u32[]{:S(2)}) collective-permute-start(bf16[32,6144]{1,0:T(8,128)(2,1)S(1)} %get-tuple-element.157.refs_1_), channel_id=1, source_target_pairs={{0,1},{2,0},{4,2},{6,4},{7,6},{5,7},{3,5},{1,3},{8,9},{10,8},{12,1... | collective-permute-start | bytes 1179656 | tf_op jit(solution)/shard_map/window_8/ppermute | solution.py:44
  77.8 15.9 %collective-permute-start.19 = (bf16[32,6144]{1,0:T(8,128)(2,1)S(1)}, bf16[32,6144]{1,0:T(8,128)(2,1)S(1)}, u32[]{:S(2)}, u32[]{:S(2)}) collective-permute-start(bf16[32,6144]{1,0:T(8,128)(2,1)S(1)} %get-tuple-element.159.refs_7_), channel_id=1, source_target_pairs={{0,2},{2,4},{4,6},{6,7},{7,5},{5,3},{3,1},{1,0},{8,10},{10,12},{12... | collective-permute-start | bytes 1179656 | tf_op jit(solution)/shard_map/window_10/ppermute | solution.py:44
  79.1 14.6 %collective-permute-start.20 = (bf16[32,6144]{1,0:T(8,128)(2,1)S(1)}, bf16[32,6144]{1,0:T(8,128)(2,1)S(1)}, u32[]{:S(2)}, u32[]{:S(2)}) collective-permute-start(bf16[32,6144]{1,0:T(8,128)(2,1)S(1)} %get-tuple-element.160.refs_2_), channel_id=1, source_target_pairs={{0,1},{2,0},{4,2},{6,4},{7,6},{5,7},{3,5},{1,3},{8,9},{10,8},{12,1... | collective-permute-start | bytes 1179656 | tf_op jit(solution)/shard_map/window_10/ppermute | solution.py:44
  93.8 13.4 %collective-permute-start.27 = (bf16[32,6144]{1,0:T(8,128)(2,1)S(1)}, bf16[32,6144]{1,0:T(8,128)(2,1)S(1)}, u32[]{:S(2)}, u32[]{:S(2)}) collective-permute-start(bf16[32,6144]{1,0:T(8,128)(2,1)S(1)} %get-tuple-element.177), channel_id=1, source_target_pairs={{0,2},{2,4},{4,6},{6,7},{7,5},{5,3},{3,1},{1,0},{8,10},{10,12},{12... | collective-permute-start | bytes 1179656 | tf_op jit(solution)/shard_map/window_12/ppermute | solution.py:44
  95.1 12.0 %collective-permute-start.28 = (bf16[32,6144]{1,0:T(8,128)(2,1)S(1)}, bf16[32,6144]{1,0:T(8,128)(2,1)S(1)}, u32[]{:S(2)}, u32[]{:S(2)}) collective-permute-start(bf16[32,6144]{1,0:T(8,128)(2,1)S(1)} %get-tuple-element.178), channel_id=1, source_target_pairs={{0,1},{2,0},{4,2},{6,4},{7,6},{5,7},{3,5},{1,3},{8,9},{10,8},{12,1... | collective-permute-start | bytes 1179656 | tf_op jit(solution)/shard_map/window_12/ppermute | solution.py:44
  95.3 30.6 %collective-permute-start.33 = (bf16[128,6144]{1,0:T(8,128)(2,1)S(1)}, bf16[128,6144]{1,0:T(8,128)(2,1)S(1)}, u32[]{:S(2)}, u32[]{:S(2)}) collective-permute-start(bf16[128,6144]{1,0:T(8,128)(2,1)S(1)} %bitcast.34), channel_id=1, source_target_pairs={{0,24},{8,0},{16,8},{24,16},{1,25},{9,1},{17,9},{25,17},{2,26},{10... | collective-permute-start | bytes 4718600 | tf_op jit(solution)/shard_map/ppermute | solution.py:49
  133.3 12.7 %collective-permute-start.36 = (bf16[32,6272]{1,0:T(8,128)(2,1)S(1)}, bf16[32,6272]{1,0:T(8,128)(2,1)S(1)}, u32[]{:S(2)}, u32[]{:S(2)}) collective-permute-start(bf16[32,6272]{1,0:T(8,128)(2,1)S(1)} %get-tuple-element.220), channel_id=1, source_target_pairs={{0,2},{2,4},{4,6},{6,7},{7,5},{5,3},{3,1},{1,0},{8,10},{10,12},{12... | collective-permute-start | bytes 1204232 | tf_op jit(solution)/shard_map/window_16/ppermute | solution.py:44
  146.2 15.7 %collective-permute-start.38 = (bf16[32,6272]{1,0:T(8,128)(2,1)S(1)}, bf16[32,6272]{1,0:T(8,128)(2,1)S(1)}, u32[]{:S(2)}, u32[]{:S(2)}) collective-permute-start(bf16[32,6272]{1,0:T(8,128)(2,1)S(1)} %get-tuple-element.225), channel_id=1, source_target_pairs={{0,2},{2,4},{4,6},{6,7},{7,5},{5,3},{3,1},{1,0},{8,10},{10,12},{12... | collective-permute-start | bytes 1204232 | tf_op jit(solution)/shard_map/window_17/ppermute | solution.py:44
  147.6 14.3 %collective-permute-start.39 = (bf16[32,6272]{1,0:T(8,128)(2,1)S(1)}, bf16[32,6272]{1,0:T(8,128)(2,1)S(1)}, u32[]{:S(2)}, u32[]{:S(2)}) collective-permute-start(bf16[32,6272]{1,0:T(8,128)(2,1)S(1)} %get-tuple-element.226), channel_id=1, source_target_pairs={{0,1},{2,0},{4,2},{6,4},{7,6},{5,7},{3,5},{1,3},{8,9},{10,8},{12,1... | collective-permute-start | bytes 1204232 | tf_op jit(solution)/shard_map/window_17/ppermute | solution.py:44
  148.1 13.7 %collective-permute-start.41 = (bf16[32,6144]{1,0:T(8,128)(2,1)S(1)}, bf16[32,6144]{1,0:T(8,128)(2,1)S(1)}, u32[]{:S(2)}, u32[]{:S(2)}) collective-permute-start(bf16[32,6144]{1,0:T(8,128)(2,1)S(1)} %shard_map.144), channel_id=1, source_target_pairs={{0,8},{8,16},{16,24},{24,0},{1,9},{9,17},{17,25},{25,1},{2,10},{10... | collective-permute-start | bytes 1179656 | tf_op jit(solution)/shard_map/ppermute | solution.py:49
  (28 other events, 225.9 us)

commit v6 on v5

--- a/solution.py
+++ b/solution.py
@@ -538,21 +538,27 @@
     )(rows, above, gain, scale, tilt, *sums)
 
 
-def place_kernel(select_ref, rows_ref, base_ref, out_ref):
+def place_kernel(select_ref, rows_ref, base_ref, out_ref, made, sems):
     select = select_ref[...]
     one = jnp.ones((select.shape[0], 128), bf16)
     used = lax.dot_general(select, one, first_dims, preferred_element_type=f32)[:, :1] > 0
-    for part in pieces_of(base_ref.shape[1], 6, 128):
+    copies = []
+    for k, part in enumerate(pieces_of(base_ref.shape[1], 6, 128)):
         spread_rows = lax.dot_general(select, rows_ref[:, part], first_dims, preferred_element_type=f32)
-        out_ref[:, part] = jnp.where(used, spread_rows.astype(bf16), base_ref[:, part])
+        made[:, part] = jnp.where(used, spread_rows.astype(bf16), base_ref[:, part])
+        copies.append(pltpu.make_async_copy(made.at[:, part], out_ref.at[:, part], sems.at[k]))
+        copies[-1].start()
+    for copy in copies:
+        copy.wait()
 
 
 def place_call(select, rows, base):
     return pl.pallas_call(
         place_kernel,
         in_specs=[in_vmem] * 3,
-        out_specs=in_vmem,
+        out_specs=anywhere,
         out_shape=shape_of(*base.shape),
+        scratch_shapes=[pltpu.VMEM(base.shape, bf16), pltpu.SemaphoreType.DMA((6,))],
         compiler_params=params(12),
         cost_estimate=cost(0, 4 * base.size),
     )(select, rows, base)
@@ -696,8 +702,8 @@
     put(3, ("select_f",), load("down", down), ("flag_d",))
     put(f_done, ("select_f",), active, ("active",))
     put(f_done + 1, ("active",), outpart, ("corner_o",))
-    put(h_done-3, ("act_base",), nothing, ())
-    put(out+1, ("grad_base",), nothing, ())
+    put(h_done - 3, ("act_base",), nothing, ())
+    put(out + 2, ("grad_base",), nothing, ())
     put(h_done - 2, ("select_f",), back, ("back",))
     put(h_done - 1, ("select_f",), load("up", up), ("flag_u",))
     put(h_done, ("back",), cots, ("gate_cot", "up_cot", "slope"))

time: 183 us -> 183 us (level)
  transfers between devices with their start and end apart: 46 -> 46, of which waited for: 25 -> 26; matrix products, arithmetic and copies ran while one was open for 0% -> 0% of each run, Pallas kernels for 32% -> 32%
where the time goes in v6:
time: 183 us
  Pallas kernels  63.9 us (35%)
  starting transfers between devices  61.1 us (33%)
  waiting for transfers between devices  56.6 us (31%)
    ppermute x40, waiting for transfers between devices, hop(): lax.ppermute(value, 'expert', [(ring[i], ring[(i + steps) % count]) for i...  50 us
    ppermute x40, starting transfers between devices, hop(): lax.ppermute(value, 'expert', [(ring[i], ring[(i + steps) % count]) for i...  30.8 us
    ppermute x6, starting transfers between devices, shifted(): lax.ppermute(value, 'section', [(source, (source + steps) % count) for so...  30.3 us
    pallas_call x3, Pallas kernels, load_call(): pl.pallas_call(load_kernel, in_specs=[anywhere, in_hbm], out_specs=[in_vm...  14.2 us
    pallas_call x1, Pallas kernels, active_call(): pl.pallas_call(functools.partial(active_kernel, widths_of(held)), in_spec...  8.67 us
    pallas_call x1, Pallas kernels, cots_call(): pl.pallas_call(functools.partial(cots_kernel, widths_of(held)), in_specs=...  8.55 us
    pallas_call x1, Pallas kernels, rowpart_call(): pl.pallas_call(functools.partial(rowpart_kernel, held), in_specs=[in_vmem...  6.68 us
    ppermute x6, waiting for transfers between devices, shifted(): lax.ppermute(value, 'section', [(source, (source + steps) % count) for so...  6.55 us
  transfers between devices with their start and end apart: 46, of which 26 were waited for; matrix products, arithmetic and copies ran while one was open for 0% of the time, Pallas kernels for 32%

profile of v6, /device:TPU:1, one launch (start us, length us, event | category | flops | bytes accessed | tf_op | source)
XLA Modules:
  0.0 182.9 jit_solution(8253545288619584089)
XLA Ops:
  2.7 2.2 %collective-permute-start.2 = (bf16[32,6144]{1,0:T(8,128)(2,1)S(1)}, bf16[32,6144]{1,0:T(8,128)(2,1)S(1)}, u32[]{:S(2)}, u32[]{:S(2)}) collective-permute-start(bf16[32,6144]{1,0:T(8,128)(2,1)S(1)} %get-tuple-element.131.refs_0_), channel_id=1, source_target_pairs={{0,2},{2,4},{4,6},{6,7},{7,5},{5,3},{3,1},{1,0},{8,10},{10,12},{12... | collective-permute-start | bytes 1179656 | tf_op jit(solution)/shard_map/window_0/ppermute | solution.py:44
  8.3 2.4 %shard_map.117 = (bf16[32,128]{1,0:T(8,128)(2,1)}, bf16[32,6144]{1,0:T(8,128)(2,1)S(1)}, bf16[32,6144]{1,0:T(8,128)(2,1)S(1)}) custom-call(bf16[32,128]{1,0:T(8,128)(2,1)S(1)} %get-tuple-element.132.after_ref.refs_3_, s32[2,128]{1,0:T(2,128)} %bitcast.20, bf16[128,6144]{1,0:T(8,128)(2,1)} %bitcast.30, f32[1,6144]{1,0:T(1,128)} %gain_ref.5), custom_call_target="tpu_custom_call" | custom-call | bytes 6291456 | tf_op jit(solution)/shard_map/pallas_call | solution.py:487
  10.7 3.0 %collective-permute-done.2.refs_0_ = bf16[32,6144]{1,0:T(8,128)(2,1)S(1)} collective-permute-done((bf16[32,6144]{1,0:T(8,128)(2,1)S(1)}, bf16[32,6144]{1,0:T(8,128)(2,1)S(1)}, u32[]{:S(2)}, u32[]{:S(2)}) %collective-permute-start.2) | collective-permute-done | bytes 393248 | tf_op jit(solution)/shard_map/window_0/ppermute | solution.py:44
  16.0 4.8 %shard_map.119 = (bf16[6144,1024]{1,0:T(8,128)(2,1)S(1)}, f32[8,128]{1,0:T(8,128)S(1)}) custom-call(bf16[32,128]{1,0:T(8,128)(2,1)S(1)} %get-tuple-element.134.after_ref.refs_3_, bf16[6144,1024]{1,0:T(8,128)(2,1)} %bitcast.26), custom_call_target="tpu_custom_call" | custom-call | bytes 25165824 | tf_op jit(solution)/shard_map/pallas_call | solution.py:223
  24.5 5.0 %collective-permute-start.18 = (bf16[128,6144]{1,0:T(8,128)(2,1)S(1)}, bf16[128,6144]{1,0:T(8,128)(2,1)S(1)}, u32[]{:S(2)}, u32[]{:S(2)}) collective-permute-start(bf16[128,6144]{1,0:T(8,128)(2,1)S(1)} %bitcast.32), channel_id=1, source_target_pairs={{0,8},{8,16},{16,24},{24,0},{1,9},{9,17},{17,25},{25,1},{2,10},{10... | collective-permute-start | bytes 4718600 | tf_op jit(solution)/shard_map/ppermute | solution.py:49
  29.5 4.7 %shard_map.122 = (bf16[1024,6144]{1,0:T(8,128)(2,1)S(1)}, f32[8,128]{1,0:T(8,128)S(1)}) custom-call(bf16[32,128]{1,0:T(8,128)(2,1)S(1)} %get-tuple-element.142.after_ref.refs_2_, bf16[1024,6144]{1,0:T(8,128)(2,1)} %bitcast.27), custom_call_target="tpu_custom_call" | custom-call | bytes 25165824 | tf_op jit(solution)/shard_map/pallas_call | solution.py:223
  35.7 3.3 %collective-permute-done.4.refs_0_ = bf16[32,6144]{1,0:T(8,128)(2,1)S(1)} collective-permute-done((bf16[32,6144]{1,0:T(8,128)(2,1)S(1)}, bf16[32,6144]{1,0:T(8,128)(2,1)S(1)}, u32[]{:S(2)}, u32[]{:S(2)}) %collective-permute-start.4) | collective-permute-done | bytes 393248 | tf_op jit(solution)/shard_map/window_3/ppermute | solution.py:44
  41.3 6.1 %collective-permute-done.10.refs_0_ = bf16[32,6144]{1,0:T(8,128)(2,1)S(1)} collective-permute-done((bf16[32,6144]{1,0:T(8,128)(2,1)S(1)}, bf16[32,6144]{1,0:T(8,128)(2,1)S(1)}, u32[]{:S(2)}, u32[]{:S(2)}) %collective-permute-start.10) | collective-permute-done | bytes 393248 | tf_op jit(solution)/shard_map/window_4/ppermute | solution.py:44
  49.9 5.9 %collective-permute-done.14.refs_0_ = bf16[32,6144]{1,0:T(8,128)(2,1)S(1)} collective-permute-done((bf16[32,6144]{1,0:T(8,128)(2,1)S(1)}, bf16[32,6144]{1,0:T(8,128)(2,1)S(1)}, u32[]{:S(2)}, u32[]{:S(2)}) %collective-permute-start.14) | collective-permute-done | bytes 393248 | tf_op jit(solution)/shard_map/window_5/ppermute | solution.py:44
  57.3 2.7 %collective-permute-done.12.refs_0_ = bf16[32,3072]{1,0:T(8,128)(2,1)S(1)} collective-permute-done((bf16[32,3072]{1,0:T(8,128)(2,1)S(1)}, bf16[32,3072]{1,0:T(8,128)(2,1)S(1)}, u32[]{:S(2)}, u32[]{:S(2)}) %collective-permute-start.12) | collective-permute-done | bytes 196640 | tf_op jit(solution)/shard_map/window_6/ppermute | solution.py:44
  61.5 8.7 %shard_map.126.refs_2_ = bf16[256,1024]{1,0:T(8,128)(2,1)S(1)} custom-call(bf16[32,6144]{1,0:T(8,128)(2,1)S(1)} %get-tuple-element.131.refs_0_, bf16[32,6144]{1,0:T(8,128)(2,1)S(1)} %get-tuple-element.140.refs_1_, bf16[32,6144]{1,0:T(8,128)(2,1)S(1)} %get-tuple-element.144.refs_2_, bf16[32,6144]{1,0:T(8,128)(2,1)S(1)} %get-tuple-element.146.refs_3_, ...), custom_call_target="tpu_custom_call" | custom-call | flops 6442450944 | bytes 28311552 | tf_op jit(solution)/shard_map/pallas_call | solution.py:311
  71.8 5.3 %shard_map.128 = (bf16[32,6144]{1,0:T(8,128)(2,1)S(1)}, bf16[32,6144]{1,0:T(8,128)(2,1)S(1)}, bf16[32,6144]{1,0:T(8,128)(2,1)S(1)}, bf16[32,6144]{1,0:T(8,128)(2...) custom-call(bf16[256,1024]{1,0:T(8,128)(2,1)S(1)} %get-tuple-element, ...), custom_call_target="tpu_custom_call" | custom-call | flops 3221225472 | bytes 12582912 | tf_op jit(solution)/shard_map/pallas_call | solution.py:407
  83.5 5.0 %shard_map.132.refs_4_ = f32[256,1024]{1,0:T(8,128)S(1)} custom-call(bf16[32,6144]{1,0:T(8,128)(2,1)S(1)} %get-tuple-element.130.refs_0_, bf16[32,6144]{1,0:T(8,128)(2,1)S(1)} %get-tuple-element.137.refs_1_, bf16[32,6144]{1,0:T(8,128)(2,1)S(1)} %get-tuple-element.139.refs_2_, bf16[32,6144]{1,0:T(8,128)(2,1)S(1)} %get-tuple-element.162.refs_3_, ...), custom_call_target="tpu_custom_call" | custom-call | flops 3221225472 | bytes 15728640 | tf_op jit(solution)/shard_map/pallas_call | solution.py:248
  88.4 3.7 %collective-permute-done.23.refs_2_ = bf16[32,3072]{1,0:T(8,128)(2,1)S(1)} collective-permute-done((bf16[32,3072]{1,0:T(8,128)(2,1)S(1)}, bf16[32,3072]{1,0:T(8,128)(2,1)S(1)}, u32[]{:S(2)}, u32[]{:S(2)}) %collective-permute-start.23) | collective-permute-done | bytes 196640 | tf_op jit(solution)/shard_map/window_11/ppermute | solution.py:44
  96.9 4.0 %collective-permute-start.35 = (bf16[128,6144]{1,0:T(8,128)(2,1)S(1)}, bf16[128,6144]{1,0:T(8,128)(2,1)S(1)}, u32[]{:S(2)}, u32[]{:S(2)}) collective-permute-start(bf16[128,6144]{1,0:T(8,128)(2,1)S(1)} %bitcast.34), channel_id=1, source_target_pairs={{0,24},{8,0},{16,8},{24,16},{1,25},{9,1},{17,9},{25,17},{2,26},{10... | collective-permute-start | bytes 4718600 | tf_op jit(solution)/shard_map/ppermute | solution.py:49
  100.9 4.7 %shard_map.134 = (bf16[6144,1024]{1,0:T(8,128)(2,1)S(1)}, f32[8,128]{1,0:T(8,128)S(1)}) custom-call(bf16[32,128]{1,0:T(8,128)(2,1)S(1)} %get-tuple-element.179.after_ref.refs_2_, bf16[6144,1024]{1,0:T(8,128)(2,1)} %bitcast.25), custom_call_target="tpu_custom_call" | custom-call | bytes 25165824 | tf_op jit(solution)/shard_map/pallas_call | solution.py:223
  108.5 8.6 %shard_map.136 = (bf16[256,1024]{1,0:T(8,128)(2,1)S(1)}, bf16[256,1024]{1,0:T(8,128)(2,1)S(1)}, f32[256,128]{1,0:T(8,128)S(1)}) custom-call(bf16[32,6144]{1,0:T(8,128)(2,1)S(1)} %get-tuple-element.155.refs_0_, bf16[32,6144]{1,0:T(8,128)(2,1)S(1)} %get-tuple-element.157.refs_1_, bf16[32,6144]{1,0:T(8,128)(2,1)S(1)} %get-tuple-element.160.refs_2_, ...), custom_call_target="tpu_custom_call" | custom-call | flops 6442450944 | bytes 28311552 | tf_op jit(solution)/shard_map/pallas_call | solution.py:338
  118.8 6.7 %shard_map.138 = (bf16[32,6272]{1,0:T(8,128)(2,1)S(1)}, bf16[32,6272]{1,0:T(8,128)(2,1)S(1)}, bf16[32,6272]{1,0:T(8,128)(2,1)S(1)}, bf16[32,6272]{1,0:T(8,128)(2...) custom-call(bf16[256,1024]{1,0:T(8,128)(2,1)S(1)} %get-tuple-element, ...), custom_call_target="tpu_custom_call" | custom-call | flops 6442450944 | bytes 25165824 | tf_op jit(solution)/shard_map/pallas_call | solution.py:433
  128.3 3.1 %collective-permute-done.33.refs_0_ = bf16[32,3072]{1,0:T(8,128)(2,1)S(1)} collective-permute-done((bf16[32,3072]{1,0:T(8,128)(2,1)S(1)}, bf16[32,3072]{1,0:T(8,128)(2,1)S(1)}, u32[]{:S(2)}, u32[]{:S(2)}) %collective-permute-start.33) | collective-permute-done | bytes 196640 | tf_op jit(solution)/shard_map/window_15/ppermute | solution.py:44
  134.6 10.6 %collective-permute-start.40 = (bf16[32,128]{1,0:T(8,128)(2,1)S(1)}, bf16[32,128]{1,0:T(8,128)(2,1)S(1)}, u32[]{:S(2)}, u32[]{:S(2)}) collective-permute-start(bf16[32,128]{1,0:T(8,128)(2,1)S(1)} %get-tuple-element.215.after_ref.refs_2_), channel_id=1, source_target_pairs={{0,8},{8,16},{16,24},{24,0},{1,9},{9,17},{17,25},{25,1},{2,10},{10... | collective-permute-start | bytes 24584 | tf_op jit(solution)/shard_map/ppermute | solution.py:49
  148.1 9.0 %collective-permute-start.41 = (bf16[32,6144]{1,0:T(8,128)(2,1)S(1)}, bf16[32,6144]{1,0:T(8,128)(2,1)S(1)}, u32[]{:S(2)}, u32[]{:S(2)}) collective-permute-start(bf16[32,6144]{1,0:T(8,128)(2,1)S(1)} %shard_map.144), channel_id=1, source_target_pairs={{0,8},{8,16},{16,24},{24,0},{1,9},{9,17},{17,25},{25,1},{2,10},{10... | collective-permute-start | bytes 1179656 | tf_op jit(solution)/shard_map/ppermute | solution.py:49
  157.1 3.0 %shard_map.143 = (f32[32,128]{1,0:T(8,128)S(1)}, f32[32,6144]{1,0:T(8,128)S(1)}) custom-call(bf16[32,128]{1,0:T(8,128)(2,1)S(1)} %get-tuple-element.227.after_ref, bf16[32,6144]{1,0:T(8,128)(2,1)S(1)} %get-tuple-element.228.rows_ref, f32[1,6144]{1,0:T(1,128)S(1)} %copy-done, f32[8,6144]{1,0:T(8,128)S(1)} %bitcast.18, s32[2,128]{1,0:T(2,128)S(1)} %bitcast.21), custom_call_target="tpu_custom_call" | custom-call | bytes 2359296 | tf_op jit(solution)/shard_map/pallas_call | solution.py:590
  163.6 8.9 %collective-permute-done.43.a_ref = bf16[32,6272]{1,0:T(8,128)(2,1)S(1)} collective-permute-done((bf16[32,6272]{1,0:T(8,128)(2,1)S(1)}, bf16[32,6272]{1,0:T(8,128)(2,1)S(1)}, u32[]{:S(2)}, u32[]{:S(2)}) %collective-permute-start.43) | collective-permute-done | bytes 401440 | tf_op jit(solution)/shard_map/window_18/ppermute | solution.py:44
  177.2 4.0 %collective-permute-done.45.rows_ref = bf16[32,6144]{1,0:T(8,128)(2,1)S(1)} collective-permute-done((bf16[32,6144]{1,0:T(8,128)(2,1)S(1)}, bf16[32,6144]{1,0:T(8,128)(2,1)S(1)}, u32[]{:S(2)}, u32[]{:S(2)}) %collective-permute-start.45) | collective-permute-done | bytes 393248 | tf_op jit(solution)/shard_map/ppermute | solution.py:49
  (132 shorter events, 56.5 us)
Async XLA Ops:
  6.8 15.3 %collective-permute-start = (bf16[32,6144]{1,0:T(8,128)(2,1)S(1)}, bf16[32,6144]{1,0:T(8,128)(2,1)S(1)}, u32[]{:S(2)}, u32[]{:S(2)}) collective-permute-start(bf16[32,6144]{1,0:T(8,128)(2,1)S(1)} %get-tuple-element.130.refs_0_), channel_id=1, source_target_pairs={{0,2},{2,4},{4,6},{6,7},{7,5},{5,3},{3,1},{1,0},{8,10},{10,12},{12... | collective-permute-start | bytes 1179656 | tf_op jit(solution)/shard_map/window_1/ppermute | solution.py:44
  8.3 14.7 %collective-permute-start.1 = (bf16[32,6144]{1,0:T(8,128)(2,1)S(1)}, bf16[32,6144]{1,0:T(8,128)(2,1)S(1)}, u32[]{:S(2)}, u32[]{:S(2)}) collective-permute-start(bf16[32,6144]{1,0:T(8,128)(2,1)S(1)} %get-tuple-element.130.refs_0_), channel_id=1, source_target_pairs={{0,1},{2,0},{4,2},{6,4},{7,6},{5,7},{3,5},{1,3},{8,9},{10,8},{12,1... | collective-permute-start | bytes 1179656 | tf_op jit(solution)/shard_map/window_1/ppermute | solution.py:44
  14.6 19.6 %collective-permute-start.8 = (bf16[32,6144]{1,0:T(8,128)(2,1)S(1)}, bf16[32,6144]{1,0:T(8,128)(2,1)S(1)}, u32[]{:S(2)}, u32[]{:S(2)}) collective-permute-start(bf16[32,6144]{1,0:T(8,128)(2,1)S(1)} %get-tuple-element.141.refs_8_), channel_id=1, source_target_pairs={{0,2},{2,4},{4,6},{6,7},{7,5},{5,3},{3,1},{1,0},{8,10},{10,12},{12... | collective-permute-start | bytes 1179656 | tf_op jit(solution)/shard_map/window_2/ppermute | solution.py:44
  15.9 18.3 %collective-permute-start.9 = (bf16[32,6144]{1,0:T(8,128)(2,1)S(1)}, bf16[32,6144]{1,0:T(8,128)(2,1)S(1)}, u32[]{:S(2)}, u32[]{:S(2)}) collective-permute-start(bf16[32,6144]{1,0:T(8,128)(2,1)S(1)} %get-tuple-element.140.refs_1_), channel_id=1, source_target_pairs={{0,1},{2,0},{4,2},{6,4},{7,6},{5,7},{3,5},{1,3},{8,9},{10,8},{12,1... | collective-permute-start | bytes 1179656 | tf_op jit(solution)/shard_map/window_2/ppermute | solution.py:44
  23.0 16.0 %collective-permute-start.4 = (bf16[32,6144]{1,0:T(8,128)(2,1)S(1)}, bf16[32,6144]{1,0:T(8,128)(2,1)S(1)}, u32[]{:S(2)}, u32[]{:S(2)}) collective-permute-start(bf16[32,6144]{1,0:T(8,128)(2,1)S(1)} %get-tuple-element.136.refs_8_), channel_id=1, source_target_pairs={{0,2},{2,4},{4,6},{6,7},{7,5},{5,3},{3,1},{1,0},{8,10},{10,12},{12... | collective-permute-start | bytes 1179656 | tf_op jit(solution)/shard_map/window_3/ppermute | solution.py:44
  24.3 15.6 %collective-permute-start.5 = (bf16[32,6144]{1,0:T(8,128)(2,1)S(1)}, bf16[32,6144]{1,0:T(8,128)(2,1)S(1)}, u32[]{:S(2)}, u32[]{:S(2)}) collective-permute-start(bf16[32,6144]{1,0:T(8,128)(2,1)S(1)} %get-tuple-element.137.refs_1_), channel_id=1, source_target_pairs={{0,1},{2,0},{4,2},{6,4},{7,6},{5,7},{3,5},{1,3},{8,9},{10,8},{12,1... | collective-permute-start | bytes 1179656 | tf_op jit(solution)/shard_map/window_3/ppermute | solution.py:44
  24.5 53.3 %collective-permute-start.18 = (bf16[128,6144]{1,0:T(8,128)(2,1)S(1)}, bf16[128,6144]{1,0:T(8,128)(2,1)S(1)}, u32[]{:S(2)}, u32[]{:S(2)}) collective-permute-start(bf16[128,6144]{1,0:T(8,128)(2,1)S(1)} %bitcast.32), channel_id=1, source_target_pairs={{0,8},{8,16},{16,24},{24,0},{1,9},{9,17},{17,25},{25,1},{2,10},{10... | collective-permute-start | bytes 4718600 | tf_op jit(solution)/shard_map/ppermute | solution.py:49
  34.2 13.2 %collective-permute-start.10 = (bf16[32,6144]{1,0:T(8,128)(2,1)S(1)}, bf16[32,6144]{1,0:T(8,128)(2,1)S(1)}, u32[]{:S(2)}, u32[]{:S(2)}) collective-permute-start(bf16[32,6144]{1,0:T(8,128)(2,1)S(1)} %get-tuple-element.145.refs_7_), channel_id=1, source_target_pairs={{0,2},{2,4},{4,6},{6,7},{7,5},{5,3},{3,1},{1,0},{8,10},{10,12},{12... | collective-permute-start | bytes 1179656 | tf_op jit(solution)/shard_map/window_4/ppermute | solution.py:44
  35.5 12.8 %collective-permute-start.11 = (bf16[32,6144]{1,0:T(8,128)(2,1)S(1)}, bf16[32,6144]{1,0:T(8,128)(2,1)S(1)}, u32[]{:S(2)}, u32[]{:S(2)}) collective-permute-start(bf16[32,6144]{1,0:T(8,128)(2,1)S(1)} %get-tuple-element.144.refs_2_), channel_id=1, source_target_pairs={{0,1},{2,0},{4,2},{6,4},{7,6},{5,7},{3,5},{1,3},{8,9},{10,8},{12,1... | collective-permute-start | bytes 1179656 | tf_op jit(solution)/shard_map/window_4/ppermute | solution.py:44
  39.9 16.0 %collective-permute-start.14 = (bf16[32,6144]{1,0:T(8,128)(2,1)S(1)}, bf16[32,6144]{1,0:T(8,128)(2,1)S(1)}, u32[]{:S(2)}, u32[]{:S(2)}) collective-permute-start(bf16[32,6144]{1,0:T(8,128)(2,1)S(1)} %get-tuple-element.155.refs_0_), channel_id=1, source_target_pairs={{0,2},{2,4},{4,6},{6,7},{7,5},{5,3},{3,1},{1,0},{8,10},{10,12},{12... | collective-permute-start | bytes 1179656 | tf_op jit(solution)/shard_map/window_5/ppermute | solution.py:44
  41.2 15.9 %collective-permute-start.15 = (bf16[32,6144]{1,0:T(8,128)(2,1)S(1)}, bf16[32,6144]{1,0:T(8,128)(2,1)S(1)}, u32[]{:S(2)}, u32[]{:S(2)}) collective-permute-start(bf16[32,6144]{1,0:T(8,128)(2,1)S(1)} %get-tuple-element.155.refs_0_), channel_id=1, source_target_pairs={{0,1},{2,0},{4,2},{6,4},{7,6},{5,7},{3,5},{1,3},{8,9},{10,8},{12,1... | collective-permute-start | bytes 1179656 | tf_op jit(solution)/shard_map/window_5/ppermute | solution.py:44
  48.3 11.7 %collective-permute-start.12 = (bf16[32,3072]{1,0:T(8,128)(2,1)S(1)}, bf16[32,3072]{1,0:T(8,128)(2,1)S(1)}, u32[]{:S(2)}, u32[]{:S(2)}) collective-permute-start(bf16[32,3072]{1,0:T(8,128)(2,1)S(1)} %slice.29), channel_id=1, source_target_pairs={{0,2},{2,4},{4,6},{6,7},{7,5},{5,3},{3,1},{1,0},{8,10},{10,12},{12... | collective-permute-start | bytes 589832 | tf_op jit(solution)/shard_map/window_6/ppermute | solution.py:44
  55.8 14.4 %collective-permute-start.6 = (bf16[32,6144]{1,0:T(8,128)(2,1)S(1)}, bf16[32,6144]{1,0:T(8,128)(2,1)S(1)}, u32[]{:S(2)}, u32[]{:S(2)}) collective-permute-start(bf16[32,6144]{1,0:T(8,128)(2,1)S(1)} %get-tuple-element.138.refs_7_), channel_id=1, source_target_pairs={{0,2},{2,4},{4,6},{6,7},{7,5},{5,3},{3,1},{1,0},{8,10},{10,12},{12... | collective-permute-start | bytes 1179656 | tf_op jit(solution)/shard_map/window_7/ppermute | solution.py:44
  57.0 13.2 %collective-permute-start.7 = (bf16[32,6144]{1,0:T(8,128)(2,1)S(1)}, bf16[32,6144]{1,0:T(8,128)(2,1)S(1)}, u32[]{:S(2)}, u32[]{:S(2)}) collective-permute-start(bf16[32,6144]{1,0:T(8,128)(2,1)S(1)} %get-tuple-element.139.refs_2_), channel_id=1, source_target_pairs={{0,1},{2,0},{4,2},{6,4},{7,6},{5,7},{3,5},{1,3},{8,9},{10,8},{12,1... | collective-permute-start | bytes 1179656 | tf_op jit(solution)/shard_map/window_7/ppermute | solution.py:44
  60.0 17.1 %collective-permute-start.16 = (bf16[32,6144]{1,0:T(8,128)(2,1)S(1)}, bf16[32,6144]{1,0:T(8,128)(2,1)S(1)}, u32[]{:S(2)}, u32[]{:S(2)}) collective-permute-start(bf16[32,6144]{1,0:T(8,128)(2,1)S(1)} %get-tuple-element.156.refs_8_), channel_id=1, source_target_pairs={{0,2},{2,4},{4,6},{6,7},{7,5},{5,3},{3,1},{1,0},{8,10},{10,12},{12... | collective-permute-start | bytes 1179656 | tf_op jit(solution)/shard_map/window_8/ppermute | solution.py:44
  61.2 16.5 %collective-permute-start.17 = (bf16[32,6144]{1,0:T(8,128)(2,1)S(1)}, bf16[32,6144]{1,0:T(8,128)(2,1)S(1)}, u32[]{:S(2)}, u32[]{:S(2)}) collective-permute-start(bf16[32,6144]{1,0:T(8,128)(2,1)S(1)} %get-tuple-element.157.refs_1_), channel_id=1, source_target_pairs={{0,1},{2,0},{4,2},{6,4},{7,6},{5,7},{3,5},{1,3},{8,9},{10,8},{12,1... | collective-permute-start | bytes 1179656 | tf_op jit(solution)/shard_map/window_8/ppermute | solution.py:44
  77.8 15.9 %collective-permute-start.19 = (bf16[32,6144]{1,0:T(8,128)(2,1)S(1)}, bf16[32,6144]{1,0:T(8,128)(2,1)S(1)}, u32[]{:S(2)}, u32[]{:S(2)}) collective-permute-start(bf16[32,6144]{1,0:T(8,128)(2,1)S(1)} %get-tuple-element.159.refs_7_), channel_id=1, source_target_pairs={{0,2},{2,4},{4,6},{6,7},{7,5},{5,3},{3,1},{1,0},{8,10},{10,12},{12... | collective-permute-start | bytes 1179656 | tf_op jit(solution)/shard_map/window_10/ppermute | solution.py:44
  79.1 14.6 %collective-permute-start.20 = (bf16[32,6144]{1,0:T(8,128)(2,1)S(1)}, bf16[32,6144]{1,0:T(8,128)(2,1)S(1)}, u32[]{:S(2)}, u32[]{:S(2)}) collective-permute-start(bf16[32,6144]{1,0:T(8,128)(2,1)S(1)} %get-tuple-element.160.refs_2_), channel_id=1, source_target_pairs={{0,1},{2,0},{4,2},{6,4},{7,6},{5,7},{3,5},{1,3},{8,9},{10,8},{12,1... | collective-permute-start | bytes 1179656 | tf_op jit(solution)/shard_map/window_10/ppermute | solution.py:44
  93.8 13.0 %collective-permute-start.27 = (bf16[32,6144]{1,0:T(8,128)(2,1)S(1)}, bf16[32,6144]{1,0:T(8,128)(2,1)S(1)}, u32[]{:S(2)}, u32[]{:S(2)}) collective-permute-start(bf16[32,6144]{1,0:T(8,128)(2,1)S(1)} %get-tuple-element.177), channel_id=1, source_target_pairs={{0,2},{2,4},{4,6},{6,7},{7,5},{5,3},{3,1},{1,0},{8,10},{10,12},{12... | collective-permute-start | bytes 1179656 | tf_op jit(solution)/shard_map/window_12/ppermute | solution.py:44
  96.9 31.4 %collective-permute-start.35 = (bf16[128,6144]{1,0:T(8,128)(2,1)S(1)}, bf16[128,6144]{1,0:T(8,128)(2,1)S(1)}, u32[]{:S(2)}, u32[]{:S(2)}) collective-permute-start(bf16[128,6144]{1,0:T(8,128)(2,1)S(1)} %bitcast.34), channel_id=1, source_target_pairs={{0,24},{8,0},{16,8},{24,16},{1,25},{9,1},{17,9},{25,17},{2,26},{10... | collective-permute-start | bytes 4718600 | tf_op jit(solution)/shard_map/ppermute | solution.py:49
  133.0 12.9 %collective-permute-start.36 = (bf16[32,6272]{1,0:T(8,128)(2,1)S(1)}, bf16[32,6272]{1,0:T(8,128)(2,1)S(1)}, u32[]{:S(2)}, u32[]{:S(2)}) collective-permute-start(bf16[32,6272]{1,0:T(8,128)(2,1)S(1)} %get-tuple-element.220), channel_id=1, source_target_pairs={{0,2},{2,4},{4,6},{6,7},{7,5},{5,3},{3,1},{1,0},{8,10},{10,12},{12... | collective-permute-start | bytes 1204232 | tf_op jit(solution)/shard_map/window_16/ppermute | solution.py:44
  146.2 15.7 %collective-permute-start.38 = (bf16[32,6272]{1,0:T(8,128)(2,1)S(1)}, bf16[32,6272]{1,0:T(8,128)(2,1)S(1)}, u32[]{:S(2)}, u32[]{:S(2)}) collective-permute-start(bf16[32,6272]{1,0:T(8,128)(2,1)S(1)} %get-tuple-element.225), channel_id=1, source_target_pairs={{0,2},{2,4},{4,6},{6,7},{7,5},{5,3},{3,1},{1,0},{8,10},{10,12},{12... | collective-permute-start | bytes 1204232 | tf_op jit(solution)/shard_map/window_17/ppermute | solution.py:44
  147.6 14.3 %collective-permute-start.39 = (bf16[32,6272]{1,0:T(8,128)(2,1)S(1)}, bf16[32,6272]{1,0:T(8,128)(2,1)S(1)}, u32[]{:S(2)}, u32[]{:S(2)}) collective-permute-start(bf16[32,6272]{1,0:T(8,128)(2,1)S(1)} %get-tuple-element.226), channel_id=1, source_target_pairs={{0,1},{2,0},{4,2},{6,4},{7,6},{5,7},{3,5},{1,3},{8,9},{10,8},{12,1... | collective-permute-start | bytes 1204232 | tf_op jit(solution)/shard_map/window_17/ppermute | solution.py:44
  148.1 13.7 %collective-permute-start.41 = (bf16[32,6144]{1,0:T(8,128)(2,1)S(1)}, bf16[32,6144]{1,0:T(8,128)(2,1)S(1)}, u32[]{:S(2)}, u32[]{:S(2)}) collective-permute-start(bf16[32,6144]{1,0:T(8,128)(2,1)S(1)} %shard_map.144), channel_id=1, source_target_pairs={{0,8},{8,16},{16,24},{24,0},{1,9},{9,17},{17,25},{25,1},{2,10},{10... | collective-permute-start | bytes 1179656 | tf_op jit(solution)/shard_map/ppermute | solution.py:49
  (28 other events, 234.6 us)
